TPU v7x, 32 devices: a whole 2x2x4 slice. The times are simulated.
32 devices in a mesh: fsdp: 2 (over y), ctx: 4 (over x, core), tp: 4 (over z).
Axes of the slice: x: 2, y: 2, z: 4, core: 2. Of those that a mesh axis runs over, the one named last changes fastest.
Arguments:
- tokens: bfloat16 [3, 2, 1024, 2560], P(None, 'fsdp', 'ctx'), may hold values from -6 to 6
- out_cotangent: bfloat16 [3, 2, 1024, 2560], P(None, 'fsdp', 'ctx'), may hold values from -6 to 6
- seq_lengths: int32 [3, 2], P(None, 'fsdp'), may hold values from 256 to 1024, as said below
- span_order: int32 [3, 2, 8], P(None, 'fsdp'), may hold values from 0 to 7, each once within a row
- attention_input_weight: float32 [2560, 3840], P(('fsdp', 'ctx'), 'tp'), may hold values from -0.125 to 0.125
- attention_input_first: float32 [2560, 3840], P(('fsdp', 'ctx'), 'tp'), may hold values from -20 to 20
- attention_input_squared: float32 [2560, 3840], P(('fsdp', 'ctx'), 'tp'), may hold values from 26.25792 to 420.3264
- attend_out: float32 [2560, 2560], P('tp', ('fsdp', 'ctx')), may hold values from -1 to 1
- attend_out_moment: float32 [2560, 2560], P('tp', ('fsdp', 'ctx')), may hold values from -4 to 4
- attend_out_second: float32 [2560, 2560], P('tp', ('fsdp', 'ctx')), may hold values from 1.0503168 to 16.813057
- gate_up: float32 [2560, 14336], P(('fsdp', 'ctx'), 'tp'), may hold values from -0.125 to 0.125
- gate_up_moment: float32 [2560, 14336], P(('fsdp', 'ctx'), 'tp'), may hold values from -16 to 16
- gate_up_second: float32 [2560, 14336], P(('fsdp', 'ctx'), 'tp'), may hold values from 13.654119 to 218.56973
- down_weight: float32 [7168, 2560], P('tp', ('fsdp', 'ctx')), may hold values from -0.0625 to 0.0625
- down_weight_moment: float32 [7168, 2560], P('tp', ('fsdp', 'ctx')), may hold values from -24 to 24
- down_weight_second: float32 [7168, 2560], P('tp', ('fsdp', 'ctx')), may hold values from 37.811405 to 605.27
- norm_gains: float32 [2, 2560], P(None, ('fsdp', 'ctx')), may hold values from 0.5 to 1.5
- norm_gains_moment: float32 [2, 2560], P(None, ('fsdp', 'ctx')), may hold values from -40 to 40
- norm_gains_second: float32 [2, 2560], P(None, ('fsdp', 'ctx')), may hold values from 105.03168 to 1681.3055
Outputs:
- mixed: bfloat16 [3, 2, 1024, 2560], P(None, 'fsdp', 'ctx')
- input_grad: float32 [3, 2, 1024, 2560], P(None, 'fsdp', 'ctx')
- attend_in_moment_new: float32 [2560, 3840], P(('fsdp', 'ctx'), 'tp')
- attend_in_second_new: float32 [2560, 3840], P(('fsdp', 'ctx'), 'tp')
- attend_in_new: float32 [2560, 3840], P(('fsdp', 'ctx'), 'tp')
- attend_in_copy: bfloat16 [2560, 3840], P(('fsdp', 'ctx'), 'tp')
- attend_out_moment_new: float32 [2560, 2560], P('tp', ('fsdp', 'ctx'))
- attend_out_second_new: float32 [2560, 2560], P('tp', ('fsdp', 'ctx'))
- attend_out_new: float32 [2560, 2560], P('tp', ('fsdp', 'ctx'))
- attend_out_copy: bfloat16 [2560, 2560], P('tp', ('fsdp', 'ctx'))
- gate_up_moment_new: float32 [2560, 14336], P(('fsdp', 'ctx'), 'tp')
- gate_up_second_new: float32 [2560, 14336], P(('fsdp', 'ctx'), 'tp')
- gate_up_new: float32 [2560, 14336], P(('fsdp', 'ctx'), 'tp')
- gate_up_copy: bfloat16 [2560, 14336], P(('fsdp', 'ctx'), 'tp')
- down_weight_moment_new: float32 [7168, 2560], P('tp', ('fsdp', 'ctx'))
- down_weight_second_new: float32 [7168, 2560], P('tp', ('fsdp', 'ctx'))
- down_weight_new: float32 [7168, 2560], P('tp', ('fsdp', 'ctx'))
- down_weight_copy: bfloat16 [7168, 2560], P('tp', ('fsdp', 'ctx'))
- norm_gains_moment_new: float32 [2, 2560], P(None, ('fsdp', 'ctx'))
- norm_gains_second_new: float32 [2, 2560], P(None, ('fsdp', 'ctx'))
- norm_gains_new: float32 [2, 2560], P(None, ('fsdp', 'ctx'))
Inputs may be any that keep to these rules, and one draw needn't show every extreme that they name: `seq_lengths`: for every slot index, one micro-batch drawn from the seed has length 1024; lengths are at least 256, reached in some slot. `span_order`: each row is a permutation of the span numbers.
All inputs are finite; a program needn't handle non-finite values.
Results may differ from a plain program's by a relative error of at most 0.025.
Values may be sent and summed in bfloat16 or wider, within the bound.
A program may use at most 320 MiB of HBM per device.

v0:
```python
import jax
import jax.numpy as jnp
from jax import lax
from jax.sharding import PartitionSpec as P

QUERY_HEADS = 32
KEY_VALUE_HEADS = 8
HEAD_DIMENSION = 80
STEP = 10


rope_base = 1000000.0
norm_eps = 1e-05
beta_one = 0.9
beta_two = 0.95
adam_eps = 1e-08
weight_decay = 0.1
learn_rates = (0.1, 0.5, 0.05, 0.04, 0.8)
decay_flags = (1.0, 1.0, 1.0, 1.0, 0.0)
neg_big = -1e30
slice_dims = (0, 1, 0, 1, 1)


def rope_tables(token_positions):
    half_width = HEAD_DIMENSION // 2
    inverse = rope_base ** (-(jnp.arange(half_width, dtype=jnp.float32) * 2.0 / HEAD_DIMENSION))
    angles = token_positions.astype(jnp.float32)[..., None] * inverse
    return (jnp.cos(angles), jnp.sin(angles))


def rotate(values, cosine_table, sine_table):
    half_width = values.shape[-1] // 2
    first_half = values[..., :half_width]
    second_half = values[..., half_width:]
    return jnp.concatenate(
        [
            first_half * cosine_table - second_half * sine_table,
            second_half * cosine_table + first_half * sine_table,
        ],
        -1,
    )


def unrotate(gradient, cosine_table, sine_table):
    half_width = gradient.shape[-1] // 2
    first_half = gradient[..., :half_width]
    second_half = gradient[..., half_width:]
    return jnp.concatenate(
        [
            first_half * cosine_table + second_half * sine_table,
            second_half * cosine_table - first_half * sine_table,
        ],
        -1,
    )


def adam_update(weight, moment, second, gradient, learn_rate, decay_flag):
    moment = beta_one * moment + (1.0 - beta_one) * gradient
    second = beta_two * second + (1.0 - beta_two) * gradient * gradient
    moment_hat = moment / (1.0 - beta_one**STEP)
    second_hat = second / (1.0 - beta_two**STEP)
    weight = weight - learn_rate * (
        moment_hat / (jnp.sqrt(second_hat) + adam_eps) + decay_flag * weight_decay * weight
    )
    return (moment, second, weight)


def fetch_weights(attention_input_weight, attend_out, gate_up, down_weight, norm_gains):
    return (
        lax.all_gather(
            attention_input_weight.astype(jnp.bfloat16), ("fsdp", "ctx"), axis=0, tiled=True
        ),
        lax.all_gather(attend_out.astype(jnp.bfloat16), ("fsdp", "ctx"), axis=1, tiled=True),
        lax.all_gather(gate_up.astype(jnp.bfloat16), ("fsdp", "ctx"), axis=0, tiled=True),
        lax.all_gather(down_weight.astype(jnp.bfloat16), ("fsdp", "ctx"), axis=1, tiled=True),
        lax.all_gather(norm_gains.astype(jnp.bfloat16), ("fsdp", "ctx"), axis=1, tiled=True),
    )


def widened(array, dim_index, factor):
    full_shape = list(array.shape)
    full_shape[dim_index] = full_shape[dim_index] * factor
    return jnp.zeros(tuple(full_shape), jnp.float32)


def on_device(
    tokens,
    out_cotangent,
    seq_lengths,
    span_order,
    attention_input_weight,
    attention_input_first,
    attention_input_squared,
    attend_out,
    attend_out_moment,
    attend_out_second,
    gate_up,
    gate_up_moment,
    gate_up_second,
    down_weight,
    down_weight_moment,
    down_weight_second,
    norm_gains,
    norm_gains_moment,
    norm_gains_second,
):
    masters = (attention_input_weight, attend_out, gate_up, down_weight, norm_gains)
    firsts = (
        attention_input_first,
        attend_out_moment,
        gate_up_moment,
        down_weight_moment,
        norm_gains_moment,
    )
    seconds = (
        attention_input_squared,
        attend_out_second,
        gate_up_second,
        down_weight_second,
        norm_gains_second,
    )
    micro_count, slot_count, row_count, model_width = tokens.shape
    ctx_size = lax.axis_size("ctx")
    shard_count = lax.axis_size(("fsdp", "ctx"))
    sequence_length = row_count * ctx_size
    span_len = sequence_length // (2 * ctx_size)
    query_group_width = QUERY_HEADS // KEY_VALUE_HEADS
    local_groups = attention_input_weight.shape[1] // ((query_group_width + 2) * HEAD_DIMENSION)
    hidden_local = down_weight.shape[0]
    first_row = lax.axis_index("ctx") * row_count
    within = jnp.arange(sequence_length, dtype=jnp.int32)
    block_ids = jnp.arange(2 * ctx_size, dtype=jnp.int32)
    score_scale = HEAD_DIMENSION ** (-0.5)
    summed = tuple(
        (widened(master, dim_index, shard_count) for master, dim_index in zip(masters, slice_dims))
    )
    mixed_parts = []
    input_parts = []
    for micro_index in range(micro_count):
        fetched = fetch_weights(
            attention_input_weight, attend_out, gate_up, down_weight, norm_gains
        )
        in_proj, out_proj, pair_proj, down_proj, gain_low = fetched
        gain_row_stack = gain_low.astype(jnp.float32)
        layer_inputs = tokens[micro_index].astype(jnp.float32)
        order_rows = span_order[micro_index]
        length_row = seq_lengths[micro_index]
        table = jnp.where(
            block_ids[None, None, :] == (within // span_len)[None, :, None],
            order_rows[:, None, :],
            0,
        )
        pos_all = jnp.sum(table, -1) * span_len + within % span_len
        pos_here = lax.dynamic_slice_in_dim(pos_all, first_row, row_count, 1)
        valid_key = pos_all < length_row[:, None]
        cosine_table, sine_table = rope_tables(pos_here)
        cos_query = cosine_table[:, :, None, None, :]
        sin_query = sine_table[:, :, None, None, :]
        cos_key = cosine_table[:, :, None, :]
        sin_key = sine_table[:, :, None, :]
        first_inverse_root = lax.rsqrt(
            jnp.mean(layer_inputs * layer_inputs, -1, keepdims=True) + norm_eps
        )
        first_standardized = layer_inputs * first_inverse_root
        first_normalized = (first_standardized * gain_row_stack[0]).astype(jnp.bfloat16)
        projected_output = jnp.einsum(
            "srd,dc->src", first_normalized, in_proj, preferred_element_type=jnp.float32
        ).reshape(slot_count, row_count, local_groups, query_group_width + 2, HEAD_DIMENSION)
        query_row_block = rotate(
            projected_output[:, :, :, :query_group_width], cos_query, sin_query
        ).astype(jnp.bfloat16)
        key_rows = rotate(projected_output[:, :, :, query_group_width], cos_key, sin_key).astype(
            jnp.bfloat16
        )
        value_rows = projected_output[:, :, :, query_group_width + 1].astype(jnp.bfloat16)
        start_top = jnp.full(
            (slot_count, row_count, local_groups, query_group_width), neg_big, jnp.float32
        )
        running_top = start_top
        key_piece = lax.all_gather(key_rows, "ctx", axis=1, tiled=True)
        value_piece = lax.all_gather(value_rows, "ctx", axis=1, tiled=True)
        allowed = ((pos_all[:, None, :] <= pos_here[:, :, None]) & valid_key[:, None, :])[
            :, :, None, None, :
        ]
        scores = (
            jnp.einsum(
                "srgha,snga->srghn", query_row_block, key_piece, preferred_element_type=jnp.float32
            )
            * score_scale
        )
        scores = jnp.where(allowed, scores, neg_big)
        new_top = jnp.maximum(running_top, jnp.max(scores, -1))
        weights = jnp.where(allowed, jnp.exp(scores - new_top[..., None]), 0.0)
        running_sum = jnp.sum(weights, -1)
        accum = jnp.einsum(
            "srghn,snga->srgha",
            weights.astype(jnp.bfloat16),
            value_piece,
            preferred_element_type=jnp.float32,
        )
        accum, running_top, running_sum = (accum, new_top, running_sum)
        attended_full = accum / running_sum[..., None]
        log_total = running_top + jnp.log(running_sum)
        attention_output = attended_full.reshape(
            slot_count, row_count, local_groups * query_group_width * HEAD_DIMENSION
        ).astype(jnp.bfloat16)
        attend_part = jnp.einsum(
            "src,cd->srd", attention_output, out_proj, preferred_element_type=jnp.float32
        )
        residual_stream = layer_inputs + lax.psum(attend_part.astype(jnp.bfloat16), "tp").astype(
            jnp.float32
        )
        second_inverse_root = lax.rsqrt(
            jnp.mean(residual_stream * residual_stream, -1, keepdims=True) + norm_eps
        )
        second_standardized = residual_stream * second_inverse_root
        second_normalized = (second_standardized * gain_row_stack[1]).astype(jnp.bfloat16)
        hidden_pair = jnp.einsum(
            "srd,dc->src", second_normalized, pair_proj, preferred_element_type=jnp.float32
        )
        gate_value = hidden_pair[..., :hidden_local]
        up_value = hidden_pair[..., hidden_local:]
        sigmoid_gate = jax.nn.sigmoid(gate_value)
        silu_gate = gate_value * sigmoid_gate
        inner_act = (silu_gate * up_value).astype(jnp.bfloat16)
        expand_part = jnp.einsum(
            "src,cd->srd", inner_act, down_proj, preferred_element_type=jnp.float32
        )
        result = residual_stream + lax.psum(expand_part.astype(jnp.bfloat16), "tp").astype(
            jnp.float32
        )
        mixed_parts.append(result.astype(jnp.bfloat16))
        in_proj, out_proj, pair_proj, down_proj, gain_low = fetch_weights(
            attention_input_weight, attend_out, gate_up, down_weight, norm_gains
        )
        keep_mask = (pos_here < length_row[:, None]).astype(jnp.float32)[..., None]
        grad_out = out_cotangent[micro_index].astype(jnp.float32) * keep_mask
        grad_out_low = grad_out.astype(jnp.bfloat16)
        grad_down = jnp.einsum(
            "src,srd->cd", inner_act, grad_out_low, preferred_element_type=jnp.float32
        )
        grad_inner = jnp.einsum(
            "srd,cd->src", grad_out_low, down_proj, preferred_element_type=jnp.float32
        )
        grad_gate = (
            grad_inner * up_value * sigmoid_gate * (1.0 + gate_value * (1.0 - sigmoid_gate))
        ).astype(jnp.bfloat16)
        grad_up = (grad_inner * silu_gate).astype(jnp.bfloat16)
        grad_pair = jnp.concatenate([grad_gate, grad_up], -1)
        grad_gate_up = jnp.einsum(
            "srd,src->dc", second_normalized, grad_pair, preferred_element_type=jnp.float32
        )
        second_normalized_gradient = lax.psum(
            jnp.einsum(
                "src,dc->srd", grad_pair, pair_proj, preferred_element_type=jnp.float32
            ).astype(jnp.bfloat16),
            "tp",
        ).astype(jnp.float32)
        second_gain_gradient = jnp.sum(second_normalized_gradient * second_standardized, (0, 1))
        second_scaled_input = second_normalized_gradient * gain_row_stack[1]
        grad_residual = grad_out + second_inverse_root * (
            second_scaled_input
            - second_standardized
            * jnp.mean(second_scaled_input * second_standardized, -1, keepdims=True)
        )
        grad_residual_low = grad_residual.astype(jnp.bfloat16)
        grad_attend_out = jnp.einsum(
            "src,srd->cd", attention_output, grad_residual_low, preferred_element_type=jnp.float32
        )
        grad_attended = (
            jnp.einsum(
                "srd,cd->src", grad_residual_low, out_proj, preferred_element_type=jnp.float32
            )
            .astype(jnp.bfloat16)
            .reshape(slot_count, row_count, local_groups, query_group_width, HEAD_DIMENSION)
        )
        delta_rows = jnp.sum(grad_attended.astype(jnp.float32) * attended_full, -1)
        whole_keys, whole_values = (
            lax.all_gather(key_rows, "ctx", axis=1, tiled=True),
            lax.all_gather(value_rows, "ctx", axis=1, tiled=True),
        )
        allowed = ((pos_all[:, None, :] <= pos_here[:, :, None]) & valid_key[:, None, :])[
            :, :, None, None, :
        ]
        scores = (
            jnp.einsum(
                "srgha,snga->srghn", query_row_block, whole_keys, preferred_element_type=jnp.float32
            )
            * score_scale
        )
        scores = jnp.where(allowed, scores, neg_big)
        probs = jnp.where(allowed, jnp.exp(scores - log_total[..., None]), 0.0)
        grad_probs = jnp.einsum(
            "srgha,snga->srghn", grad_attended, whole_values, preferred_element_type=jnp.float32
        )
        grad_scores = (probs * (grad_probs - delta_rows[..., None])).astype(jnp.bfloat16)
        grad_query = (
            jnp.einsum(
                "srghn,snga->srgha", grad_scores, whole_keys, preferred_element_type=jnp.float32
            )
            * score_scale
        )
        grad_keys_all = (
            jnp.einsum(
                "srghn,srgha->snga",
                grad_scores,
                query_row_block,
                preferred_element_type=jnp.float32,
            )
            * score_scale
        )
        grad_values_all = jnp.einsum(
            "srghn,srgha->snga",
            probs.astype(jnp.bfloat16),
            grad_attended,
            preferred_element_type=jnp.float32,
        )
        grad_keys, grad_values = (
            lax.psum_scatter(
                grad_keys_all.astype(jnp.bfloat16), "ctx", scatter_dimension=1, tiled=True
            ).astype(jnp.float32),
            lax.psum_scatter(
                grad_values_all.astype(jnp.bfloat16), "ctx", scatter_dimension=1, tiled=True
            ).astype(jnp.float32),
        )
        grad_query_low = unrotate(grad_query, cos_query, sin_query).astype(jnp.bfloat16)
        grad_keys_low = unrotate(grad_keys, cos_key, sin_key).astype(jnp.bfloat16)
        grad_values_low = grad_values.astype(jnp.bfloat16)
        grad_projected = jnp.concatenate(
            [grad_query_low, grad_keys_low[:, :, :, None], grad_values_low[:, :, :, None]], 3
        ).reshape(slot_count, row_count, local_groups * (query_group_width + 2) * HEAD_DIMENSION)
        grad_attend_in = jnp.einsum(
            "srd,src->dc", first_normalized, grad_projected, preferred_element_type=jnp.float32
        )
        first_normalized_gradient = lax.psum(
            jnp.einsum(
                "src,dc->srd", grad_projected, in_proj, preferred_element_type=jnp.float32
            ).astype(jnp.bfloat16),
            "tp",
        ).astype(jnp.float32)
        first_gain_gradient = jnp.sum(first_normalized_gradient * first_standardized, (0, 1))
        first_scaled_input = first_normalized_gradient * gain_row_stack[0]
        input_part = grad_residual + first_inverse_root * (
            first_scaled_input
            - first_standardized
            * jnp.mean(first_scaled_input * first_standardized, -1, keepdims=True)
        )
        input_parts.append(input_part)
        gain_grads = jnp.stack([first_gain_gradient, second_gain_gradient])
        summed = tuple(
            (
                running + term_part
                for running, term_part in zip(
                    summed, (grad_attend_in, grad_attend_out, grad_gate_up, grad_down, gain_grads)
                )
            )
        )
    summed = (
        lax.psum_scatter(
            summed[0].astype(jnp.bfloat16), ("fsdp", "ctx"), scatter_dimension=0, tiled=True
        ).astype(jnp.float32),
        lax.psum_scatter(
            summed[1].astype(jnp.bfloat16), ("fsdp", "ctx"), scatter_dimension=1, tiled=True
        ).astype(jnp.float32),
        lax.psum_scatter(
            summed[2].astype(jnp.bfloat16), ("fsdp", "ctx"), scatter_dimension=0, tiled=True
        ).astype(jnp.float32),
        lax.psum_scatter(
            summed[3].astype(jnp.bfloat16), ("fsdp", "ctx"), scatter_dimension=1, tiled=True
        ).astype(jnp.float32),
        lax.psum_scatter(
            summed[4].astype(jnp.bfloat16), ("fsdp", "ctx"), scatter_dimension=1, tiled=True
        ).astype(jnp.float32),
    )
    updated = [
        adam_update(master, first_moment, second_moment, gradient, learn_rate, decay_flag)
        for master, first_moment, second_moment, gradient, learn_rate, decay_flag in zip(
            masters, firsts, seconds, summed, learn_rates, decay_flags
        )
    ]
    return (
        jnp.stack(mixed_parts),
        jnp.stack(input_parts),
        updated[0][0],
        updated[0][1],
        updated[0][2],
        updated[0][2].astype(jnp.bfloat16),
        updated[1][0],
        updated[1][1],
        updated[1][2],
        updated[1][2].astype(jnp.bfloat16),
        updated[2][0],
        updated[2][1],
        updated[2][2],
        updated[2][2].astype(jnp.bfloat16),
        updated[3][0],
        updated[3][1],
        updated[3][2],
        updated[3][2].astype(jnp.bfloat16),
        updated[4][0],
        updated[4][1],
        updated[4][2],
    )


def solution(mesh):
    placed = (
        P(None, "fsdp", "ctx", None),
        P(None, "fsdp", "ctx", None),
        P(None, "fsdp"),
        P(None, "fsdp", None),
        P(("fsdp", "ctx"), "tp"),
        P(("fsdp", "ctx"), "tp"),
        P(("fsdp", "ctx"), "tp"),
        P("tp", ("fsdp", "ctx")),
        P("tp", ("fsdp", "ctx")),
        P("tp", ("fsdp", "ctx")),
        P(("fsdp", "ctx"), "tp"),
        P(("fsdp", "ctx"), "tp"),
        P(("fsdp", "ctx"), "tp"),
        P("tp", ("fsdp", "ctx")),
        P("tp", ("fsdp", "ctx")),
        P("tp", ("fsdp", "ctx")),
        P(None, ("fsdp", "ctx")),
        P(None, ("fsdp", "ctx")),
        P(None, ("fsdp", "ctx")),
    )
    return jax.shard_map(
        on_device,
        mesh=mesh,
        in_specs=placed,
        out_specs=(
            P(None, "fsdp", "ctx", None),
            P(None, "fsdp", "ctx", None),
            P(("fsdp", "ctx"), "tp"),
            P(("fsdp", "ctx"), "tp"),
            P(("fsdp", "ctx"), "tp"),
            P(("fsdp", "ctx"), "tp"),
            P("tp", ("fsdp", "ctx")),
            P("tp", ("fsdp", "ctx")),
            P("tp", ("fsdp", "ctx")),
            P("tp", ("fsdp", "ctx")),
            P(("fsdp", "ctx"), "tp"),
            P(("fsdp", "ctx"), "tp"),
            P(("fsdp", "ctx"), "tp"),
            P(("fsdp", "ctx"), "tp"),
            P("tp", ("fsdp", "ctx")),
            P("tp", ("fsdp", "ctx")),
            P("tp", ("fsdp", "ctx")),
            P("tp", ("fsdp", "ctx")),
            P(None, ("fsdp", "ctx")),
            P(None, ("fsdp", "ctx")),
            P(None, ("fsdp", "ctx")),
        ),
        check_vma=False,
    )
```

profile of v0, /device:TPU:0, one launch (start us, length us, event | category | flops | bytes accessed | tf_op | source)
XLA Modules:
  0.0 1488.2 jit_solution(15997899855558807795)
XLA Ops:
  15.0 10.4 all-gather.3
  31.0 23.4 %all-gather.9.cloned.1.call-done = bf16[2560,960]{1,0:T(8,128)(2,1)} async-done(((bf16[320,960]{1,0:T(8,128)(2,1)}), bf16[2560,960]{1,0:T(8,128)(2,1)}) %all-gather.9.cloned.1.call-update) | async-done | bytes 4915216 | tf_op jit(solution)/shard_map/all_gather | solution.py:70
  54.4 7.9 copy.205
  62.3 4.8 fusion.162
  71.5 6.2 all_gather.32
  79.2 8.4 all-gather.2
  87.7 6.2 all_gather.25
  94.0 6.2 all-gather
  100.2 6.2 all_gather.30
  106.4 6.7 all-gather.1
  132.7 4.4 fusion.58
  141.7 3.9 convert_element_type.948
  148.5 140.6 %all-reduce.11.cloned.1.call-done = (bf16[1,256,2560]{2,1,0:T(8,128)(2,1)}, bf16[1,256,2560]{2,1,0:T(8,128)(2,1)}, bf16[1,256,2560]{2,1,0:T(8,128)(2,1)}) async-done(((bf16[1,256,2560]{2,1,0:T(8,128)(2,1)}, bf16[1,256,2560]{2,1,0:T(8,128)(2,1)}, bf16[1,256,2560]{2,1,0:T(8,128)(2,1)}), (bf16[1,256,2560]{2,1,0:T(8,128)(2,1)}, bf16[1,256,2560]{2,1,0:T(8,128)(2,1)}, ...) | async-done | bytes 3932176 | tf_op jit(solution)/shard_map/psum | solution.py:210
  289.1 4.7 multiply_reduce_fusion.2
  293.9 93.1 %all-gather.13.cloned.1.call-done = bf16[2560,3584]{1,0:T(8,128)(2,1)} async-done(((bf16[320,3584]{1,0:T(8,128)(2,1)}), bf16[2560,3584]{1,0:T(8,128)(2,1)}) %all-gather.13.cloned.1.call-update) | async-done | bytes 18350096 | tf_op jit(solution)/shard_map/all_gather | solution.py:74
  387.0 13.5 convolution_bitcast_fusion
  400.5 11.2 convolution_bitcast_fusion.1
  411.7 10.8 convolution_bitcast_fusion.2
  422.5 24.5 %all-gather.15.cloned.1.call-done = bf16[1792,2560]{0,1:T(8,128)(2,1)} async-done(((bf16[1792,320]{0,1:T(8,128)(2,1)}), bf16[1792,2560]{0,1:T(8,128)(2,1)}) %all-gather.15.cloned.1.call-update) | async-done | bytes 9175056 | tf_op jit(solution)/shard_map/all_gather | solution.py:75
  447.0 8.2 multiply_convert_fusion.4
  458.0 4.1 multiply_convert_fusion.6
  462.1 4.1 multiply_convert_fusion.8
  466.2 10.6 fusion.55
  476.8 10.0 fusion.53
  486.8 10.0 fusion.54
  500.8 8.1 fusion.61
  508.9 7.4 fusion.60
  516.4 3.6 fusion.59
  520.0 124.2 %all-reduce.9.cloned.1.call-done = (bf16[1,256,2560]{2,1,0:T(8,128)(2,1)}, bf16[1,256,2560]{2,1,0:T(8,128)(2,1)}, bf16[1,256,2560]{2,1,0:T(8,128)(2,1)}) async-done(((bf16[1,256,2560]{2,1,0:T(8,128)(2,1)}, bf16[1,256,2560]{2,1,0:T(8,128)(2,1)}, bf16[1,256,2560]{2,1,0:T(8,128)(2,1)}), (bf16[1,256,2560]{2,1,0:T(8,128)(2,1)}, bf16[1,256,2560]{2,1,0:T(8,128)(2,1)}, ...) | async-done | bytes 3932176 | tf_op jit(solution)/shard_map/psum | solution.py:253
  644.2 6.5 fusion.118
  658.3 5.2 fusion.32
  667.7 4.0 fusion.249
  671.8 5.6 fusion.111
  682.0 3.9 fusion.270
  689.3 5.6 fusion.31
  697.2 6.6 fusion.290
  705.1 8.5 fusion.30
  717.7 3.9 fusion.255
  721.7 6.5 fusion.293
  732.3 4.3 fusion.283
  736.9 6.6 fusion.296
  747.4 7.4 reduce-scatter.18.cloned.1.call-done
  755.8 22.6 %reduce-scatter.20.cloned.1.call-done = bf16[1,256,2,80]{1,3,2,0:T(8,128)(2,1)} async-done(((bf16[1,1024,2,80]{1,3,2,0:T(8,128)(2,1)}), bf16[1,256,2,80]{1,3,2,0:T(8,128)(2,1)}) %reduce-scatter.20.cloned.1.call-update) | async-done | bytes 81936 | tf_op jit(solution)/shard_map/reduce_scatter | solution.py:322
  780.3 21.7 %reduce-scatter.14.cloned.1.call-done = bf16[1,256,2,80]{1,3,2,0:T(8,128)(2,1)} async-done(((bf16[1,1024,2,80]{1,3,2,0:T(8,128)(2,1)}), bf16[1,256,2,80]{1,3,2,0:T(8,128)(2,1)}) %reduce-scatter.14.cloned.1.call-update) | async-done | bytes 81936 | tf_op jit(solution)/shard_map/reduce_scatter | solution.py:319
  802.9 22.6 %reduce-scatter.16.cloned.1.call-done = bf16[1,256,2,80]{1,3,2,0:T(8,128)(2,1)} async-done(((bf16[1,1024,2,80]{1,3,2,0:T(8,128)(2,1)}), bf16[1,256,2,80]{1,3,2,0:T(8,128)(2,1)}) %reduce-scatter.16.cloned.1.call-update) | async-done | bytes 81936 | tf_op jit(solution)/shard_map/reduce_scatter | solution.py:322
  826.6 5.4 fusion.64
  832.0 5.3 fusion.62
  851.9 5.6 fusion.199
  857.5 6.8 add_convert_fusion.2
  865.5 10.2 fusion.181
  875.8 10.5 fusion.177
  888.1 227.5 %all-reduce.7.cloned.1.call-done = (bf16[1,256,2560]{2,1,0:T(8,128)(2,1)}, bf16[1,256,2560]{2,1,0:T(8,128)(2,1)}, bf16[1,256,2560]{2,1,0:T(8,128)(2,1)}, bf16[1,...) async-done(((bf16[1,256,2560]{2,1,0:T(8,128)(2,1)}, bf16[1,256,2560]{2,1,0:T(8,128)(2,1)}, bf16[1,256,2560]{2,1,0:T(8,128)(2,1)}, ...) | async-done | bytes 7864336 | tf_op jit(solution)/shard_map/psum | solution.py:229
  1115.7 8.9 fusion.122
  1126.3 19.0 %add_convert_fusion.1 = bf16[1792,2560]{0,1:T(8,128)(2,1)} fusion(f32[1792,2560]{0,1:T(8,128)} %fusion.181, f32[1792,2560]{0,1:T(8,128)} %fusion.177, bf16[256,1792]{1,0:T(8,128)(2,1)S(1)} %copy-done.36, f32[256]{0:T(256)} %bitcast.867, bf16[3,1,256,2560]{3,2,1,0:T(8,128)(2,1)} %param.20), kind=kOutput, calls=%fused_computation.1 | convolution fusion | flops 2364538880 | bytes 48104448 | tf_op jit(solution)/shard_map/src,srd->cd/dot_general | solution.py:239
  1146.6 19.8 %fusion.300 = f32[2560,3584]{1,0:T(8,128)} fusion(bf16[1,256,1792]{2,1,0:T(8,128)(2,1)} %copy-done.79, bf16[1,256,1792]{2,1,0:T(8,128)(2,1)S(1)} %copy-done.78, bf16[1,256,2560]{2,1,0:T(8,128)(2,1)} %get-tuple-element.62, f32[2560]{0:T(1024)S(1)} %get-tuple-element.47, f32[256]{0:T(256)S(1)} %copy-done.130, bf16[3,1,256,2560]{3,2,1,0:T(8,128)(2,1)} %param.19), kind=kOutput, calls=%fused_computation.322 | convolution fusion | flops 4705222656 | bytes 41167872 | tf_op jit(solution)/shard_map/srd,src->dc/dot_general | solution.py:250
  1166.4 18.9 %fusion.299 = f32[2560,3584]{1,0:T(8,128)} fusion(bf16[1,256,1792]{2,1,0:T(8,128)(2,1)S(1)} %copy-done.76, bf16[1,256,1792]{2,1,0:T(8,128)(2,1)S(1)} %copy-done.74, bf16[1,256,2560]{2,1,0:T(8,128)(2,1)S(1)} %copy-done.16, f32[256]{0:T(256)S(1)} %copy-done.127, f32[2560]{0:T(1024)S(1)} %get-tuple-element.47, bf16[3,1,256,2560]{3,2,1,0:T(8,128)(2,1)} %param.19), kind=kOutput, calls=%fused_computation.321 | convolution fusion | flops 4705222656 | bytes 41167872 | tf_op jit(solution)/shard_map/srd,src->dc/dot_general | solution.py:250
  1185.2 33.2 %add_convert_fusion = bf16[2560,3584]{1,0:T(8,128)(2,1)} fusion(f32[2560,3584]{1,0:T(8,128)} %fusion.300, f32[2560,3584]{1,0:T(8,128)} %fusion.299, bf16[1,256,1792]{2,1,0:T(8,128)(2,1)} %copy-done.72, bf16[1,256,1792]{2,1,0:T(8,128)(2,1)S(1)} %copy-done.71, bf16[1,256,2560]{2,1,0:T(8,128)(2,1)S(1)} %copy-done.12, f32[256]{0:T(256)S(1)} %copy-done.121, ...), kind=kOutput, calls=%fused_computation | convolution fusion | flops 4732747776 | bytes 96218112 | tf_op jit(solution)/shard_map/srd,src->dc/dot_general | solution.py:250
  1225.6 5.4 fusion.428
  1231.1 5.8 fusion.114
  1242.6 21.5 %reduce-scatter.34.cloned.1.call-done = bf16[320,2]{1,0:T(8,128)(2,1)} async-done(((bf16[2560,2]{1,0:T(8,128)(2,1)}), bf16[320,2]{1,0:T(8,128)(2,1)}) %reduce-scatter.34.cloned.1.call-update) | async-done | bytes 1296
  1265.7 77.4 %reduce-scatter.32.cloned.1.call-done = bf16[1792,320]{0,1:T(8,128)(2,1)} async-done(((bf16[1792,2560]{0,1:T(8,128)(2,1)}), bf16[1792,320]{0,1:T(8,128)(2,1)}) %reduce-scatter.32.cloned.1.call-update) | async-done | bytes 1146896 | tf_op jit(solution)/shard_map/reduce_scatter | solution.py:368
  1343.1 7.1 fusion.419
  1350.2 119.8 %reduce-scatter.30.cloned.1.call-done = bf16[320,3584]{1,0:T(8,128)(2,1)} async-done(((bf16[2560,3584]{1,0:T(8,128)(2,1)}), bf16[320,3584]{1,0:T(8,128)(2,1)}) %reduce-scatter.30.cloned.1.call-update) | async-done | bytes 2293776 | tf_op jit(solution)/shard_map/reduce_scatter | solution.py:365
  1469.9 11.2 fusion.422
  (502 shorter events, 127.6 us)
Async XLA Ops:
  7.2 47.2 %all-gather.9.cloned.1.call-start = ((), (), s32[]{:S(2)}) async-start(), calls=%async_computation.11 | async-start | bytes 5898240 | tf_op jit(solution)/shard_map/all_gather | solution.py:70
  9.6 123.0 %all-gather.11.cloned.1.call-start = ((), (), s32[]{:S(2)}) async-start(), calls=%async_computation.12 | async-start | bytes 3686400 | tf_op jit(solution)/shard_map/all_gather | solution.py:73
  10.5 278.6 %all-reduce.11.cloned.1.call-start = ((), (), s32[]{:S(2)}) async-start(), calls=%async_computation.28 | async-start | bytes 7864320 | tf_op jit(solution)/shard_map/psum | solution.py:210
  25.5 44.2 %copy-start.82 = (f32[2560]{0:T(1024)}, f32[2560]{0:T(1024)S(1)}, u32[]{:S(2)}) copy-start(f32[2560]{0:T(1024)S(1)} %get-tuple-element.48) | copy-start | bytes 30724
  29.3 37.8 %copy-start.122 = (f32[256]{0:T(256)}, f32[256]{0:T(256)S(1)}, u32[]{:S(2)}) copy-start(f32[256]{0:T(256)S(1)} %add_rsqrt_fusion.5) | copy-start | bytes 3076
  29.4 32.9 %copy-start.134 = (f32[256]{0:T(256)}, f32[256]{0:T(256)S(1)}, u32[]{:S(2)}) copy-start(f32[256]{0:T(256)S(1)} %get-tuple-element.173) | copy-start | bytes 3076
  29.4 40.3 %copy-start.131 = (f32[256]{0:T(256)}, f32[256]{0:T(256)S(1)}, u32[]{:S(2)}) copy-start(f32[256]{0:T(256)S(1)} %get-tuple-element.174) | copy-start | bytes 3076
  29.7 93.5 %copy-start.59 = (pred[256,1024]{0,1:T(8,128)(4,1)}, pred[256,1024]{0,1:T(8,128)(4,1)S(1)}, u32[]{:S(2)}) copy-start(pred[256,1024]{0,1:T(8,128)(4,1)S(1)} %compare_and_fusion) | copy-start | bytes 786436
  30.1 96.3 %copy-start.31 = (pred[256,1024]{0,1:T(8,128)(4,1)}, pred[256,1024]{0,1:T(8,128)(4,1)S(1)}, u32[]{:S(2)}) copy-start(pred[256,1024]{0,1:T(8,128)(4,1)S(1)} %compare_and_fusion.2) | copy-start | bytes 786436
  30.4 99.1 %copy-start.57 = (pred[256,1024]{0,1:T(8,128)(4,1)}, pred[256,1024]{0,1:T(8,128)(4,1)S(1)}, u32[]{:S(2)}) copy-start(pred[256,1024]{0,1:T(8,128)(4,1)S(1)} %compare_and_fusion.1) | copy-start | bytes 786436
  31.0 40.4 %copy-start.66 = (f32[256,40]{0,1:T(8,128)}, f32[256,40]{0,1:T(8,128)S(1)}, u32[]{:S(2)}) copy-start(f32[256,40]{0,1:T(8,128)S(1)} %get-tuple-element.152) | copy-start | bytes 122884
  31.0 40.4 %copy-start.68 = (f32[256,40]{0,1:T(8,128)}, f32[256,40]{0,1:T(8,128)S(1)}, u32[]{:S(2)}) copy-start(f32[256,40]{0,1:T(8,128)S(1)} %get-tuple-element.153) | copy-start | bytes 122884
  31.0 82.1 %copy-start.38 = (f32[256,40]{0,1:T(8,128)}, f32[256,40]{0,1:T(8,128)S(1)}, u32[]{:S(2)}) copy-start(f32[256,40]{0,1:T(8,128)S(1)} %get-tuple-element.154) | copy-start | bytes 122884
  31.0 82.1 %copy-start.44 = (f32[256,40]{0,1:T(8,128)}, f32[256,40]{0,1:T(8,128)S(1)}, u32[]{:S(2)}) copy-start(f32[256,40]{0,1:T(8,128)S(1)} %get-tuple-element.155) | copy-start | bytes 122884
  31.0 83.8 %copy-start.62 = (f32[256,40]{0,1:T(8,128)}, f32[256,40]{0,1:T(8,128)S(1)}, u32[]{:S(2)}) copy-start(f32[256,40]{0,1:T(8,128)S(1)} %get-tuple-element.143) | copy-start | bytes 122884
  31.0 83.8 %copy-start.64 = (f32[256,40]{0,1:T(8,128)}, f32[256,40]{0,1:T(8,128)S(1)}, u32[]{:S(2)}) copy-start(f32[256,40]{0,1:T(8,128)S(1)} %get-tuple-element.144) | copy-start | bytes 122884
  79.2 44.1 %copy-start.25 = (f32[2,1024,256,4]{2,1,3,0:T(8,128)}, f32[2,1024,256,4]{2,1,3,0:T(8,128)S(1)}, u32[]{:S(2)}) copy-start(f32[2,1024,256,4]{2,1,3,0:T(8,128)S(1)} %get-tuple-element.160) | copy-start | bytes 25165828
  87.6 35.7 %copy-start.95 = (bf16[1,1024,2,1,80]{1,4,2,3,0:T(8,128)(2,1)}, bf16[1,1024,2,1,80]{1,4,2,3,0:T(8,128)(2,1)S(1)}, u32[]{:S(2)}) copy-start(bf16[1,1024,2,1,80]{1,4,2,3,0:T(8,128)(2,1)S(1)} %all-gather.2) | copy-start | bytes 983044
  94.0 20.8 %copy-start.50 = (bf16[1,1024,2,80]{1,3,2,0:T(8,128)(2,1)}, bf16[1,1024,2,80]{1,3,2,0:T(8,128)(2,1)S(1)}, u32[]{:S(2)}) copy-start(bf16[1,1024,2,80]{1,3,2,0:T(8,128)(2,1)S(1)} %all_gather.25) | copy-start | bytes 983044
  100.2 26.2 %copy-start.88 = (bf16[1,1024,2,1,80]{1,4,3,2,0:T(8,128)(2,1)}, bf16[1,1024,2,1,80]{1,4,3,2,0:T(8,128)(2,1)S(1)}, u32[]{:S(2)}) copy-start(bf16[1,1024,2,1,80]{1,4,3,2,0:T(8,128)(2,1)S(1)} %all-gather) | copy-start | bytes 983044
  113.1 16.4 %copy-start.91 = (bf16[1,1024,2,1,80]{1,4,2,3,0:T(8,128)(2,1)}, bf16[1,1024,2,1,80]{1,4,2,3,0:T(8,128)(2,1)S(1)}, u32[]{:S(2)}) copy-start(bf16[1,1024,2,1,80]{1,4,2,3,0:T(8,128)(2,1)S(1)} %all-gather.1) | copy-start | bytes 983044
  114.8 11.6 copy-start.13
  116.9 12.6 copy-start.26
  141.7 245.3 %all-gather.13.cloned.1.call-start = ((), (), s32[]{:S(2)}) async-start(), calls=%async_computation.13 | async-start | bytes 20643840 | tf_op jit(solution)/shard_map/all_gather | solution.py:74
  145.7 301.3 %all-gather.15.cloned.1.call-start = ((), (), s32[]{:S(2)}) async-start(), calls=%async_computation.14 | async-start | bytes 10321920 | tf_op jit(solution)/shard_map/all_gather | solution.py:75
  148.5 495.7 %all-reduce.9.cloned.1.call-start = ((), (), s32[]{:S(2)}) async-start(), calls=%async_computation.27 | async-start | bytes 7864320 | tf_op jit(solution)/shard_map/psum | solution.py:253
  289.1 97.9 %copy-start.10 = (bf16[1,256,2560]{2,1,0:T(8,128)(2,1)S(1)}, bf16[1,256,2560]{2,1,0:T(8,128)(2,1)}, u32[]{:S(2)}) copy-start(bf16[1,256,2560]{2,1,0:T(8,128)(2,1)} %get-tuple-element.61) | copy-start | bytes 3932164
  293.8 356.9 %copy-start.120 = (f32[256]{0:T(256)}, f32[256]{0:T(256)S(1)}, u32[]{:S(2)}) copy-start(f32[256]{0:T(256)S(1)} %add_rsqrt_fusion) | copy-start | bytes 3076
  293.8 106.7 %copy-start.125 = (f32[256]{0:T(256)}, f32[256]{0:T(256)S(1)}, u32[]{:S(2)}) copy-start(f32[256]{0:T(256)S(1)} %add_rsqrt_fusion.2) | copy-start | bytes 3076
  293.8 117.9 %copy-start.128 = (f32[256]{0:T(256)}, f32[256]{0:T(256)S(1)}, u32[]{:S(2)}) copy-start(f32[256]{0:T(256)S(1)} %add_rsqrt_fusion.4) | copy-start | bytes 3076
  387.0 13.6 copy-start.1
  387.0 13.6 copy-start.14
  455.3 45.6 %copy-start.35 = (bf16[256,1792]{1,0:T(8,128)(2,1)}, bf16[256,1792]{1,0:T(8,128)(2,1)S(1)}, u32[]{:S(2)}) copy-start(bf16[256,1792]{1,0:T(8,128)(2,1)S(1)} %get-tuple-element.105) | copy-start | bytes 2752516
  462.1 24.8 %copy-start.73 = (bf16[1,256,1792]{2,1,0:T(8,128)(2,1)}, bf16[1,256,1792]{2,1,0:T(8,128)(2,1)S(1)}, u32[]{:S(2)}) copy-start(bf16[1,256,1792]{2,1,0:T(8,128)(2,1)S(1)} %get-tuple-element.91) | copy-start | bytes 2752516
  462.1 24.8 %copy-start.75 = (bf16[1,256,1792]{2,1,0:T(8,128)(2,1)}, bf16[1,256,1792]{2,1,0:T(8,128)(2,1)S(1)}, u32[]{:S(2)}) copy-start(bf16[1,256,1792]{2,1,0:T(8,128)(2,1)S(1)} %get-tuple-element.92) | copy-start | bytes 2752516
  496.8 248.5 %reduce-scatter.22.cloned.1.call-start = ((), (), s32[]{:S(2)}) async-start(), calls=%async_computation.19 | async-start | bytes 409600 | tf_op jit(solution)/shard_map/reduce_scatter | solution.py:319
  500.8 15.5 %slice-start.2 = ((s8[9175040]{0:T(1024)(128)(4,1)}), s8[4194304]{0:T(1024)(128)(4,1)S(1)}, s32[]{:S(2)}) async-start(s8[9175040]{0:T(1024)(128)(4,1)} %bitcast.875), calls=%async_computation.31 | async-start | bytes 8388608
  500.8 15.5 %slice-start.3 = ((s8[9175040]{0:T(1024)(128)(4,1)}), s8[4194304]{0:T(1024)(128)(4,1)S(1)}, s32[]{:S(2)}) async-start(s8[9175040]{0:T(1024)(128)(4,1)} %bitcast.875), calls=%async_computation.32 | async-start | bytes 8388608
  653.7 190.9 %copy-start.5 = (f32[1,256,2560]{2,1,0:T(8,128)}, f32[1,256,2560]{2,1,0:T(8,128)S(1)}, u32[]{:S(2)}) copy-start(f32[1,256,2560]{2,1,0:T(8,128)S(1)} %fusion.105) | copy-start | bytes 7864324
  687.9 58.4 %reduce-scatter.24.cloned.1.call-start = ((), (), s32[]{:S(2)}) async-start(), calls=%async_computation.20 | async-start | bytes 409600 | tf_op jit(solution)/shard_map/reduce_scatter | solution.py:322
  703.8 51.0 %reduce-scatter.18.cloned.1.call-start = ((), (), s32[]{:S(2)}) async-start(), calls=%async_computation.17 | async-start | bytes 409600 | tf_op jit(solution)/shard_map/reduce_scatter | solution.py:319
  721.7 56.7 %reduce-scatter.20.cloned.1.call-start = ((), (), s32[]{:S(2)}) async-start(), calls=%async_computation.18 | async-start | bytes 409600 | tf_op jit(solution)/shard_map/reduce_scatter | solution.py:322
  728.2 73.7 %reduce-scatter.14.cloned.1.call-start = ((), (), s32[]{:S(2)}) async-start(), calls=%async_computation.15 | async-start | bytes 409600 | tf_op jit(solution)/shard_map/reduce_scatter | solution.py:319
  736.7 88.9 %reduce-scatter.16.cloned.1.call-start = ((), (), s32[]{:S(2)}) async-start(), calls=%async_computation.16 | async-start | bytes 409600 | tf_op jit(solution)/shard_map/reduce_scatter | solution.py:322
  743.6 372.1 %all-reduce.7.cloned.1.call-start = ((), (), s32[]{:S(2)}) async-start(), calls=%async_computation.26 | async-start | bytes 15728640 | tf_op jit(solution)/shard_map/psum | solution.py:229
  840.0 378.5 %reduce-scatter.28.cloned.1.call-start = ((), (), s32[]{:S(2)}) async-start(), calls=%async_computation.22 | async-start | bytes 3686400 | tf_op jit(solution)/shard_map/reduce_scatter | solution.py:362
  847.7 377.9 %reduce-scatter.26.cloned.1.call-start = ((), (), s32[]{:S(2)}) async-start(), calls=%async_computation.21 | async-start | bytes 5898240 | tf_op jit(solution)/shard_map/reduce_scatter | solution.py:359
  864.4 11.4 copy-start.54
  864.4 399.7 %reduce-scatter.34.cloned.1.call-start = ((), (), s32[]{:S(2)}) async-start(), calls=%async_computation.25 | async-start | bytes 737280
  875.8 11.7 copy-start.109
  875.8 239.9 %copy-start.12 = (bf16[1,256,2560]{2,1,0:T(8,128)(2,1)S(1)}, bf16[1,256,2560]{2,1,0:T(8,128)(2,1)}, u32[]{:S(2)}) copy-start(bf16[1,256,2560]{2,1,0:T(8,128)(2,1)} %get-tuple-element.61) | copy-start | bytes 3932164
  875.8 239.8 %copy-start.18 = (bf16[1,256,2560]{2,1,0:T(8,128)(2,1)S(1)}, bf16[1,256,2560]{2,1,0:T(8,128)(2,1)}, u32[]{:S(2)}) copy-start(bf16[1,256,2560]{2,1,0:T(8,128)(2,1)} %get-tuple-element.62) | copy-start | bytes 3932164
  1125.9 217.2 %reduce-scatter.32.cloned.1.call-start = ((), (), s32[]{:S(2)}) async-start(), calls=%async_computation.24 | async-start | bytes 10321920 | tf_op jit(solution)/shard_map/reduce_scatter | solution.py:368
  1145.4 21.0 %copy-start.16 = (bf16[1,256,2560]{2,1,0:T(8,128)(2,1)S(1)}, bf16[1,256,2560]{2,1,0:T(8,128)(2,1)}, u32[]{:S(2)}) copy-start(bf16[1,256,2560]{2,1,0:T(8,128)(2,1)} %get-tuple-element.63) | copy-start | bytes 3932164
  1145.4 324.6 %reduce-scatter.30.cloned.1.call-start = ((), (), s32[]{:S(2)}) async-start(), calls=%async_computation.23 | async-start | bytes 20643840 | tf_op jit(solution)/shard_map/reduce_scatter | solution.py:365
  1146.5 19.8 %copy-start.74 = (bf16[1,256,1792]{2,1,0:T(8,128)(2,1)S(1)}, bf16[1,256,1792]{2,1,0:T(8,128)(2,1)}, u32[]{:S(2)}) copy-start(bf16[1,256,1792]{2,1,0:T(8,128)(2,1)} %copy-done.73) | copy-start | bytes 2752516
  1146.5 19.8 %copy-start.76 = (bf16[1,256,1792]{2,1,0:T(8,128)(2,1)S(1)}, bf16[1,256,1792]{2,1,0:T(8,128)(2,1)}, u32[]{:S(2)}) copy-start(bf16[1,256,1792]{2,1,0:T(8,128)(2,1)} %copy-done.75) | copy-start | bytes 2752516
  1146.5 19.8 %copy-start.127 = (f32[256]{0:T(256)S(1)}, f32[256]{0:T(256)}, u32[]{:S(2)}) copy-start(f32[256]{0:T(256)} %copy-done.125) | copy-start | bytes 3076
  1166.4 18.9 %copy-start.71 = (bf16[1,256,1792]{2,1,0:T(8,128)(2,1)S(1)}, bf16[1,256,1792]{2,1,0:T(8,128)(2,1)}, u32[]{:S(2)}) copy-start(bf16[1,256,1792]{2,1,0:T(8,128)(2,1)} %copy-done.70) | copy-start | bytes 2752516
  1166.4 18.9 %copy-start.121 = (f32[256]{0:T(256)S(1)}, f32[256]{0:T(256)}, u32[]{:S(2)}) copy-start(f32[256]{0:T(256)} %copy-done.120) | copy-start | bytes 3076
  1239.1 25.9 %copy-start.138 = (f32[2,320]{1,0:T(2,128)S(1)}, f32[2,320]{1,0:T(2,128)}, u32[]{:S(2)}) copy-start(f32[2,320]{1,0:T(2,128)} %param.35) | copy-start | bytes 7684
  1239.1 25.9 %copy-start.155 = (f32[2,320]{1,0:T(2,128)S(1)}, f32[2,320]{1,0:T(2,128)}, u32[]{:S(2)}) copy-start(f32[2,320]{1,0:T(2,128)} %param.37) | copy-start | bytes 7684
  1239.1 25.9 %copy-start.156 = (f32[2,320]{1,0:T(2,128)S(1)}, f32[2,320]{1,0:T(2,128)}, u32[]{:S(2)}) copy-start(f32[2,320]{1,0:T(2,128)} %param.36) | copy-start | bytes 7684
  1239.1 104.0 %copy-start.24 = (f32[1792,320]{0,1:T(8,128)S(1)}, f32[1792,320]{0,1:T(8,128)}, u32[]{:S(2)}) copy-start(f32[1792,320]{0,1:T(8,128)} %param.32) | copy-start | bytes 6881284
  (123 other events, 682.4 us)
Sparse Core Ops, SparseCore 0:
  10.5 43.8 all-gather.8
  56.8 34.4 all-gather.10
  141.8 147.2 all-reduce.10
  291.4 95.5 all-gather.12
  389.3 57.7 all-gather.14
  496.9 147.1 all-reduce.8
  688.0 19.4 reduce-scatter.21
  710.7 20.4 reduce-scatter.23
  734.3 20.4 reduce-scatter.17
  757.9 20.4 reduce-scatter.19
  781.4 20.4 reduce-scatter.13
  805.0 20.4 reduce-scatter.15
  840.1 275.4 all-reduce.6
  1119.5 45.6 reduce-scatter.27
  1169.0 56.5 reduce-scatter.25
  1229.5 34.5 reduce-scatter.33
  1268.0 75.0 reduce-scatter.31
  1346.6 123.2 reduce-scatter.29
where the time goes:
time: 1500 us; the launch traced here: 1490 us
  waiting for transfers between devices  929 us (62%)
  matrix products  344 us (23%)
  other arithmetic  113 us (8%)
  blocking collectives  50.2 us (3%)
  local copies, waits for them, and re-layouts  33.5 us (2%)
  between operations  16.5 us (1%)
    psum x1, waiting for transfers between devices, on_device(): lax.psum(expand_part.astype(jnp.bfloat16), 'tp').astype(jnp.float32)  228 us
    psum x1, waiting for transfers between devices, on_device(): lax.psum(attend_part.astype(jnp.bfloat16), 'tp').astype(jnp.float32)  141 us
    psum x1, waiting for transfers between devices, on_device(): lax.psum(jnp.einsum('src,dc->srd', grad_pair, pair_proj, preferred_elemen...  124 us
    reduce_scatter x1, waiting for transfers between devices, on_device(): lax.psum_scatter(summed[2].astype(jnp.bfloat16), ('fsdp', 'ctx'), scatter...  120 us
    all_gather x1, waiting for transfers between devices, fetch_weights(): lax.all_gather(gate_up.astype(jnp.bfloat16), ('fsdp', 'ctx'), axis=0, til...  93.1 us
    reduce_scatter x1, waiting for transfers between devices, on_device(): lax.psum_scatter(summed[3].astype(jnp.bfloat16), ('fsdp', 'ctx'), scatter...  77.4 us
    dot_general x3, matrix products, on_device(): jnp.einsum('srd,src->dc', second_normalized, grad_pair, preferred_element...  71.8 us
    reduce_scatter x3, waiting for transfers between devices, on_device(): lax.psum_scatter(grad_values_all.astype(jnp.bfloat16), 'ctx', scatter_dim...  45.3 us
  transfers between devices with their start and end apart: 18, of which 14 were waited for; matrix products, arithmetic and copies ran while one was open for 24% of the time, Pallas kernels for 0%

commit v1 on v0

v1 whole, which is shorter than its diff:
```python
import functools

import jax
import jax.numpy as jnp
from jax import lax
from jax.experimental import pallas as pl
from jax.experimental.pallas import tpu as pltpu
from jax.sharding import PartitionSpec as P

QUERY_HEADS = 32
KEY_VALUE_HEADS = 8
HEAD_DIMENSION = 80
STEP = 10
GROUP = QUERY_HEADS // KEY_VALUE_HEADS

rope_base = 1000000.0
norm_eps = 1e-05
beta_one = 0.9
beta_two = 0.95
adam_eps = 1e-08
weight_decay = 0.1
learn_rates = (0.1, 0.5, 0.05, 0.04, 0.8)
decay_flags = (1.0, 1.0, 1.0, 1.0, 0.0)
neg_big = -1e30
log2_e = 1.4426950408889634
MESH = pl.DeviceIdType.MESH
VMEM = pltpu.VMEM


def adam_update(weight, moment, second, gradient, learn_rate, decay_flag):
    moment = beta_one * moment + (1.0 - beta_one) * gradient
    second = beta_two * second + (1.0 - beta_two) * gradient * gradient
    moment_hat = moment / (1.0 - beta_one**STEP)
    second_hat = second / (1.0 - beta_two**STEP)
    weight = weight - learn_rate * (
        moment_hat / (jnp.sqrt(second_hat) + adam_eps) + decay_flag * weight_decay * weight
    )
    return (moment, second, weight)


def line_body(
    n, chunks, chunk_rows, lag, p_ref, o_ref, inbox, red_send, red_recv, back_send, back_recv
):
    z = lax.axis_index("tp")
    half = chunks * chunk_rows
    barrier = pltpu.get_barrier_semaphore()

    @pl.when(z > 0)
    def _():
        pl.semaphore_signal(barrier, inc=1, device_id={"tp": z - 1}, device_id_type=MESH)

    @pl.when(z < n - 1)
    def _():
        pl.semaphore_signal(barrier, inc=1, device_id={"tp": z + 1}, device_id_type=MESH)

    pl.semaphore_wait(barrier, (z > 0).astype(jnp.int32) + (z < n - 1).astype(jnp.int32))

    def rows_of(flow, k):
        return pl.ds(pl.multiple_of(flow * half + k * chunk_rows, chunk_rows), chunk_rows)

    def hop_of(flow):
        return (n - 1 - z) if flow == 0 else z

    def onward(flow):
        return {"tp": jnp.maximum(z - 1, 0) if flow == 0 else jnp.minimum(z + 1, n - 1)}

    def backward(flow):
        return {"tp": jnp.minimum(z + 1, n - 1) if flow == 0 else jnp.maximum(z - 1, 0)}

    def reduce_copy(flow, k, source):
        return pltpu.make_async_remote_copy(
            src_ref=source,
            dst_ref=inbox.at[rows_of(flow, k)],
            send_sem=red_send.at[flow, k],
            recv_sem=red_recv.at[flow, k],
            device_id=onward(flow),
            device_id_type=MESH,
        )

    def back_copy(flow, k):
        rows = rows_of(flow, k)
        return pltpu.make_async_remote_copy(
            src_ref=o_ref.at[rows],
            dst_ref=o_ref.at[rows],
            send_sem=back_send.at[flow, k],
            recv_sem=back_recv.at[flow, k],
            device_id=backward(flow),
            device_id_type=MESH,
        )

    def added(rows):
        return (inbox[rows, :].astype(jnp.float32) + p_ref[rows, :].astype(jnp.float32)).astype(
            jnp.bfloat16
        )

    def step(t, carry):
        for flow in (0, 1):
            hop = hop_of(flow)
            k = t - hop * lag

            @pl.when((k >= 0) & (k < chunks))
            def _():
                rows = rows_of(flow, k)

                @pl.when(hop == 0)
                def _():
                    reduce_copy(flow, k, p_ref.at[rows]).start()

                @pl.when((hop > 0) & (hop < n - 1))
                def _():
                    reduce_copy(flow, k, p_ref.at[rows]).wait_recv()
                    inbox[rows, :] = added(rows)
                    reduce_copy(flow, k, inbox.at[rows]).start()

                @pl.when(hop == n - 1)
                def _():
                    reduce_copy(flow, k, p_ref.at[rows]).wait_recv()
                    o_ref[rows, :] = added(rows)
                    back_copy(flow, k).start()

        for flow in (0, 1):
            hop = hop_of(flow)
            k2 = t - (n - 1) * lag - (n - 1 - hop) * lag

            @pl.when((k2 >= 0) & (k2 < chunks) & (hop < n - 1))
            def _():
                back_copy(flow, k2).wait_recv()

                @pl.when(hop > 0)
                def _():
                    back_copy(flow, k2).start()

        return carry

    lax.fori_loop(0, chunks + 2 * (n - 1) * lag, step, 0)

    def drain(k, carry):
        for flow in (0, 1):
            hop = hop_of(flow)

            @pl.when(hop < n - 1)
            def _():
                reduce_copy(flow, k, p_ref.at[rows_of(flow, k)]).wait_send()

            @pl.when(hop > 0)
            def _():
                back_copy(flow, k).wait_send()

        return carry

    lax.fori_loop(0, chunks, drain, 0)


def line_sum(part, n, ident, chunk_rows=16, lag=2):
    rows, width = part.shape
    chunks = rows // 2 // chunk_rows
    return pl.pallas_call(
        functools.partial(line_body, n, chunks, chunk_rows, lag),
        out_shape=jax.ShapeDtypeStruct((rows, width), jnp.bfloat16),
        in_specs=[pl.BlockSpec(memory_space=VMEM)],
        out_specs=pl.BlockSpec(memory_space=VMEM),
        scratch_shapes=[VMEM((rows, width), jnp.bfloat16)]
        + [pltpu.SemaphoreType.DMA((2, chunks))] * 4,
        compiler_params=pltpu.CompilerParams(
            collective_id=ident, has_side_effects=True, vmem_limit_bytes=48 * 2**20
        ),
        cost_estimate=pl.CostEstimate(
            flops=rows * width, bytes_accessed=80 * rows * width, transcendentals=0
        ),
        name="line_sum",
    )(part)


def greet(n):
    me = lax.axis_index("ctx")
    barrier = pltpu.get_barrier_semaphore()
    for step in range(1, n):
        pl.semaphore_signal(
            barrier, inc=1, device_id={"ctx": lax.rem(me + step, n)}, device_id_type=MESH
        )
    pl.semaphore_wait(barrier, n - 1)
    return me


def turn(first, second, cosine, sine):
    return jnp.concatenate([first * cosine - second * sine, second * cosine + first * sine], 0)


def turn_back(first, second, cosine, sine):
    return jnp.concatenate([first * cosine + second * sine, second * cosine - first * sine], 0)


def mask_bias(key_position, query_position, length):
    allowed = (key_position <= query_position) & (key_position < length)
    return jnp.where(allowed, 0.0, neg_big)


def attend_body(
    n,
    groups,
    proj_ref,
    cos_ref,
    sin_ref,
    key_pos_ref,
    query_pos_ref,
    length_ref,
    q_ref,
    kv_ref,
    full_ref,
    low_ref,
    log_ref,
    bias,
    send_sem,
    recv_sem,
):
    me = greet(n)
    seqs, _, rows = q_ref.shape
    dim = HEAD_DIMENSION
    half = dim // 2
    group_width = (GROUP + 2) * dim

    def block(m, col):
        return proj_ref[m, col : col + half, :], proj_ref[m, col + half : col + dim, :]

    def copy(m, step):
        return pltpu.make_async_remote_copy(
            src_ref=kv_ref.at[m, me],
            dst_ref=kv_ref.at[m, me],
            send_sem=send_sem.at[m, step - 1],
            recv_sem=recv_sem.at[m, step - 1],
            device_id={"ctx": lax.rem(me + step, n)},
            device_id_type=MESH,
        )

    def spread(m, carry):
        for g in range(groups):
            col = g * group_width + GROUP * dim
            kv_ref[m, me, g, :dim, :] = turn(*block(m, col), cos_ref[m], sin_ref[m]).astype(
                jnp.bfloat16
            )
            kv_ref[m, me, g, dim:, :] = proj_ref[m, col + dim : col + 2 * dim, :].astype(
                jnp.bfloat16
            )
        for step in range(1, n):
            copy(m, step).start()
        return carry

    lax.fori_loop(0, seqs, spread, 0)

    def sequence(m, carry):
        for g in range(groups):
            for h in range(GROUP):
                low = (g * GROUP + h) * dim
                q_ref[m, low : low + dim, :] = turn(
                    *block(m, g * group_width + h * dim), cos_ref[m], sin_ref[m]
                ).astype(jnp.bfloat16)
        bias[...] = mask_bias(key_pos_ref[m], query_pos_ref[m], length_ref[m])
        for step in range(1, n):
            copy(m, step).wait_recv()
        for g in range(groups):
            for h in range(GROUP):
                low = (g * GROUP + h) * dim
                query = q_ref[m, low : low + dim, :]
                scores = [
                    lax.dot_general(
                        kv_ref[m, j, g, :dim, :],
                        query,
                        (((0,), (0,)), ((), ())),
                        preferred_element_type=jnp.float32,
                    )
                    * (log2_e * dim**-0.5)
                    + bias[j * rows : (j + 1) * rows, :]
                    for j in range(n)
                ]
                top = functools.reduce(
                    jnp.maximum, [jnp.max(s, axis=0, keepdims=True) for s in scores]
                )
                total = jnp.zeros_like(top)
                out = jnp.zeros((dim, rows), jnp.float32)
                for j in range(n):
                    weights = jnp.exp2(scores[j] - top)
                    total += jnp.sum(weights, axis=0, keepdims=True)
                    out += jnp.dot(
                        kv_ref[m, j, g, dim:, :],
                        weights.astype(jnp.bfloat16),
                        preferred_element_type=jnp.float32,
                    )
                out = out / total
                full_ref[m, low : low + dim, :] = out
                low_ref[m, low : low + dim, :] = out.astype(jnp.bfloat16)
                log_ref[m, g * GROUP + h : g * GROUP + h + 1, :] = top + jnp.log2(total)
        return carry

    lax.fori_loop(0, seqs, sequence, 0)

    def drain(m, carry):
        for step in range(1, n):
            copy(m, step).wait_send()
        return carry

    lax.fori_loop(0, seqs, drain, 0)


def attend(projected, cosine, sine, key_pos, query_pos, lengths, n, ident):
    seqs, width, rows = projected.shape
    groups = width // ((GROUP + 2) * HEAD_DIMENSION)
    heads = groups * GROUP
    shape = jax.ShapeDtypeStruct
    vmem = pl.BlockSpec(memory_space=VMEM)
    return pl.pallas_call(
        functools.partial(attend_body, n, groups),
        out_shape=(
            shape((seqs, heads * HEAD_DIMENSION, rows), jnp.bfloat16),
            shape((seqs, n, groups, 2 * HEAD_DIMENSION, rows), jnp.bfloat16),
            shape((seqs, heads * HEAD_DIMENSION, rows), jnp.float32),
            shape((seqs, heads * HEAD_DIMENSION, rows), jnp.bfloat16),
            shape((seqs, heads, rows), jnp.float32),
        ),
        in_specs=[vmem] * 6,
        out_specs=(vmem,) * 5,
        scratch_shapes=[
            VMEM((n * rows, rows), jnp.float32),
            pltpu.SemaphoreType.DMA((seqs, n - 1)),
            pltpu.SemaphoreType.DMA((seqs, n - 1)),
        ],
        compiler_params=pltpu.CompilerParams(
            collective_id=ident, has_side_effects=True, vmem_limit_bytes=56 * 2**20
        ),
        name="attend",
    )(projected, cosine, sine, key_pos, query_pos, lengths)


def attend_back_body(
    n,
    groups,
    q_ref,
    kv_ref,
    full_ref,
    log_ref,
    grad_ref,
    cos_ref,
    sin_ref,
    key_pos_ref,
    query_pos_ref,
    length_ref,
    out_ref,
    bias,
    outbox,
    inbox,
    send_sem,
    recv_sem,
):
    me = greet(n)
    seqs, _, rows = q_ref.shape
    dim = HEAD_DIMENSION
    half = dim // 2
    scale = dim**-0.5
    group_width = (GROUP + 2) * dim

    def copy(m, step):
        to = lax.rem(me + step, n)
        return pltpu.make_async_remote_copy(
            src_ref=outbox.at[m, to],
            dst_ref=inbox.at[m, step - 1],
            send_sem=send_sem.at[m, step - 1],
            recv_sem=recv_sem.at[m, step - 1],
            device_id={"ctx": to},
            device_id_type=MESH,
        )

    def sequence(m, carry):
        bias[...] = mask_bias(key_pos_ref[m], query_pos_ref[m], length_ref[m])
        for g in range(groups):
            key_sums = [jnp.zeros((dim, rows), jnp.float32) for _ in range(n)]
            value_sums = [jnp.zeros((dim, rows), jnp.float32) for _ in range(n)]
            for h in range(GROUP):
                low = (g * GROUP + h) * dim
                query = q_ref[m, low : low + dim, :]
                grad = grad_ref[m, low : low + dim, :]
                delta = jnp.sum(
                    grad.astype(jnp.float32) * full_ref[m, low : low + dim, :],
                    axis=0,
                    keepdims=True,
                )
                log_total = log_ref[m, g * GROUP + h : g * GROUP + h + 1, :]
                query_sum = jnp.zeros((dim, rows), jnp.float32)
                for j in range(n):
                    keys = kv_ref[m, j, g, :dim, :]
                    values = kv_ref[m, j, g, dim:, :]
                    scores = lax.dot_general(
                        keys, query, (((0,), (0,)), ((), ())), preferred_element_type=jnp.float32
                    )
                    probs = jnp.exp2(
                        scores * (log2_e * scale)
                        + (bias[j * rows : (j + 1) * rows, :] - log_total)
                    )
                    grad_probs = lax.dot_general(
                        values, grad, (((0,), (0,)), ((), ())), preferred_element_type=jnp.float32
                    )
                    grad_scores = (probs * (grad_probs - delta)).astype(jnp.bfloat16)
                    query_sum += jnp.dot(keys, grad_scores, preferred_element_type=jnp.float32)
                    key_sums[j] += lax.dot_general(
                        query,
                        grad_scores,
                        (((1,), (1,)), ((), ())),
                        preferred_element_type=jnp.float32,
                    )
                    value_sums[j] += lax.dot_general(
                        grad,
                        probs.astype(jnp.bfloat16),
                        (((1,), (1,)), ((), ())),
                        preferred_element_type=jnp.float32,
                    )
                query_sum = query_sum * scale
                col = g * group_width + h * dim
                out_ref[m, col : col + dim, :] = turn_back(
                    query_sum[:half], query_sum[half:], cos_ref[m], sin_ref[m]
                ).astype(jnp.bfloat16)
            for j in range(n):
                outbox[m, j, g, :dim, :] = (key_sums[j] * scale).astype(jnp.bfloat16)
                outbox[m, j, g, dim:, :] = value_sums[j].astype(jnp.bfloat16)
        for step in range(1, n):
            copy(m, step).start()
        return carry

    lax.fori_loop(0, seqs, sequence, 0)

    def gather(m, carry):
        for step in range(1, n):
            copy(m, step).wait_recv()
        for g in range(groups):
            total = outbox[m, me, g].astype(jnp.float32)
            for step in range(1, n):
                total += inbox[m, step - 1, g].astype(jnp.float32)
            col = g * group_width + GROUP * dim
            out_ref[m, col : col + dim, :] = turn_back(
                total[:half], total[half:dim], cos_ref[m], sin_ref[m]
            ).astype(jnp.bfloat16)
            out_ref[m, col + dim : col + 2 * dim, :] = total[dim:].astype(jnp.bfloat16)
        for step in range(1, n):
            copy(m, step).wait_send()
        return carry

    lax.fori_loop(0, seqs, gather, 0)


def attend_back(
    queries, key_values, full, log_total, grads, cosine, sine, key_pos, query_pos, lengths, n, ident
):
    seqs, width, rows = queries.shape
    groups = key_values.shape[2]
    vmem = pl.BlockSpec(memory_space=VMEM)
    return pl.pallas_call(
        functools.partial(attend_back_body, n, groups),
        out_shape=jax.ShapeDtypeStruct(
            (seqs, groups * (GROUP + 2) * HEAD_DIMENSION, rows), jnp.bfloat16
        ),
        in_specs=[vmem] * 10,
        out_specs=vmem,
        scratch_shapes=[
            VMEM((n * rows, rows), jnp.float32),
            VMEM((seqs, n, groups, 2 * HEAD_DIMENSION, rows), jnp.bfloat16),
            VMEM((seqs, n - 1, groups, 2 * HEAD_DIMENSION, rows), jnp.bfloat16),
            pltpu.SemaphoreType.DMA((seqs, n - 1)),
            pltpu.SemaphoreType.DMA((seqs, n - 1)),
        ],
        compiler_params=pltpu.CompilerParams(
            collective_id=ident, has_side_effects=True, vmem_limit_bytes=56 * 2**20
        ),
        name="attend_back",
    )(queries, key_values, full, log_total, grads, cosine, sine, key_pos, query_pos, lengths)


def grads_body(rows_last, left_ref, right_ref, *rest):
    out_ref, turned = rest[-2:]

    @pl.when(pl.program_id(0) == 0)
    def _():
        turned[...] = left_ref[...].T

    contract = (((1,), (1 if rows_last else 0,)), ((), ()))
    width = turned.shape[0]
    part = 512 if width % 512 == 0 else width
    for low in range(0, width, part):
        out_ref[low : low + part, :] = lax.dot_general(
            turned[low : low + part, :],
            right_ref[...],
            contract,
            preferred_element_type=jnp.float32,
        ).astype(out_ref.dtype)


def grads_into(buffer, columns, first, left, right, rows_last, tile):
    rows, width = left.shape
    n = right.shape[0] if rows_last else right.shape[1]
    in_specs = [
        pl.BlockSpec(memory_space=VMEM),
        pl.BlockSpec((tile, rows), lambda i: (i, 0))
        if rows_last
        else pl.BlockSpec((rows, tile), lambda i: (0, i)),
    ]
    operands = [left, right]
    aliases = {}
    if buffer is not None:
        in_specs.append(pl.BlockSpec(memory_space=pl.ANY))
        operands.append(buffer)
        aliases = {2: 0}
    return pl.pallas_call(
        functools.partial(grads_body, rows_last),
        grid=(n // tile,),
        out_shape=jax.ShapeDtypeStruct((width, columns), jnp.bfloat16),
        in_specs=in_specs,
        out_specs=pl.BlockSpec((width, tile), lambda i: (0, first // tile + i)),
        scratch_shapes=[VMEM((width, rows), jnp.bfloat16)],
        input_output_aliases=aliases,
        compiler_params=pltpu.CompilerParams(vmem_limit_bytes=48 * 2**20),
        cost_estimate=pl.CostEstimate(
            flops=2 * rows * width * n,
            bytes_accessed=2 * (rows * width + rows * n + width * n),
            transcendentals=0,
        ),
        name="weight_grads",
    )(*operands)


def gain_body(ctx_size, x_ref, o_ref, inbox, send_sem, recv_sem):
    shards = x_ref.shape[0]
    me = lax.axis_index("fsdp") * ctx_size + lax.axis_index("ctx")

    def to(step):
        other = lax.rem(me + step, shards)
        return other, {"fsdp": other // ctx_size, "ctx": lax.rem(other, ctx_size)}

    barrier = pltpu.get_barrier_semaphore()
    for step in range(1, shards):
        pl.semaphore_signal(barrier, inc=1, device_id=to(step)[1], device_id_type=MESH)
    pl.semaphore_wait(barrier, shards - 1)

    def copy(step):
        other, where = to(step)
        return pltpu.make_async_remote_copy(
            src_ref=x_ref.at[other],
            dst_ref=inbox.at[step - 1],
            send_sem=send_sem.at[step - 1],
            recv_sem=recv_sem.at[step - 1],
            device_id=where,
            device_id_type=MESH,
        )

    for step in range(1, shards):
        copy(step).start()
    total = x_ref[me]
    for step in range(1, shards):
        copy(step).wait()
        total += inbox[step - 1]
    o_ref[...] = total


def gain_sum(partial, shards, ctx_size, ident):
    two, width = partial.shape
    own = width // shards
    padded = -(-own // 128) * 128
    pieces = jnp.pad(
        partial.reshape(two, shards, own).transpose(1, 0, 2),
        ((0, 0), (0, 8 - two), (0, padded - own)),
    )
    total = pl.pallas_call(
        functools.partial(gain_body, ctx_size),
        out_shape=jax.ShapeDtypeStruct((8, padded), jnp.float32),
        in_specs=[pl.BlockSpec(memory_space=VMEM)],
        out_specs=pl.BlockSpec(memory_space=VMEM),
        scratch_shapes=[
            VMEM((shards - 1, 8, padded), jnp.float32),
            pltpu.SemaphoreType.DMA((shards - 1,)),
            pltpu.SemaphoreType.DMA((shards - 1,)),
        ],
        compiler_params=pltpu.CompilerParams(collective_id=ident, has_side_effects=True),
        name="gain_sum",
    )(pieces)
    return total[:two, :own]


def dot(spec, left, right):
    return jnp.einsum(spec, left, right, preferred_element_type=jnp.float32)


def on_device(
    tokens,
    out_cotangent,
    seq_lengths,
    span_order,
    attention_input_weight,
    attention_input_first,
    attention_input_squared,
    attend_out,
    attend_out_moment,
    attend_out_second,
    gate_up,
    gate_up_moment,
    gate_up_second,
    down_weight,
    down_weight_moment,
    down_weight_second,
    norm_gains,
    norm_gains_moment,
    norm_gains_second,
):
    low = jnp.bfloat16
    micro_count, slot_count, row_count, model_width = tokens.shape
    seqs = micro_count * slot_count
    ctx_size = lax.axis_size("ctx")
    tp_size = lax.axis_size("tp")
    sequence_length = row_count * ctx_size
    span_len = sequence_length // (2 * ctx_size)
    hidden = down_weight.shape[0]
    out_width = attend_out.shape[0]
    in_width = attention_input_weight.shape[1]
    shards = ("fsdp", "ctx")

    first_pack = jnp.concatenate([attend_out.T, attention_input_weight], 1).astype(low)
    second_pack = jnp.concatenate([gate_up, down_weight.T], 1).astype(low)
    first_whole = lax.all_gather(first_pack, shards, axis=0, tiled=True)
    gains = lax.all_gather(norm_gains.astype(low), shards, axis=1, tiled=True).astype(jnp.float32)
    second_whole = lax.all_gather(second_pack, shards, axis=0, tiled=True)
    out_proj = first_whole[:, :out_width]
    in_proj = first_whole[:, out_width:]
    pair_proj = second_whole[:, : 2 * hidden]
    down_proj = second_whole[:, 2 * hidden :]

    orders = span_order.reshape(seqs, 2 * ctx_size)
    lengths = seq_lengths.reshape(seqs)
    within = jnp.arange(sequence_length, dtype=jnp.int32)
    block_ids = jnp.arange(2 * ctx_size, dtype=jnp.int32)
    table = jnp.where(
        block_ids[None, None, :] == (within // span_len)[None, :, None], orders[:, None, :], 0
    )
    pos_all = jnp.sum(table, -1) * span_len + within % span_len
    pos_here = lax.dynamic_slice_in_dim(pos_all, lax.axis_index("ctx") * row_count, row_count, 1)
    half_width = HEAD_DIMENSION // 2
    inverse = rope_base ** (-(jnp.arange(half_width, dtype=jnp.float32) * 2.0 / HEAD_DIMENSION))
    angles = pos_here.astype(jnp.float32)[:, None, :] * inverse[None, :, None]
    cosine, sine = jnp.cos(angles), jnp.sin(angles)
    key_pos = pos_all[:, :, None]
    query_pos = pos_here[:, None, :]
    length_row = jnp.broadcast_to(lengths[:, None, None], query_pos.shape)
    where = (cosine, sine, key_pos, query_pos, length_row)

    layer_inputs = tokens.reshape(seqs, row_count, model_width).astype(jnp.float32)
    first_root = lax.rsqrt(jnp.mean(layer_inputs * layer_inputs, -1, keepdims=True) + norm_eps)
    first_standard = layer_inputs * first_root
    first_normal = (first_standard * gains[0]).astype(low)
    projected = dot("dc,mrd->mcr", in_proj, first_normal)
    queries, key_values, attended_full, attended, log_total = attend(
        projected, *where, ctx_size, 1
    )

    def over_tp(part, ident):
        flat = part.astype(low).reshape(seqs * row_count, model_width)
        return line_sum(flat, tp_size, ident).reshape(part.shape).astype(jnp.float32)

    residual = layer_inputs + over_tp(dot("mcr,dc->mrd", attended, out_proj), 2)

    second_root = lax.rsqrt(jnp.mean(residual * residual, -1, keepdims=True) + norm_eps)
    second_standard = residual * second_root
    second_normal = (second_standard * gains[1]).astype(low)
    gate = dot("mrd,dc->mrc", second_normal, pair_proj[:, :hidden])
    up = dot("mrd,dc->mrc", second_normal, pair_proj[:, hidden:])
    sigmoid = jax.nn.sigmoid(gate)
    silu = gate * sigmoid
    inner = (silu * up).astype(low)
    keep = (pos_here < lengths[:, None]).astype(jnp.float32)[..., None]
    grad_out = out_cotangent.reshape(seqs, row_count, model_width).astype(jnp.float32) * keep
    grad_out_low = grad_out.astype(low)
    grad_inner = dot("mrd,dc->mrc", grad_out_low, down_proj)
    grad_gate = (grad_inner * up * sigmoid * (1.0 + gate * (1.0 - sigmoid))).astype(low)
    grad_up = (grad_inner * silu).astype(low)
    grad_pair = jnp.concatenate([grad_gate, grad_up], -1)
    all_rows = seqs * row_count
    pair_flat = grad_pair.reshape(all_rows, 2 * hidden)
    second_grads = grads_into(
        None, 3 * hidden, 0, second_normal.reshape(all_rows, model_width), pair_flat, False, 256
    )
    second_grads = grads_into(
        second_grads,
        3 * hidden,
        2 * hidden,
        grad_out_low.reshape(all_rows, model_width),
        inner.reshape(all_rows, hidden),
        False,
        256,
    )
    grad_pair, second_grads = lax.optimization_barrier((grad_pair, second_grads))
    second_share = lax.psum_scatter(second_grads, shards, scatter_dimension=0, tiled=True)
    grad_normal_two = over_tp(dot("mrc,dc->mrd", grad_pair, pair_proj), 3)
    second_gain = jnp.sum(grad_normal_two * second_standard, (0, 1))
    scaled = grad_normal_two * gains[1]
    grad_residual = grad_out + second_root * (
        scaled - second_standard * jnp.mean(scaled * second_standard, -1, keepdims=True)
    )
    grad_residual_low = grad_residual.astype(low)

    grad_attended = dot("dc,mrd->mcr", out_proj, grad_residual_low).astype(low)
    grad_projected = attend_back(
        queries, key_values, attended_full, log_total, grad_attended, *where, ctx_size, 4
    )
    first_grads = jnp.concatenate(
        [
            dot("mrd,mcr->dc", grad_residual_low, attended).astype(low),
            dot("mrd,mcr->dc", first_normal, grad_projected).astype(low),
        ],
        1,
    )
    grad_projected, first_grads, second_share = lax.optimization_barrier(
        (grad_projected, first_grads, second_share)
    )
    first_share = lax.psum_scatter(first_grads, shards, scatter_dimension=0, tiled=True)
    grad_normal_one = over_tp(dot("mcr,dc->mrd", grad_projected, in_proj), 5)
    first_gain = jnp.sum(grad_normal_one * first_standard, (0, 1))
    gain_share = gain_sum(
        jnp.stack([first_gain, second_gain]),
        lax.axis_size("fsdp") * ctx_size,
        ctx_size,
        7,
    )
    scaled = grad_normal_one * gains[0]
    input_grad = grad_residual + first_root * (
        scaled - first_standard * jnp.mean(scaled * first_standard, -1, keepdims=True)
    )
    mixed = (residual + over_tp(dot("mrc,dc->mrd", inner, down_proj), 6)).astype(low)

    gradients = (
        first_share[:, out_width:],
        first_share[:, :out_width].T,
        second_share[:, : 2 * hidden],
        second_share[:, 2 * hidden :].T,
        gain_share,
    )
    masters = (attention_input_weight, attend_out, gate_up, down_weight, norm_gains)
    firsts = (
        attention_input_first,
        attend_out_moment,
        gate_up_moment,
        down_weight_moment,
        norm_gains_moment,
    )
    seconds = (
        attention_input_squared,
        attend_out_second,
        gate_up_second,
        down_weight_second,
        norm_gains_second,
    )
    results = [mixed.reshape(tokens.shape), input_grad.reshape(tokens.shape)]
    for at in range(5):
        updated = adam_update(
            masters[at],
            firsts[at],
            seconds[at],
            gradients[at].astype(jnp.float32),
            learn_rates[at],
            decay_flags[at],
        )
        results.extend(updated)
        if at < 4:
            results.append(updated[2].astype(low))
    return tuple(results)


def solution(mesh):
    rows = P(None, "fsdp", "ctx", None)
    upper = P(("fsdp", "ctx"), "tp")
    lower = P("tp", ("fsdp", "ctx"))
    gain = P(None, ("fsdp", "ctx"))
    return jax.shard_map(
        on_device,
        mesh=mesh,
        in_specs=(rows, rows, P(None, "fsdp"), P(None, "fsdp", None))
        + (upper,) * 3
        + (lower,) * 3
        + (upper,) * 3
        + (lower,) * 3
        + (gain,) * 3,
        out_specs=(rows, rows)
        + (upper,) * 4
        + (lower,) * 4
        + (upper,) * 4
        + (lower,) * 4
        + (gain,) * 3,
        check_vma=False,
    )
```

time: 1500 us -> 896 us (0.60)
  waiting for transfers between devices: 929 us -> 32.7 us
  Pallas kernels: 0 us -> 540 us
  matrix products: 344 us -> 117 us
  blocking collectives: 50.2 us -> 10.3 us
  local copies, waits for them, and re-layouts: 33.5 us -> 63.3 us
    pallas_call x0 -> x9, Pallas kernels: none -> 540 us  [the longest x4 407 us: line_sum(): pl.pallas_call(functools.partial(line_body, n, chunks, chunk_rows, lag),...]
    psum x3 -> x0, waiting for transfers between devices: 492 us -> none  [the longest x1 228 us: on_device(): lax.psum(expand_part.astype(jnp.bfloat16), 'tp').astype(jnp.float32)]
    reduce_scatter x10 -> x1, waiting for transfers between devices: 274 us -> 0.01 us  [on_device(): lax.psum_scatter(second_grads, shards, scatter_dimension=0, tiled=True)]
    dot_general x54 -> x11, matrix products: 344 us -> 117 us  [dot(): return jnp.einsum(spec, left, right, preferred_element_type=jnp.float32)]
    all_gather x4 -> x2, waiting for transfers between devices: 141 us -> 32.6 us  [the longest x1 32.6 us: on_device(): first_whole = lax.all_gather(first_pack, shards, axis=0, tiled=True)]
    unnamed x340 -> x92, local copies, waits for them, and re-layouts: 16.4 us -> 57.5 us
    all_gather x7 -> x1, blocking collectives: 50.2 us -> 10.3 us  [on_device(): lax.all_gather(norm_gains.astype(low), shards, axis=1, tiled=True)]
    reduce_sum x9 -> x3, other arithmetic: 30.3 us -> 6.76 us  [the longest x1 3.04 us: on_device(): second_gain = jnp.sum(grad_normal_two * second_standard, (0, 1))]
  transfers between devices with their start and end apart: 18 -> 4, of which waited for: 14 -> 1; matrix products, arithmetic and copies ran while one was open for 24% -> 21% of each run, Pallas kernels for 0% -> 57%
where the time goes in v1:
time: 896 us; the launch traced here: 888 us
  Pallas kernels  540 us (60%)
  matrix products  117 us (13%)
  other arithmetic  110 us (12%)
  local copies, waits for them, and re-layouts  63.3 us (7%)
  waiting for transfers between devices  32.7 us (4%)
  between operations  14.6 us (2%)
  blocking collectives  10.3 us (1%)
    pallas_call x4, Pallas kernels, line_sum(): pl.pallas_call(functools.partial(line_body, n, chunks, chunk_rows, lag),...  407 us
    dot_general x11, matrix products, dot(): return jnp.einsum(spec, left, right, preferred_element_type=jnp.float32)  117 us
    unnamed x92, local copies, waits for them, and re-layouts  57.5 us
    pallas_call x1, Pallas kernels, attend(): pl.pallas_call(functools.partial(attend_body, n, groups), out_shape=(shap...  50.7 us
    pallas_call x1, Pallas kernels, attend_back(): pl.pallas_call(functools.partial(attend_back_body, n, groups), out_shape=...  40.5 us
    pallas_call x2, Pallas kernels, grads_into(): pl.pallas_call(functools.partial(grads_body, rows_last), grid=(n // tile,...  33.7 us
    all_gather x1, waiting for transfers between devices, on_device(): first_whole = lax.all_gather(first_pack, shards, axis=0, tiled=True)  32.6 us
    convert_element_type x4, other arithmetic, on_device(): results.append(updated[2].astype(low))  27.2 us
  transfers between devices with their start and end apart: 4, of which 1 were waited for; matrix products, arithmetic and copies ran while one was open for 21% of the time, Pallas kernels for 57%

profile of v1, /device:TPU:0, one launch (start us, length us, event | category | flops | bytes accessed | tf_op | source)
XLA Modules:
  0.0 888.1 jit_solution(12902154569280599552)
XLA Ops:
  7.2 1.4 convert.27
  11.0 2.5 convert.28
  13.7 2.1 pad_maximum_fusion.2
  16.8 10.3 %all-gather = bf16[8,320,2]{1,2,0:T(2,128)(2,1)S(1)} all-gather(bf16[1,320,2]{1,2,0:T(2,128)(2,1)S(1)} %convert_bitcast_fusion.4), channel_id=1, replica_groups=mesh['fsdp'=2,'ctx'=4,'tp'=4] {'fsdp','ctx'}, dimensions={0}, use_global_device_ids=true | all-gather | bytes 11520 | tf_op jit(solution)/shard_map/all_gather | solution.py:623
  27.8 3.1 fusion.11
  31.0 1.2 multiply_sine_fusion
  32.2 1.3 broadcast_add_fusion.key_pos_ref
  33.5 2.6 fusion.19.left_ref
  36.1 32.6 %all-gather.4.cloned.1.call-done = bf16[2560,1600]{1,0:T(8,128)(2,1)} async-done(((bf16[320,1600]{1,0:T(8,128)(2,1)}), bf16[2560,1600]{1,0:T(8,128)(2,1)}) %all-gather.4.cloned.1.call-update) | async-done | bytes 8192016 | tf_op jit(solution)/shard_map/all_gather | solution.py:622
  68.8 9.7 %fusion.38.proj_ref = f32[3,960,256]{2,1,0:T(8,128)} fusion(bf16[2560,1600]{1,0:T(8,128)(2,1)} %all-gather.4.cloned.1.call-done, bf16[3,1,256,2560]{3,2,1,0:T(8,128)(2,1)} %param.19, f32[2560]{0:T(1024)S(1)} %get-tuple-element.150, f32[3,256]{1,0:T(4,128)S(1)} %add_rsqrt_fusion.1), kind=kOutput, calls=%fused_computation.75 | convolution fusion | flops 3782737920 | bytes 12137472 | tf_op jit(solution)/shard_map/dc,mrd->mcr/dot_general | solution.py:584
  79.1 50.7 %attend.1 = (bf16[3,640,256]{2,1,0:T(8,128)(2,1)}, bf16[3,4,2,160,256]{4,3,2,1,0:T(8,128)(2,1)}, f32[3,640,256]{2,1,0:T(8,128)}, bf16[3,640,256]{2,1,0:T(8,128)(2,1)}, f32[3,8,256]{2,1,0:T(8,128)}) custom-call(f32[3,960,256]{2,1,0:T(8,128)} %fusion.38.proj_ref, f32[3,40,256]{2,1,0:T(8,128)} %get-tuple-element.179.cos_ref, ...), custom_call_target="tpu_custom_call" | custom-call | tf_op jit(solution)/shard_map/attend/pallas_call | solution.py:310
  129.8 7.4 convolution_convert_fusion.1
  137.2 100.7 %line_sum.4 = bf16[768,2560]{1,0:T(8,128)(2,1)S(1)} custom-call(bf16[768,2560]{1,0:T(8,128)(2,1)} %bitcast.195), custom_call_target="tpu_custom_call" | custom-call | flops 1966080 | bytes 157286400 | tf_op jit(solution)/shard_map/line_sum/pallas_call | solution.py:157
  240.0 2.6 copy-done.5
  243.8 7.3 multiply_convert_fusion.left_ref
  251.2 3.9 multiply_convert_fusion.1
  255.2 13.4 %fusion.21 = f32[3,256,1792]{2,1,0:T(8,128)} fusion(bf16[2560,5376]{1,0:T(8,128)(2,1)} %all-gather.6.cloned.1.call-done, bf16[3,1,256,2560]{3,2,1,0:T(8,128)(2,1)} %param.20, f32[3,256]{1,0:T(4,128)S(1)} %get-tuple-element.171), kind=kOutput, calls=%fused_computation.42 | convolution fusion | flops 7052328960 | bytes 18615296 | tf_op jit(solution)/shard_map/mrd,dc->mrc/dot_general | solution.py:584
  268.6 12.4 %fusion.1 = f32[3,256,1792]{2,1,0:T(8,128)} fusion(bf16[3,256,2560]{2,1,0:T(8,128)(2,1)S(1)} %copy-done.21, bf16[2560,5376]{1,0:T(8,128)(2,1)} %all-gather.6.cloned.1.call-done), kind=kOutput, calls=%fused_computation.5 | convolution fusion | flops 7046430720 | bytes 18612224 | tf_op jit(solution)/shard_map/mrd,dc->mrc/dot_general | solution.py:584
  281.0 15.9 %multiply_convert_fusion.3 = (bf16[3,256,1792]{2,1,0:T(8,128)(2,1)S(1)}, bf16[3,256,1792]{2,1,0:T(8,128)(2,1)}, bf16[3,256,1792]{2,1,0:T(8,128)(2,1)S(1)}) fusion(f32[3,256,1792]{2,1,0:T(8,128)} %fusion.21, f32[3,256,1792]{2,1,0:T(8,128)} %fusion.1, bf16[3,256,2560]{2,1,0:T(8,128)(2,1)S(1)} %copy-done.21, bf16[2560,5376]{1,0:T(8,128)(2,1)} %all-gather.6.cloned.1.call-done), kind=kOutput, calls=%fused_computation.49 | convolution fusion | flops 7067074560 | bytes 32374784 | tf_op jit(solution)/shard_map/mrd,dc->mrc/dot_general | solution.py:584
  296.8 4.7 pad_maximum_fusion.1
  301.5 20.7 %weight_grads.2.rest_0_ = bf16[2560,5376]{1,0:T(8,128)(2,1)} custom-call(bf16[768,2560]{1,0:T(8,128)(2,1)S(1)} %copy-done.4, bf16[768,3584]{1,0:T(8,128)(2,1)} %bitcast.191), custom_call_target="tpu_custom_call" | custom-call | flops 14092861440 | bytes 27787264 | tf_op jit(solution)/shard_map/weight_grads/pallas_call | solution.py:508
  322.2 13.0 %weight_grads.3 = bf16[2560,5376]{1,0:T(8,128)(2,1)} custom-call(bf16[768,2560]{1,0:T(8,128)(2,1)} %fusion.19.left_ref, bf16[768,1792]{1,0:T(8,128)(2,1)S(1)} %bitcast.181, bf16[2560,5376]{1,0:T(8,128)(2,1)} %weight_grads.2.rest_0_), custom_call_target="tpu_custom_call", output_to_operand_aliasing={{}: (2, {})} | custom-call | flops 7046430720 | bytes 15859712 | tf_op jit(solution)/shard_map/weight_grads/pallas_call | solution.py:508
  335.3 21.0 %fusion.24 = bf16[3,256,2560]{2,1,0:T(8,128)(2,1)} fusion(bf16[3,256,3584]{2,1,0:T(8,128)(2,1)} %pad_maximum_fusion.1, bf16[2560,5376]{1,0:T(8,128)(2,1)} %all-gather.6.cloned.1.call-done), kind=kOutput, calls=%fused_computation.54 | convolution fusion | flops 14094827520 | bytes 27787264 | tf_op jit(solution)/shard_map/mrc,dc->mrd/dot_general | solution.py:584
  356.4 102.4 %line_sum.6 = bf16[768,2560]{1,0:T(8,128)(2,1)S(1)} custom-call(bf16[768,2560]{1,0:T(8,128)(2,1)} %bitcast.194), custom_call_target="tpu_custom_call" | custom-call | flops 1966080 | bytes 157286400 | tf_op jit(solution)/shard_map/line_sum/pallas_call | solution.py:157
  458.8 5.1 convert_element_type.275
  463.9 1.2 copy-done.7
  465.1 3.0 multiply_reduce_fusion
  468.2 10.0 %add_convert_fusion = bf16[3,256,2560]{2,1,0:T(8,128)(2,1)S(1)} fusion(f32[3,256,2560]{2,1,0:T(8,128)} %bitcast.189, bf16[3,1,256,2560]{3,2,1,0:T(8,128)(2,1)} %param.20, f32[3,256]{1,0:T(4,128)S(1)} %div.116, f32[3,256]{1,0:T(4,128)S(1)} %get-tuple-element.171, f32[2560]{0:T(1024)S(1)} %get-tuple-element.151, f32[3,256]{1,0:T(4,128)S(1)} %add_rsqrt_fusion, ...), kind=kLoop, calls=%fused_computation.36 | loop fusion | flops 21626880 | bytes 27544576 | tf_op jit(solution)/shard_map/convert_element_type | solution.py:700
  478.1 6.0 fusion.44.grad_ref
  484.1 40.5 %attend_back.1 = bf16[3,960,256]{2,1,0:T(8,128)(2,1)} custom-call(bf16[3,640,256]{2,1,0:T(8,128)(2,1)} %get-tuple-element.33.q_ref, bf16[3,4,2,160,256]{4,3,2,1,0:T(8,128)(2,1)} %get-tuple-element.34.kv_ref, f32[3,640,256]{2,1,0:T(8,128)} %get-tuple-element.35.full_ref, f32[3,8,256]{2,1,0:T(8,128)} %get-tuple-element.36.log_ref, ...), custom_call_target="tpu_custom_call" | custom-call | tf_op jit(solution)/shard_map/attend_back/pallas_call | solution.py:453
  524.7 5.4 bitcast_convert_fusion.1
  530.2 6.0 bitcast_convert_fusion
  536.2 7.1 pad_maximum_fusion
  543.3 12.1 %copy.177 = bf16[2560,1600]{1,0:T(8,128)(2,1)} copy(bf16[2560,1600]{0,1:T(8,128)(2,1)} %pad_maximum_fusion) | data formatting | bytes 16384000
  555.5 3.0 copy.161
  558.4 2.5 copy.165
  560.9 2.9 copy.158
  563.8 3.0 copy.159
  566.8 2.5 copy.162
  569.3 2.5 copy.163
  572.0 11.4 %fusion.25 = bf16[3,256,2560]{2,1,0:T(8,128)(2,1)} fusion(bf16[3,256,1792]{2,1,0:T(8,128)(2,1)S(1)} %get-tuple-element.175, bf16[2560,5376]{1,0:T(8,128)(2,1)} %all-gather.6.cloned.1.call-done), kind=kOutput, calls=%fused_computation.56 | convolution fusion | flops 7048396800 | bytes 15859712 | tf_op jit(solution)/shard_map/mrc,dc->mrd/dot_general | solution.py:584
  583.4 102.5 %line_sum.5 = bf16[768,2560]{1,0:T(8,128)(2,1)S(1)} custom-call(bf16[768,2560]{1,0:T(8,128)(2,1)} %bitcast.192), custom_call_target="tpu_custom_call" | custom-call | flops 1966080 | bytes 157286400 | tf_op jit(solution)/shard_map/line_sum/pallas_call | solution.py:157
  685.9 7.3 fusion.30
  693.3 8.4 convolution_convert_fusion
  701.7 101.4 %line_sum.7 = bf16[768,2560]{1,0:T(8,128)(2,1)S(1)} custom-call(bf16[768,2560]{1,0:T(8,128)(2,1)} %bitcast.193), custom_call_target="tpu_custom_call" | custom-call | flops 1966080 | bytes 157286400 | tf_op jit(solution)/shard_map/line_sum/pallas_call | solution.py:157
  803.1 1.9 copy-done.2
  805.0 2.6 fusion.10
  808.4 7.9 gain_sum.1
  816.4 1.3 multiply_subtract_fusion.4
  817.7 7.2 fusion.57
  825.0 11.9 %fusion.60 = (bf16[320,3584]{1,0:T(8,128)(2,1)}, f32[320,3584]{1,0:T(8,128)}, f32[320,3584]{1,0:T(8,128)}, f32[320,3584]{1,0:T(8,128)}) fusion(f32[320,3584]{1,0:T(8,128)} %param.29, bf16[320,5376]{1,0:T(8,128)(2,1)S(1)} %copy-done.22, f32[320,3584]{1,0:T(8,128)} %param.31, f32[320,3584]{1,0:T(8,128)} %param.30), kind=kLoop, calls=%fused_computation.125 | loop fusion | flops 19496960 | bytes 32112640 | tf_op jit(solution)/shard_map/convert_element_type | solution.py:765
  837.6 1.2 slice-done.1
  838.8 11.3 %bitcast_add_fusion = f32[3,1,256,2560]{3,2,1,0:T(8,128)} fusion(bf16[3,1,256,2560]{3,2,1,0:T(8,128)(2,1)S(1)} %copy-done.10, f32[3,1,256,2560]{3,2,0,1:T(8,128)} %bitcast.190, f32[3,1,256,2560]{3,2,0,1:T(8,128)S(1)} %bitcast.188, bf16[3,1,256,2560]{3,2,1,0:T(8,128)(2,1)} %param.20, f32[3,256]{1,0:T(4,128)S(1)} %div.118, f32[2560]{0:T(1024)S(1)} %copy-done.26, ...), kind=kLoop, calls=%fused_computation.11 | loop fusion | flops 33423360 | bytes 35425280 | tf_op jit(solution)/shard_map/add | solution.py:726
  850.2 2.0 slice.64
  852.1 2.2 copy.181
  854.4 4.7 fusion.66
  859.0 3.0 copy.167
  862.0 3.0 copy.168
  865.1 1.5 copy.169
  866.6 2.2 copy.170
  870.8 3.5 fusion.63
  874.3 2.4 copy.171
  876.7 2.4 copy.172
  879.1 1.2 copy.173
  (120 shorter events, 12.9 us)
Async XLA Ops:
  7.2 61.6 %all-gather.4.cloned.1.call-start = ((), (), s32[]{:S(2)}) async-start(), calls=%async_computation.2 | async-start | bytes 9584640 | tf_op jit(solution)/shard_map/all_gather | solution.py:622
  9.8 3.7 copy-start.14
  11.0 244.2 %all-gather.6.cloned.1.call-start = ((), (), s32[]{:S(2)}) async-start(), calls=%async_computation.3 | async-start | bytes 30965760 | tf_op jit(solution)/shard_map/all_gather | solution.py:624
  13.7 2.2 copy-start.34
  13.7 2.4 copy-start.33
  13.7 3.1 copy-start.29
  15.8 527.5 %reduce-scatter.5.cloned.1.call-start = ((), (), s32[]{:S(2)}) async-start(), calls=%async_computation.4 | async-start | bytes 30965760 | tf_op jit(solution)/shard_map/reduce_scatter | solution.py:693
  27.7 5.8 copy-start.13
  27.8 41.0 %copy-start.25 = (f32[2560]{0:T(1024)}, f32[2560]{0:T(1024)S(1)}, u32[]{:S(2)}) copy-start(f32[2560]{0:T(1024)S(1)} %get-tuple-element.150) | copy-start | bytes 30724
  30.9 37.8 %copy-start.27 = (f32[3,256]{1,0:T(4,128)}, f32[3,256]{1,0:T(4,128)S(1)}, u32[]{:S(2)}) copy-start(f32[3,256]{1,0:T(4,128)S(1)} %add_rsqrt_fusion.1) | copy-start | bytes 9220
  237.9 2.1 copy-start
  237.9 4.7 copy-start.5
  240.0 3.7 copy-start.11
  243.8 7.3 copy-start.6
  243.8 7.5 copy-start.12
  255.2 13.4 %copy-start.21 = (bf16[3,256,2560]{2,1,0:T(8,128)(2,1)S(1)}, bf16[3,256,2560]{2,1,0:T(8,128)(2,1)}, u32[]{:S(2)}) copy-start(bf16[3,256,2560]{2,1,0:T(8,128)(2,1)} %multiply_convert_fusion.1) | copy-start | bytes 11796484
  296.8 4.7 copy-start.4
  335.3 514.9 %reduce-scatter.7.cloned.1.call-start = ((), (), s32[]{:S(2)}) async-start(), calls=%async_computation.5 | async-start | bytes 9584640
  458.8 5.1 copy-start.1
  458.8 6.3 copy-start.7
  524.7 5.5 copy-start.8
  524.7 5.5 copy-start.23
  524.7 5.5 copy-start.26
  524.7 5.5 copy-start.28
  583.4 102.5 %copy-start.9 = (bf16[3,1,256,2560]{3,2,1,0:T(8,128)(2,1)S(1)}, bf16[3,1,256,2560]{3,2,1,0:T(8,128)(2,1)}, u32[]{:S(2)}) copy-start(bf16[3,1,256,2560]{3,2,1,0:T(8,128)(2,1)} %param.19) | copy-start | bytes 11796484
  685.9 7.4 copy-start.24
  803.1 1.9 copy-start.2
  805.0 11.4 %copy-start.30 = (f32[2,320]{1,0:T(2,128)S(1)}, f32[2,320]{1,0:T(2,128)}, u32[]{:S(2)}) copy-start(f32[2,320]{1,0:T(2,128)} %param.35) | copy-start | bytes 7684
  805.0 11.4 %copy-start.31 = (f32[2,320]{1,0:T(2,128)S(1)}, f32[2,320]{1,0:T(2,128)}, u32[]{:S(2)}) copy-start(f32[2,320]{1,0:T(2,128)} %param.37) | copy-start | bytes 7684
  805.0 11.4 %copy-start.32 = (f32[2,320]{1,0:T(2,128)S(1)}, f32[2,320]{1,0:T(2,128)}, u32[]{:S(2)}) copy-start(f32[2,320]{1,0:T(2,128)} %param.36) | copy-start | bytes 7684
  805.0 12.7 %copy-start.15 = (f32[1792,320]{0,1:T(8,128)S(1)}, f32[1792,320]{0,1:T(8,128)}, u32[]{:S(2)}) copy-start(f32[1792,320]{0,1:T(8,128)} %param.32) | copy-start | bytes 6881284
  817.7 7.2 copy-start.22
  817.7 19.1 %slice-start = ((s8[7864320]{0:T(1024)(128)(4,1)}), s8[4194304]{0:T(1024)(128)(4,1)S(1)}, s32[]{:S(2)}) async-start(s8[7864320]{0:T(1024)(128)(4,1)} %bitcast.186), calls=%async_computation.6 | async-start | bytes 8388608
  824.9 11.9 %copy-start.3 = (bf16[768,2560]{1,0:T(8,128)(2,1)S(1)}, bf16[768,2560]{1,0:T(8,128)(2,1)}, u32[]{:S(2)}) copy-start(bf16[768,2560]{1,0:T(8,128)(2,1)} %copy-done.2) | copy-start | bytes 11796484
  824.9 12.7 %copy-start.10 = (bf16[3,1,256,2560]{3,2,1,0:T(8,128)(2,1)S(1)}, bf16[3,1,256,2560]{3,2,1,0:T(8,128)(2,1)}, u32[]{:S(2)}) copy-start(bf16[3,1,256,2560]{3,2,1,0:T(8,128)(2,1)} %param.19) | copy-start | bytes 11796484
  824.9 13.9 %slice-start.1 = ((s8[7864320]{0:T(1024)(128)(4,1)}), s8[3670016]{0:T(1024)(128)(4,1)S(1)}, s32[]{:S(2)}) async-start(s8[7864320]{0:T(1024)(128)(4,1)} %bitcast.186), calls=%async_computation.7 | async-start | bytes 7340032
  838.8 15.6 %copy-start.16 = (f32[320,960]{0,1:T(8,128)S(1)}, f32[320,960]{0,1:T(8,128)}, u32[]{:S(2)}) copy-start(f32[320,960]{0,1:T(8,128)} %copy.161) | copy-start | bytes 3686404
  838.8 15.6 %copy-start.17 = (f32[320,960]{0,1:T(8,128)S(1)}, f32[320,960]{0,1:T(8,128)}, u32[]{:S(2)}) copy-start(f32[320,960]{0,1:T(8,128)} %copy.158) | copy-start | bytes 3686404
  859.0 6.0 copy-start.18
  862.0 8.8 copy-start.19
  862.0 8.8 copy-start.20
Sparse Core Ops, SparseCore 0:
  11.1 57.6 all-gather.3
  70.6 155.9 all-gather.5
  335.4 174.6 reduce-scatter.4
  555.6 73.7 reduce-scatter.6

commit v2 on v1

--- a/solution.py
+++ b/solution.py
@@ -25,6 +25,8 @@
 log2_e = 1.4426950408889634
 MESH = pl.DeviceIdType.MESH
 VMEM = pltpu.VMEM
+CHUNK = 16
+LAG = 2
 
 
 def adam_update(weight, moment, second, gradient, learn_rate, decay_flag):
@@ -38,11 +40,7 @@
     return (moment, second, weight)
 
 
-def line_body(
-    n, chunks, chunk_rows, lag, p_ref, o_ref, inbox, red_send, red_recv, back_send, back_recv
-):
-    z = lax.axis_index("tp")
-    half = chunks * chunk_rows
+def line_greet(n, z):
     barrier = pltpu.get_barrier_semaphore()
 
     @pl.when(z > 0)
@@ -53,122 +51,177 @@
     def _():
         pl.semaphore_signal(barrier, inc=1, device_id={"tp": z + 1}, device_id_type=MESH)
 
-    pl.semaphore_wait(barrier, (z > 0).astype(jnp.int32) + (z < n - 1).astype(jnp.int32))
-
-    def rows_of(flow, k):
-        return pl.ds(pl.multiple_of(flow * half + k * chunk_rows, chunk_rows), chunk_rows)
-
-    def hop_of(flow):
-        return (n - 1 - z) if flow == 0 else z
-
-    def onward(flow):
-        return {"tp": jnp.maximum(z - 1, 0) if flow == 0 else jnp.minimum(z + 1, n - 1)}
-
-    def backward(flow):
-        return {"tp": jnp.minimum(z + 1, n - 1) if flow == 0 else jnp.maximum(z - 1, 0)}
-
-    def reduce_copy(flow, k, source):
+    return (z > 0).astype(jnp.int32) + (z < n - 1).astype(jnp.int32)
+
+
+class Line:
+    def __init__(self, n, z, segments, segment_rows, parts, inbox, out, sems, finish):
+        self.n, self.z = n, z
+        self.segment_rows = segment_rows
+        self.per_segment = segment_rows // (2 * CHUNK)
+        self.chunks = segments * self.per_segment
+        self.parts, self.inbox, self.out = parts, inbox, out
+        self.red_send, self.red_recv, self.back_send, self.back_recv = sems
+        self.finish = finish
+        self.ticks = self.chunks + 2 * (n - 1) * LAG
+
+    def ready(self, segments):
+        return segments * self.per_segment + 2 * (self.n - 1) * LAG
+
+    def rows(self, flow, g):
+        start = (
+            (g // self.per_segment) * self.segment_rows
+            + flow * (self.segment_rows // 2)
+            + (g % self.per_segment) * CHUNK
+        )
+        return pl.ds(pl.multiple_of(start, CHUNK), CHUNK)
+
+    def hop(self, flow):
+        return (self.n - 1 - self.z) if flow == 0 else self.z
+
+    def neighbour(self, up):
+        z = jnp.minimum(self.z + 1, self.n - 1) if up else jnp.maximum(self.z - 1, 0)
+        return {"tp": z}
+
+    def reduce_copy(self, flow, g, source):
         return pltpu.make_async_remote_copy(
             src_ref=source,
-            dst_ref=inbox.at[rows_of(flow, k)],
-            send_sem=red_send.at[flow, k],
-            recv_sem=red_recv.at[flow, k],
-            device_id=onward(flow),
+            dst_ref=self.inbox.at[self.rows(flow, g)],
+            send_sem=self.red_send.at[flow, g],
+            recv_sem=self.red_recv.at[flow, g],
+            device_id=self.neighbour(flow == 1),
             device_id_type=MESH,
         )
 
-    def back_copy(flow, k):
-        rows = rows_of(flow, k)
+    def back_copy(self, flow, g):
+        rows = self.rows(flow, g)
         return pltpu.make_async_remote_copy(
-            src_ref=o_ref.at[rows],
-            dst_ref=o_ref.at[rows],
-            send_sem=back_send.at[flow, k],
-            recv_sem=back_recv.at[flow, k],
-            device_id=backward(flow),
+            src_ref=self.out.at[rows],
+            dst_ref=self.out.at[rows],
+            send_sem=self.back_send.at[flow, g],
+            recv_sem=self.back_recv.at[flow, g],
+            device_id=self.neighbour(flow == 0),
             device_id_type=MESH,
         )
 
-    def added(rows):
-        return (inbox[rows, :].astype(jnp.float32) + p_ref[rows, :].astype(jnp.float32)).astype(
-            jnp.bfloat16
-        )
-
-    def step(t, carry):
+    def tick(self, t):
+        n = self.n
         for flow in (0, 1):
-            hop = hop_of(flow)
-            k = t - hop * lag
-
-            @pl.when((k >= 0) & (k < chunks))
+            hop = self.hop(flow)
+            g = t - hop * LAG
+
+            @pl.when((g >= 0) & (g < self.chunks))
             def _():
-                rows = rows_of(flow, k)
+                rows = self.rows(flow, g)
 
                 @pl.when(hop == 0)
                 def _():
-                    reduce_copy(flow, k, p_ref.at[rows]).start()
-
-                @pl.when((hop > 0) & (hop < n - 1))
-                def _():
-                    reduce_copy(flow, k, p_ref.at[rows]).wait_recv()
-                    inbox[rows, :] = added(rows)
-                    reduce_copy(flow, k, inbox.at[rows]).start()
-
-                @pl.when(hop == n - 1)
-                def _():
-                    reduce_copy(flow, k, p_ref.at[rows]).wait_recv()
-                    o_ref[rows, :] = added(rows)
-                    back_copy(flow, k).start()
-
-        for flow in (0, 1):
-            hop = hop_of(flow)
-            k2 = t - (n - 1) * lag - (n - 1 - hop) * lag
-
-            @pl.when((k2 >= 0) & (k2 < chunks) & (hop < n - 1))
-            def _():
-                back_copy(flow, k2).wait_recv()
+                    self.reduce_copy(flow, g, self.parts.at[rows]).start()
 
                 @pl.when(hop > 0)
                 def _():
-                    back_copy(flow, k2).start()
-
-        return carry
-
-    lax.fori_loop(0, chunks + 2 * (n - 1) * lag, step, 0)
-
-    def drain(k, carry):
+                    self.reduce_copy(flow, g, self.parts.at[rows]).wait_recv()
+                    total = self.inbox[rows, :].astype(jnp.float32) + self.parts[rows, :].astype(
+                        jnp.float32
+                    )
+
+                    @pl.when(hop < n - 1)
+                    def _():
+                        self.inbox[rows, :] = total.astype(jnp.bfloat16)
+                        self.reduce_copy(flow, g, self.inbox.at[rows]).start()
+
+                    @pl.when(hop == n - 1)
+                    def _():
+                        self.finish(g // self.per_segment, rows, total)
+                        self.back_copy(flow, g).start()
+
         for flow in (0, 1):
-            hop = hop_of(flow)
-
-            @pl.when(hop < n - 1)
+            hop = self.hop(flow)
+            back = t - (n - 1) * LAG - (n - 1 - hop) * LAG
+
+            @pl.when((back >= 0) & (back < self.chunks) & (hop < n - 1))
             def _():
-                reduce_copy(flow, k, p_ref.at[rows_of(flow, k)]).wait_send()
-
-            @pl.when(hop > 0)
-            def _():
-                back_copy(flow, k).wait_send()
-
-        return carry
-
-    lax.fori_loop(0, chunks, drain, 0)
-
-
-def line_sum(part, n, ident, chunk_rows=16, lag=2):
+                self.back_copy(flow, back).wait_recv()
+
+                @pl.when(hop > 0)
+                def _():
+                    self.back_copy(flow, back).start()
+
+    def run(self, first, last):
+        def step(t, carry):
+            self.tick(t)
+            return carry
+
+        lax.fori_loop(first, last, step, 0)
+
+    def drain(self):
+        def step(g, carry):
+            for flow in (0, 1):
+                hop = self.hop(flow)
+
+                @pl.when(hop < self.n - 1)
+                def _():
+                    self.reduce_copy(flow, g, self.parts.at[self.rows(flow, g)]).wait_send()
+
+                @pl.when(hop > 0)
+                def _():
+                    self.back_copy(flow, g).wait_send()
+
+            return carry
+
+        lax.fori_loop(0, self.chunks, step, 0)
+
+
+def line_scratch(rows, width, segments, segment_rows):
+    chunks = segments * (segment_rows // (2 * CHUNK))
+    return [VMEM((rows, width), jnp.bfloat16)] + [pltpu.SemaphoreType.DMA((2, chunks))] * 4
+
+
+def line_body(n, segments, p_ref, o_ref, inbox, *sems):
+    z = lax.axis_index("tp")
+    pl.semaphore_wait(pltpu.get_barrier_semaphore(), line_greet(n, z))
+
+    def finish(segment, rows, total):
+        o_ref[rows, :] = total.astype(jnp.bfloat16)
+
+    line = Line(n, z, segments, p_ref.shape[0] // segments, p_ref, inbox, o_ref, sems, finish)
+    line.run(0, line.ticks)
+    line.drain()
+
+
+def line_cost(rows, width):
+    return pl.CostEstimate(flops=rows * width, bytes_accessed=80 * rows * width, transcendentals=0)
+
+
+def line_sum(part, n, segments, ident):
     rows, width = part.shape
-    chunks = rows // 2 // chunk_rows
     return pl.pallas_call(
-        functools.partial(line_body, n, chunks, chunk_rows, lag),
+        functools.partial(line_body, n, segments),
         out_shape=jax.ShapeDtypeStruct((rows, width), jnp.bfloat16),
         in_specs=[pl.BlockSpec(memory_space=VMEM)],
         out_specs=pl.BlockSpec(memory_space=VMEM),
-        scratch_shapes=[VMEM((rows, width), jnp.bfloat16)]
-        + [pltpu.SemaphoreType.DMA((2, chunks))] * 4,
+        scratch_shapes=line_scratch(rows, width, segments, rows // segments),
         compiler_params=pltpu.CompilerParams(
             collective_id=ident, has_side_effects=True, vmem_limit_bytes=48 * 2**20
         ),
-        cost_estimate=pl.CostEstimate(
-            flops=rows * width, bytes_accessed=80 * rows * width, transcendentals=0
-        ),
+        cost_estimate=line_cost(rows, width),
         name="line_sum",
     )(part)
+
+
+def mean_of(values):
+    return jnp.mean(values, axis=-1, keepdims=True)
+
+
+def norm_back(total, values, gain, gain_sums):
+    root = lax.rsqrt(mean_of(values * values) + norm_eps)
+    standard = values * root
+    terms = total * standard
+    gain_sums[...] += functools.reduce(
+        lambda a, b: a + b, [terms[low : low + 8] for low in range(0, CHUNK, 8)]
+    )
+    scaled = total * gain
+    return root * (scaled - standard * mean_of(scaled * standard))
 
 
 def greet(n):
@@ -287,7 +340,9 @@
                     )
                 out = out / total
                 full_ref[m, low : low + dim, :] = out
-                low_ref[m, low : low + dim, :] = out.astype(jnp.bfloat16)
+                low_ref[low : low + dim, pl.ds(pl.multiple_of(m * rows, 128), rows)] = out.astype(
+                    jnp.bfloat16
+                )
                 log_ref[m, g * GROUP + h : g * GROUP + h + 1, :] = top + jnp.log2(total)
         return carry
 
@@ -313,7 +368,7 @@
             shape((seqs, heads * HEAD_DIMENSION, rows), jnp.bfloat16),
             shape((seqs, n, groups, 2 * HEAD_DIMENSION, rows), jnp.bfloat16),
             shape((seqs, heads * HEAD_DIMENSION, rows), jnp.float32),
-            shape((seqs, heads * HEAD_DIMENSION, rows), jnp.bfloat16),
+            shape((heads * HEAD_DIMENSION, seqs * rows), jnp.bfloat16),
             shape((seqs, heads, rows), jnp.float32),
         ),
         in_specs=[vmem] * 6,
@@ -330,145 +385,331 @@
     )(projected, cosine, sine, key_pos, query_pos, lengths)
 
 
-def attend_back_body(
+def back_one_body(
     n,
+    tp,
     groups,
+    normal_ref,
+    mixed_ref,
+    residual_ref,
+    grad_out_ref,
+    gain_ref,
+    weight_ref,
     q_ref,
     kv_ref,
     full_ref,
     log_ref,
-    grad_ref,
     cos_ref,
     sin_ref,
     key_pos_ref,
     query_pos_ref,
     length_ref,
     out_ref,
+    proj_ref,
+    gain_sums,
+    parts,
+    out_proj,
+    grads,
+    sums,
     bias,
     outbox,
-    inbox,
+    kv_inbox,
+    load_sem,
     send_sem,
     recv_sem,
+    inbox,
+    *sems,
 ):
-    me = greet(n)
+    z = lax.axis_index("tp")
+    me = lax.axis_index("ctx")
     seqs, _, rows = q_ref.shape
+    all_rows = seqs * rows
+    loads = [
+        pltpu.make_async_copy(normal_ref, parts.at[pl.ds(0, all_rows)], load_sem.at[0]),
+        pltpu.make_async_copy(mixed_ref, parts.at[pl.ds(all_rows, all_rows)], load_sem.at[1]),
+        pltpu.make_async_copy(
+            weight_ref.at[:, pl.ds(0, out_proj.shape[1])], out_proj, load_sem.at[2]
+        ),
+    ]
+    for load in loads:
+        load.start()
+    peers = line_greet(tp, z)
+    barrier = pltpu.get_barrier_semaphore()
+    for step in range(1, n):
+        pl.semaphore_signal(
+            barrier, inc=1, device_id={"ctx": lax.rem(me + step, n)}, device_id_type=MESH
+        )
+    pl.semaphore_wait(barrier, peers + n - 1)
+
     dim = HEAD_DIMENSION
     half = dim // 2
     scale = dim**-0.5
     group_width = (GROUP + 2) * dim
+    heads = groups * GROUP
+    gain_sums[...] = jnp.zeros_like(gain_sums)
+
+    def finish(segment, at, total):
+        @pl.when(segment < seqs)
+        def _():
+            grad = norm_back(total, residual_ref[at, :], gain_ref[1:2, :], gain_sums)
+            out_ref[at, :] = (grad_out_ref[at, :].astype(jnp.float32) + grad).astype(jnp.bfloat16)
+
+        @pl.when(segment >= seqs)
+        def _():
+            start = pl.multiple_of(at.start - all_rows, CHUNK)
+            out_ref[at, :] = (residual_ref[pl.ds(start, CHUNK), :] + total).astype(jnp.bfloat16)
+
+    line = Line(tp, z, 2 * seqs, rows, parts, inbox, out_ref, sems, finish)
 
     def copy(m, step):
         to = lax.rem(me + step, n)
         return pltpu.make_async_remote_copy(
             src_ref=outbox.at[m, to],
-            dst_ref=inbox.at[m, step - 1],
+            dst_ref=kv_inbox.at[m, step - 1],
             send_sem=send_sem.at[m, step - 1],
             recv_sem=recv_sem.at[m, step - 1],
             device_id={"ctx": to},
             device_id_type=MESH,
         )
 
-    def sequence(m, carry):
+    def columns(m):
+        return pl.ds(pl.multiple_of(m * rows, 128), rows)
+
+    def attended_grads(m):
+        grads[...] = (
+            jnp.dot(
+                out_ref[pl.ds(pl.multiple_of(m * rows, CHUNK), rows), :],
+                out_proj[...],
+                preferred_element_type=jnp.float32,
+            )
+            .T.astype(jnp.bfloat16)
+        )
         bias[...] = mask_bias(key_pos_ref[m], query_pos_ref[m], length_ref[m])
-        for g in range(groups):
-            key_sums = [jnp.zeros((dim, rows), jnp.float32) for _ in range(n)]
-            value_sums = [jnp.zeros((dim, rows), jnp.float32) for _ in range(n)]
-            for h in range(GROUP):
-                low = (g * GROUP + h) * dim
-                query = q_ref[m, low : low + dim, :]
-                grad = grad_ref[m, low : low + dim, :]
-                delta = jnp.sum(
-                    grad.astype(jnp.float32) * full_ref[m, low : low + dim, :],
-                    axis=0,
-                    keepdims=True,
-                )
-                log_total = log_ref[m, g * GROUP + h : g * GROUP + h + 1, :]
-                query_sum = jnp.zeros((dim, rows), jnp.float32)
-                for j in range(n):
-                    keys = kv_ref[m, j, g, :dim, :]
-                    values = kv_ref[m, j, g, dim:, :]
-                    scores = lax.dot_general(
-                        keys, query, (((0,), (0,)), ((), ())), preferred_element_type=jnp.float32
-                    )
-                    probs = jnp.exp2(
-                        scores * (log2_e * scale)
-                        + (bias[j * rows : (j + 1) * rows, :] - log_total)
-                    )
-                    grad_probs = lax.dot_general(
-                        values, grad, (((0,), (0,)), ((), ())), preferred_element_type=jnp.float32
-                    )
-                    grad_scores = (probs * (grad_probs - delta)).astype(jnp.bfloat16)
-                    query_sum += jnp.dot(keys, grad_scores, preferred_element_type=jnp.float32)
-                    key_sums[j] += lax.dot_general(
-                        query,
-                        grad_scores,
-                        (((1,), (1,)), ((), ())),
-                        preferred_element_type=jnp.float32,
-                    )
-                    value_sums[j] += lax.dot_general(
-                        grad,
-                        probs.astype(jnp.bfloat16),
-                        (((1,), (1,)), ((), ())),
-                        preferred_element_type=jnp.float32,
-                    )
-                query_sum = query_sum * scale
-                col = g * group_width + h * dim
-                out_ref[m, col : col + dim, :] = turn_back(
-                    query_sum[:half], query_sum[half:], cos_ref[m], sin_ref[m]
-                ).astype(jnp.bfloat16)
+
+    def head(m, at):
+        g = at // GROUP
+        h = at % GROUP
+        low = pl.ds(pl.multiple_of(at * dim, 16), dim)
+        query = q_ref[m, low, :]
+        grad = grads[low, :]
+        delta = jnp.sum(
+            grad.astype(jnp.float32) * full_ref[m, low, :], axis=0, keepdims=True
+        )
+        log_total = log_ref[m, at]
+        query_sum = jnp.zeros((dim, rows), jnp.float32)
+
+        @pl.when(h == 0)
+        def _():
+            sums[...] = jnp.zeros_like(sums)
+
+        for j in range(n):
+            keys = kv_ref[m, j, g, :dim, :]
+            values = kv_ref[m, j, g, dim:, :]
+            scores = lax.dot_general(
+                keys, query, (((0,), (0,)), ((), ())), preferred_element_type=jnp.float32
+            )
+            probs = jnp.exp2(
+                scores * (log2_e * scale) + (bias[j * rows : (j + 1) * rows, :] - log_total)
+            )
+            grad_probs = lax.dot_general(
+                values, grad, (((0,), (0,)), ((), ())), preferred_element_type=jnp.float32
+            )
+            grad_scores = (probs * (grad_probs - delta)).astype(jnp.bfloat16)
+            query_sum += jnp.dot(keys, grad_scores, preferred_element_type=jnp.float32)
+            sums[j, :dim, :] += lax.dot_general(
+                query, grad_scores, (((1,), (1,)), ((), ())), preferred_element_type=jnp.float32
+            )
+            sums[j, dim:, :] += lax.dot_general(
+                grad,
+                probs.astype(jnp.bfloat16),
+                (((1,), (1,)), ((), ())),
+                preferred_element_type=jnp.float32,
+            )
+        query_sum = query_sum * scale
+        col = pl.ds(pl.multiple_of(g * group_width + h * dim, 16), dim)
+        proj_ref[col, columns(m)] = turn_back(
+            query_sum[:half], query_sum[half:], cos_ref[m], sin_ref[m]
+        ).astype(jnp.bfloat16)
+
+        @pl.when(h == GROUP - 1)
+        def _():
             for j in range(n):
-                outbox[m, j, g, :dim, :] = (key_sums[j] * scale).astype(jnp.bfloat16)
-                outbox[m, j, g, dim:, :] = value_sums[j].astype(jnp.bfloat16)
-        for step in range(1, n):
-            copy(m, step).start()
-        return carry
-
-    lax.fori_loop(0, seqs, sequence, 0)
-
-    def gather(m, carry):
+                outbox[m, j, g, :dim, :] = (sums[j, :dim, :] * scale).astype(jnp.bfloat16)
+                outbox[m, j, g, dim:, :] = sums[j, dim:, :].astype(jnp.bfloat16)
+
+    def gather(m):
         for step in range(1, n):
             copy(m, step).wait_recv()
         for g in range(groups):
             total = outbox[m, me, g].astype(jnp.float32)
             for step in range(1, n):
-                total += inbox[m, step - 1, g].astype(jnp.float32)
+                total += kv_inbox[m, step - 1, g].astype(jnp.float32)
             col = g * group_width + GROUP * dim
-            out_ref[m, col : col + dim, :] = turn_back(
+            proj_ref[col : col + dim, columns(m)] = turn_back(
                 total[:half], total[half:dim], cos_ref[m], sin_ref[m]
             ).astype(jnp.bfloat16)
-            out_ref[m, col + dim : col + 2 * dim, :] = total[dim:].astype(jnp.bfloat16)
+            proj_ref[col + dim : col + 2 * dim, columns(m)] = total[dim:].astype(jnp.bfloat16)
         for step in range(1, n):
             copy(m, step).wait_send()
+
+    loads[0].wait()
+    line.run(0, line.ready(1))
+    loads[1].wait()
+    loads[2].wait()
+
+    def sequence(m, carry):
+        first = line.ready(1) + m * (heads + 1)
+        line.tick(first)
+        attended_grads(m)
+
+        def item(at, inner):
+            line.tick(first + 1 + at)
+            head(m, at)
+            return inner
+
+        lax.fori_loop(0, heads, item, 0)
+        for step in range(1, n):
+            copy(m, step).start()
         return carry
 
-    lax.fori_loop(0, seqs, gather, 0)
-
-
-def attend_back(
-    queries, key_values, full, log_total, grads, cosine, sine, key_pos, query_pos, lengths, n, ident
+    lax.fori_loop(0, seqs, sequence, 0)
+    line.run(line.ready(1) + seqs * (heads + 1), line.ticks)
+
+    def collect(m, carry):
+        gather(m)
+        return carry
+
+    lax.fori_loop(0, seqs, collect, 0)
+    line.drain()
+
+
+def back_one(
+    normal_part,
+    mixed_part,
+    residual,
+    grad_out,
+    gains,
+    first_whole,
+    queries,
+    key_values,
+    full,
+    log_total,
+    where,
+    n,
+    tp,
+    ident,
 ):
     seqs, width, rows = queries.shape
     groups = key_values.shape[2]
+    all_rows, model_width = normal_part.shape
     vmem = pl.BlockSpec(memory_space=VMEM)
+    hbm = pl.BlockSpec(memory_space=pl.ANY)
+    shape = jax.ShapeDtypeStruct
     return pl.pallas_call(
-        functools.partial(attend_back_body, n, groups),
-        out_shape=jax.ShapeDtypeStruct(
-            (seqs, groups * (GROUP + 2) * HEAD_DIMENSION, rows), jnp.bfloat16
+        functools.partial(back_one_body, n, tp, groups),
+        out_shape=(
+            shape((2 * all_rows, model_width), jnp.bfloat16),
+            shape((groups * (GROUP + 2) * HEAD_DIMENSION, all_rows), jnp.bfloat16),
+            shape((8, model_width), jnp.float32),
         ),
-        in_specs=[vmem] * 10,
-        out_specs=vmem,
+        in_specs=[hbm, hbm, vmem, vmem, vmem, hbm] + [vmem] * 9,
+        out_specs=(vmem,) * 3,
         scratch_shapes=[
+            VMEM((2 * all_rows, model_width), jnp.bfloat16),
+            VMEM((model_width, width), jnp.bfloat16),
+            VMEM((width, rows), jnp.bfloat16),
+            VMEM((n, 2 * HEAD_DIMENSION, rows), jnp.float32),
             VMEM((n * rows, rows), jnp.float32),
             VMEM((seqs, n, groups, 2 * HEAD_DIMENSION, rows), jnp.bfloat16),
             VMEM((seqs, n - 1, groups, 2 * HEAD_DIMENSION, rows), jnp.bfloat16),
+            pltpu.SemaphoreType.DMA((3,)),
             pltpu.SemaphoreType.DMA((seqs, n - 1)),
             pltpu.SemaphoreType.DMA((seqs, n - 1)),
-        ],
+        ]
+        + line_scratch(2 * all_rows, model_width, 2 * seqs, rows),
+        compiler_params=pltpu.CompilerParams(
+            collective_id=ident, has_side_effects=True, vmem_limit_bytes=60 * 2**20
+        ),
+        cost_estimate=line_cost(2 * all_rows, model_width),
+        name="back_one",
+    )(
+        normal_part,
+        mixed_part,
+        residual,
+        grad_out,
+        gains,
+        first_whole,
+        queries,
+        key_values,
+        full,
+        log_total,
+        *where,
+    )
+
+
+def back_two_body(
+    tp,
+    seqs,
+    proj_ref,
+    weight_ref,
+    token_ref,
+    residual_grad_ref,
+    gain_ref,
+    out_ref,
+    gain_sums,
+    parts,
+    inbox,
+    *sems,
+):
+    z = lax.axis_index("tp")
+    pl.semaphore_wait(pltpu.get_barrier_semaphore(), line_greet(tp, z))
+    gain_sums[...] = jnp.zeros_like(gain_sums)
+    rows = token_ref.shape[0] // seqs
+    skip = weight_ref.shape[1] - proj_ref.shape[0]
+    width = weight_ref.shape[0]
+    tile = 512 if width % 512 == 0 else width
+
+    def finish(segment, at, total):
+        values = token_ref[at, :].astype(jnp.float32)
+        grad = norm_back(total, values, gain_ref[0:1, :], gain_sums)
+        out_ref[at, :] = (residual_grad_ref[at, :].astype(jnp.float32) + grad).astype(jnp.bfloat16)
+
+    line = Line(tp, z, seqs, rows, parts, inbox, out_ref, sems, finish)
+
+    def product(m):
+        left = proj_ref[:, m * rows : (m + 1) * rows].T
+        for low in range(0, width, tile):
+            parts[m * rows : (m + 1) * rows, low : low + tile] = lax.dot_general(
+                left,
+                weight_ref[low : low + tile, skip:],
+                (((1,), (1,)), ((), ())),
+                preferred_element_type=jnp.float32,
+            ).astype(jnp.bfloat16)
+
+    for m in range(seqs):
+        product(m)
+        line.run(2 * m, 2 * m + 2)
+    line.run(2 * seqs, line.ticks)
+    line.drain()
+
+
+def back_two(projected, first_whole, tokens, residual_grad, gains, seqs, tp, ident):
+    rows, width = tokens.shape
+    vmem = pl.BlockSpec(memory_space=VMEM)
+    shape = jax.ShapeDtypeStruct
+    return pl.pallas_call(
+        functools.partial(back_two_body, tp, seqs),
+        out_shape=(shape((rows, width), jnp.bfloat16), shape((8, width), jnp.float32)),
+        in_specs=[vmem] * 5,
+        out_specs=(vmem,) * 2,
+        scratch_shapes=[VMEM((rows, width), jnp.bfloat16)]
+        + line_scratch(rows, width, seqs, rows // seqs),
         compiler_params=pltpu.CompilerParams(
             collective_id=ident, has_side_effects=True, vmem_limit_bytes=56 * 2**20
         ),
-        name="attend_back",
-    )(queries, key_values, full, log_total, grads, cosine, sine, key_pos, query_pos, lengths)
+        cost_estimate=line_cost(rows, width),
+        name="back_two",
+    )(projected, first_whole, tokens, residual_grad, gains)
 
 
 def grads_body(rows_last, left_ref, right_ref, *rest):
@@ -523,9 +764,49 @@
     )(*operands)
 
 
-def gain_body(ctx_size, x_ref, o_ref, inbox, send_sem, recv_sem):
+def first_grads_body(normal_ref, proj_ref, residual_ref, attended_ref, out_ref):
+    width = out_ref.shape[0]
+    split = attended_ref.shape[0]
+    tile = 512 if width % 512 == 0 else width
+    contract = (((1,), (1,)), ((), ()))
+    for low in range(0, width, tile):
+        out_ref[low : low + tile, :split] = lax.dot_general(
+            residual_ref[:, low : low + tile].T,
+            attended_ref[...],
+            contract,
+            preferred_element_type=jnp.float32,
+        ).astype(jnp.bfloat16)
+        out_ref[low : low + tile, split:] = lax.dot_general(
+            normal_ref[:, low : low + tile].T,
+            proj_ref[...],
+            contract,
+            preferred_element_type=jnp.float32,
+        ).astype(jnp.bfloat16)
+
+
+def first_grads_of(normal, projected, residual_grad, attended):
+    rows, width = normal.shape
+    columns = projected.shape[0] + attended.shape[0]
+    vmem = pl.BlockSpec(memory_space=VMEM)
+    return pl.pallas_call(
+        first_grads_body,
+        out_shape=jax.ShapeDtypeStruct((width, columns), jnp.bfloat16),
+        in_specs=[vmem] * 4,
+        out_specs=vmem,
+        compiler_params=pltpu.CompilerParams(vmem_limit_bytes=48 * 2**20),
+        cost_estimate=pl.CostEstimate(
+            flops=2 * rows * width * columns,
+            bytes_accessed=2 * (2 * rows * width + (rows + width) * columns),
+            transcendentals=0,
+        ),
+        name="first_grads",
+    )(normal, projected, residual_grad, attended)
+
+
+def gain_body(ctx_size, tp, x_ref, o_ref, inbox, tp_inbox, send_sem, recv_sem, tp_send, tp_recv):
     shards = x_ref.shape[0]
     me = lax.axis_index("fsdp") * ctx_size + lax.axis_index("ctx")
+    z = lax.axis_index("tp")
 
     def to(step):
         other = lax.rem(me + step, shards)
@@ -534,7 +815,11 @@
     barrier = pltpu.get_barrier_semaphore()
     for step in range(1, shards):
         pl.semaphore_signal(barrier, inc=1, device_id=to(step)[1], device_id_type=MESH)
-    pl.semaphore_wait(barrier, shards - 1)
+    for step in range(1, tp):
+        pl.semaphore_signal(
+            barrier, inc=1, device_id={"tp": lax.rem(z + step, tp)}, device_id_type=MESH
+        )
+    pl.semaphore_wait(barrier, shards - 1 + tp - 1)
 
     def copy(step):
         other, where = to(step)
@@ -547,16 +832,32 @@
             device_id_type=MESH,
         )
 
+    def tp_copy(step):
+        return pltpu.make_async_remote_copy(
+            src_ref=tp_inbox.at[0],
+            dst_ref=tp_inbox.at[step],
+            send_sem=tp_send.at[step - 1],
+            recv_sem=tp_recv.at[step - 1],
+            device_id={"tp": lax.rem(z + step, tp)},
+            device_id_type=MESH,
+        )
+
     for step in range(1, shards):
         copy(step).start()
     total = x_ref[me]
     for step in range(1, shards):
         copy(step).wait()
         total += inbox[step - 1]
+    tp_inbox[0] = total
+    for step in range(1, tp):
+        tp_copy(step).start()
+    for step in range(1, tp):
+        tp_copy(step).wait()
+        total += tp_inbox[step]
     o_ref[...] = total
 
 
-def gain_sum(partial, shards, ctx_size, ident):
+def gain_sum(partial, shards, ctx_size, tp, ident):
     two, width = partial.shape
     own = width // shards
     padded = -(-own // 128) * 128
@@ -565,14 +866,17 @@
         ((0, 0), (0, 8 - two), (0, padded - own)),
     )
     total = pl.pallas_call(
-        functools.partial(gain_body, ctx_size),
+        functools.partial(gain_body, ctx_size, tp),
         out_shape=jax.ShapeDtypeStruct((8, padded), jnp.float32),
         in_specs=[pl.BlockSpec(memory_space=VMEM)],
         out_specs=pl.BlockSpec(memory_space=VMEM),
         scratch_shapes=[
             VMEM((shards - 1, 8, padded), jnp.float32),
+            VMEM((tp, 8, padded), jnp.float32),
             pltpu.SemaphoreType.DMA((shards - 1,)),
             pltpu.SemaphoreType.DMA((shards - 1,)),
+            pltpu.SemaphoreType.DMA((tp - 1,)),
+            pltpu.SemaphoreType.DMA((tp - 1,)),
         ],
         compiler_params=pltpu.CompilerParams(collective_id=ident, has_side_effects=True),
         name="gain_sum",
@@ -654,11 +958,15 @@
         projected, *where, ctx_size, 1
     )
 
+    all_rows = seqs * row_count
+
     def over_tp(part, ident):
-        flat = part.astype(low).reshape(seqs * row_count, model_width)
-        return line_sum(flat, tp_size, ident).reshape(part.shape).astype(jnp.float32)
-
-    residual = layer_inputs + over_tp(dot("mcr,dc->mrd", attended, out_proj), 2)
+        flat = part.astype(low).reshape(all_rows, model_width)
+        return line_sum(flat, tp_size, seqs, ident).reshape(part.shape).astype(jnp.float32)
+
+    residual = layer_inputs + over_tp(
+        dot("cr,dc->rd", attended, out_proj).reshape(layer_inputs.shape), 2
+    )
 
     second_root = lax.rsqrt(jnp.mean(residual * residual, -1, keepdims=True) + norm_eps)
     second_standard = residual * second_root
@@ -675,7 +983,6 @@
     grad_gate = (grad_inner * up * sigmoid * (1.0 + gate * (1.0 - sigmoid))).astype(low)
     grad_up = (grad_inner * silu).astype(low)
     grad_pair = jnp.concatenate([grad_gate, grad_up], -1)
-    all_rows = seqs * row_count
     pair_flat = grad_pair.reshape(all_rows, 2 * hidden)
     second_grads = grads_into(
         None, 3 * hidden, 0, second_normal.reshape(all_rows, model_width), pair_flat, False, 256
@@ -691,42 +998,51 @@
     )
     grad_pair, second_grads = lax.optimization_barrier((grad_pair, second_grads))
     second_share = lax.psum_scatter(second_grads, shards, scatter_dimension=0, tiled=True)
-    grad_normal_two = over_tp(dot("mrc,dc->mrd", grad_pair, pair_proj), 3)
-    second_gain = jnp.sum(grad_normal_two * second_standard, (0, 1))
-    scaled = grad_normal_two * gains[1]
-    grad_residual = grad_out + second_root * (
-        scaled - second_standard * jnp.mean(scaled * second_standard, -1, keepdims=True)
-    )
-    grad_residual_low = grad_residual.astype(low)
-
-    grad_attended = dot("dc,mrd->mcr", out_proj, grad_residual_low).astype(low)
-    grad_projected = attend_back(
-        queries, key_values, attended_full, log_total, grad_attended, *where, ctx_size, 4
-    )
-    first_grads = jnp.concatenate(
-        [
-            dot("mrd,mcr->dc", grad_residual_low, attended).astype(low),
-            dot("mrd,mcr->dc", first_normal, grad_projected).astype(low),
-        ],
-        1,
+    normal_part = dot("mrc,dc->mrd", grad_pair, pair_proj).astype(low)
+    mixed_part = dot("mrc,dc->mrd", inner, down_proj).astype(low)
+
+    back, grad_projected, second_gain = back_one(
+        normal_part.reshape(all_rows, model_width),
+        mixed_part.reshape(all_rows, model_width),
+        residual.reshape(all_rows, model_width),
+        grad_out_low.reshape(all_rows, model_width),
+        gains,
+        first_whole,
+        queries,
+        key_values,
+        attended_full,
+        log_total[:, :, None, :],
+        where,
+        ctx_size,
+        tp_size,
+        4,
+    )
+    grad_residual_low = back[:all_rows]
+    mixed = back[all_rows:]
+    first_grads = first_grads_of(
+        first_normal.reshape(all_rows, model_width), grad_projected, grad_residual_low, attended
     )
     grad_projected, first_grads, second_share = lax.optimization_barrier(
         (grad_projected, first_grads, second_share)
     )
     first_share = lax.psum_scatter(first_grads, shards, scatter_dimension=0, tiled=True)
-    grad_normal_one = over_tp(dot("mcr,dc->mrd", grad_projected, in_proj), 5)
-    first_gain = jnp.sum(grad_normal_one * first_standard, (0, 1))
+    input_grad, first_gain = back_two(
+        grad_projected,
+        first_whole,
+        tokens.reshape(all_rows, model_width),
+        grad_residual_low,
+        gains,
+        seqs,
+        tp_size,
+        5,
+    )
     gain_share = gain_sum(
-        jnp.stack([first_gain, second_gain]),
+        jnp.stack([first_gain.sum(0), second_gain.sum(0)]),
         lax.axis_size("fsdp") * ctx_size,
         ctx_size,
+        tp_size,
         7,
     )
-    scaled = grad_normal_one * gains[0]
-    input_grad = grad_residual + first_root * (
-        scaled - first_standard * jnp.mean(scaled * first_standard, -1, keepdims=True)
-    )
-    mixed = (residual + over_tp(dot("mrc,dc->mrd", inner, down_proj), 6)).astype(low)
 
     gradients = (
         first_share[:, out_width:],
@@ -750,7 +1066,7 @@
         down_weight_second,
         norm_gains_second,
     )
-    results = [mixed.reshape(tokens.shape), input_grad.reshape(tokens.shape)]
+    results = [mixed.reshape(tokens.shape), input_grad.reshape(tokens.shape).astype(jnp.float32)]
     for at in range(5):
         updated = adam_update(
             masters[at],

time: 896 us -> 765 us (0.85)
  local copies, waits for them, and re-layouts: 63.3 us -> 11.9 us
  other arithmetic: 110 us -> 73.8 us
  matrix products: 117 us -> 93.1 us
  Pallas kernels: 540 us -> 524 us
    unnamed x92 -> x65, local copies, waits for them, and re-layouts: 57.5 us -> 2.67 us
    dot_general x11 -> x7, matrix products: 117 us -> 93.1 us  [dot(): return jnp.einsum(spec, left, right, preferred_element_type=jnp.float32)]
    pallas_call x6 -> x5, Pallas kernels: 455 us -> 439 us  [the longest x1 199 us: back_one(): pl.pallas_call(functools.partial(back_one_body, n, tp, groups), out_shape...]
    convert_element_type x3 -> x0, other arithmetic: 16.1 us -> none  [the longest x1 9.97 us: on_device(): grad_residual_low = grad_residual.astype(low)]
  transfers between devices with their start and end apart: 4 -> 4, of which waited for: 1 -> 1; matrix products, arithmetic and copies ran while one was open for 21% -> 16% of each run, Pallas kernels for 57% -> 65%
where the time goes in v2:
time: 765 us; the launch traced here: 758 us
  Pallas kernels  524 us (68%)
  matrix products  93.1 us (12%)
  other arithmetic  73.8 us (10%)
  waiting for transfers between devices  30.4 us (4%)
  between operations  14.4 us (2%)
  local copies, waits for them, and re-layouts  11.9 us (2%)
  blocking collectives  10.3 us (1%)
    pallas_call x1, Pallas kernels, back_one(): pl.pallas_call(functools.partial(back_one_body, n, tp, groups), out_shape...  199 us
    pallas_call x1, Pallas kernels, back_two(): pl.pallas_call(functools.partial(back_two_body, tp, seqs), out_shape=(sha...  109 us
    pallas_call x1, Pallas kernels, line_sum(): pl.pallas_call(functools.partial(line_body, n, segments), out_shape=jax.S...  101 us
    dot_general x7, matrix products, dot(): return jnp.einsum(spec, left, right, preferred_element_type=jnp.float32)  93.1 us
    pallas_call x1, Pallas kernels, attend(): pl.pallas_call(functools.partial(attend_body, n, groups), out_shape=(shap...  50.9 us
    pallas_call x2, Pallas kernels, grads_into(): pl.pallas_call(functools.partial(grads_body, rows_last), grid=(n // tile,...  33.7 us
    all_gather x1, waiting for transfers between devices, on_device(): first_whole = lax.all_gather(first_pack, shards, axis=0, tiled=True)  30.3 us
    convert_element_type x4, other arithmetic, on_device(): results.append(updated[2].astype(low))  21.1 us
  transfers between devices with their start and end apart: 4, of which 1 were waited for; matrix products, arithmetic and copies ran while one was open for 16% of the time, Pallas kernels for 65%

profile of v2, /device:TPU:0, one launch (start us, length us, event | category | flops | bytes accessed | tf_op | source)
XLA Modules:
  0.0 757.8 jit_solution(588559666938598875)
XLA Ops:
  7.2 0.0 all-gather.6.cloned.1.call-start
  7.2 1.4 convert.24
  8.7 1.2 convert_bitcast_fusion.1
  9.8 1.1 pad_maximum_fusion.2
  10.9 0.0 all-gather.6.cloned.1.call-update
  10.9 0.0 all-gather.4.cloned.1.call-start
  11.0 2.7 convert.21
  13.7 0.3 copy-done.7
  13.9 0.1 convert_bitcast_fusion
  14.1 2.0 pad_maximum_fusion.1
  16.1 0.0 all-gather.4.cloned.1.call-update
  16.2 0.0 reduce-scatter.3.cloned.1.call-start
  16.2 0.1 dynamic-slice
  16.3 0.1 select_reduce_fusion
  16.5 0.6 broadcast_in_dim.46.query_pos_ref
  17.1 10.3 %all-gather = bf16[8,320,2]{1,2,0:T(2,128)(2,1)S(1)} all-gather(bf16[1,320,2]{1,2,0:T(2,128)(2,1)S(1)} %convert_bitcast_fusion.2), channel_id=1, replica_groups=mesh['fsdp'=2,'ctx'=4,'tp'=4] {'fsdp','ctx'}, dimensions={0}, use_global_device_ids=true | all-gather | bytes 11520 | tf_op jit(solution)/shard_map/all_gather | solution.py:927
  27.4 0.1 reshape.237
  27.5 0.5 copy.62
  28.0 3.0 fusion.5
  31.0 0.1 compare_convert_fusion
  31.1 0.1 slice_reduce_fusion
  31.2 1.2 multiply_sine_fusion
  32.4 1.3 broadcast_add_fusion.key_pos_ref
  33.7 4.7 fusion.8.left_ref.grad_out_ref
  38.5 30.3 %all-gather.6.cloned.1.call-done.weight_ref = bf16[2560,1600]{1,0:T(8,128)(2,1)} async-done(((bf16[320,1600]{1,0:T(8,128)(2,1)}), bf16[2560,1600]{1,0:T(8,128)(2,1)}) %all-gather.6.cloned.1.call-update) | async-done | bytes 8192016 | tf_op jit(solution)/shard_map/all_gather | solution.py:926
  68.8 9.7 %fusion.28.proj_ref = f32[3,960,256]{2,1,0:T(8,128)} fusion(bf16[2560,1600]{1,0:T(8,128)(2,1)} %all-gather.6.cloned.1.call-done.weight_ref, bf16[3,1,256,2560]{3,2,1,0:T(8,128)(2,1)} %param.19, f32[2560]{0:T(1024)S(1)} %get-tuple-element.157, f32[3,256]{1,0:T(4,128)S(1)} %add_rsqrt_fusion.1), kind=kOutput, calls=%fused_computation.55 | convolution fusion | flops 3782737920 | bytes 12137472 | tf_op jit(solution)/shard_map/dc,mrd->mcr/dot_general | solution.py:888
  78.4 0.6 broadcast_in_dim.47.length_ref
  79.1 50.9 %attend.1 = (bf16[3,640,256]{2,1,0:T(8,128)(2,1)}, bf16[3,4,2,160,256]{4,3,2,1,0:T(8,128)(2,1)}, f32[3,640,256]{2,1,0:T(8,128)}, bf16[640,768]{1,0:T(8,128)(2,1)}, f32[3,8,256]{2,1,0:T(8,128)}) custom-call(f32[3,960,256]{2,1,0:T(8,128)} %fusion.28.proj_ref, f32[3,40,256]{2,1,0:T(8,128)} %get-tuple-element.192.cos_ref, ...), custom_call_target="tpu_custom_call" | custom-call | tf_op jit(solution)/shard_map/attend/pallas_call | solution.py:365
  130.0 7.4 convolution_convert_fusion.p_ref
  137.4 100.6 %line_sum.1 = bf16[768,2560]{1,0:T(8,128)(2,1)S(1)} custom-call(bf16[768,2560]{1,0:T(8,128)(2,1)} %convolution_convert_fusion.p_ref), custom_call_target="tpu_custom_call" | custom-call | flops 1966080 | bytes 157286400 | tf_op jit(solution)/shard_map/line_sum/pallas_call | solution.py:198
  238.1 4.5 multiply_reduce_fusion
  242.6 8.2 %multiply_convert_fusion.1 = bf16[3,256,2560]{2,1,0:T(8,128)(2,1)} fusion(f32[3,256,2560]{2,1,0:T(8,128)} %get-tuple-element.178, bf16[3,1,256,2560]{3,2,1,0:T(8,128)(2,1)} %param.19, f32[2560]{0:T(1024)S(1)} %get-tuple-element.156, f32[3,256]{1,0:T(4,128)S(1)} %add_rsqrt_fusion), kind=kLoop, calls=%fused_computation.22 | loop fusion | flops 9830400 | bytes 15741952 | tf_op jit(solution)/shard_map/convert_element_type | solution.py:973
  250.8 7.4 convert_add_fusion.1
  258.3 13.5 %fusion.11 = f32[3,256,1792]{2,1,0:T(8,128)} fusion(bf16[2560,5376]{1,0:T(8,128)(2,1)} %all-gather.4.cloned.1.call-done, f32[3,256]{1,0:T(4,128)S(1)} %compare_convert_fusion, bf16[3,1,256,2560]{3,2,1,0:T(8,128)(2,1)} %param.20), kind=kOutput, calls=%fused_computation.25 | convolution fusion | flops 7052328960 | bytes 18615296 | tf_op jit(solution)/shard_map/mrd,dc->mrc/dot_general | solution.py:888
  271.7 12.5 %fusion.1 = f32[3,256,1792]{2,1,0:T(8,128)} fusion(bf16[3,256,2560]{2,1,0:T(8,128)(2,1)S(1)} %copy-done.10, bf16[2560,5376]{1,0:T(8,128)(2,1)} %all-gather.4.cloned.1.call-done), kind=kOutput, calls=%fused_computation.8 | convolution fusion | flops 7046430720 | bytes 18612224 | tf_op jit(solution)/shard_map/mrd,dc->mrc/dot_general | solution.py:888
  284.2 14.5 %multiply_convert_fusion.2 = (bf16[3,256,1792]{2,1,0:T(8,128)(2,1)S(1)}, bf16[3,256,1792]{2,1,0:T(8,128)(2,1)S(1)}, bf16[3,256,1792]{2,1,0:T(8,128)(2,1)S(1)}) fusion(f32[3,256,1792]{2,1,0:T(8,128)} %fusion.1, f32[3,256,1792]{2,1,0:T(8,128)} %fusion.11, bf16[3,256,2560]{2,1,0:T(8,128)(2,1)S(1)} %copy-done.10, ...), kind=kOutput, calls=%fused_computation.29 | convolution fusion | flops 7067074560 | bytes 32374784 | tf_op jit(solution)/shard_map/mrd,dc->mrc/dot_general | solution.py:888
  298.8 3.1 pad_maximum_fusion
  301.9 0.7 copy-done.2
  302.6 20.8 %weight_grads.2.rest_0_ = bf16[2560,5376]{1,0:T(8,128)(2,1)} custom-call(bf16[768,2560]{1,0:T(8,128)(2,1)S(1)} %copy-done.2, bf16[768,3584]{1,0:T(8,128)(2,1)} %bitcast.108), custom_call_target="tpu_custom_call" | custom-call | flops 14092861440 | bytes 27787264 | tf_op jit(solution)/shard_map/weight_grads/pallas_call | solution.py:749
  323.4 12.9 %weight_grads.3 = bf16[2560,5376]{1,0:T(8,128)(2,1)} custom-call(bf16[768,2560]{1,0:T(8,128)(2,1)} %fusion.8.left_ref.grad_out_ref, bf16[768,1792]{1,0:T(8,128)(2,1)S(1)} %bitcast.104, bf16[2560,5376]{1,0:T(8,128)(2,1)} %weight_grads.2.rest_0_), custom_call_target="tpu_custom_call", output_to_operand_aliasing={{}: (2, {})} | custom-call | flops 7046430720 | bytes 15859712 | tf_op jit(solution)/shard_map/weight_grads/pallas_call | solution.py:749
  336.3 0.0 reduce-scatter.3.cloned.1.call-update
  336.4 0.0 reduce-scatter.5.cloned.1.call-start
  336.4 0.7 copy-done.19
  337.1 0.6 broadcast_in_dim.48.log_ref
  337.7 11.1 %fusion.15 = bf16[3,256,2560]{2,1,0:T(8,128)(2,1)} fusion(bf16[3,256,1792]{2,1,0:T(8,128)(2,1)S(1)} %get-tuple-element.181, bf16[2560,5376]{1,0:T(8,128)(2,1)} %all-gather.4.cloned.1.call-done), kind=kOutput, calls=%fused_computation.37 | convolution fusion | flops 7048396800 | bytes 15859712 | tf_op jit(solution)/shard_map/mrc,dc->mrd/dot_general | solution.py:888
  348.8 24.4 %fusion.14 = bf16[3,256,2560]{2,1,0:T(8,128)(2,1)} fusion(bf16[3,256,3584]{2,1,0:T(8,128)(2,1)} %pad_maximum_fusion, bf16[2560,5376]{1,0:T(8,128)(2,1)} %all-gather.4.cloned.1.call-done), kind=kOutput, calls=%fused_computation.36 | convolution fusion | flops 14094827520 | bytes 27787264 | tf_op jit(solution)/shard_map/mrc,dc->mrd/dot_general | solution.py:888
  373.2 199.5 %back_one.1 = (bf16[1536,2560]{1,0:T(8,128)(2,1)}, bf16[960,768]{1,0:T(8,128)(2,1)}, f32[8,2560]{1,0:T(8,128)}) custom-call(bf16[768,2560]{1,0:T(8,128)(2,1)} %bitcast.114, bf16[768,2560]{1,0:T(8,128)(2,1)} %bitcast.113, f32[768,2560]{1,0:T(8,128)} %get-tuple-element.186.residual_ref, bf16[768,2560]{1,0:T(8,128)(2,1)} %fusion.8.left_ref.grad_out_ref, ...), custom_call_target="tpu_custom_call" | custom-call | flops 3932160 | bytes 314572800 | tf_op jit(solution)/shard_map/back_one/pallas_call | solution.py:608
  572.7 5.8 fusion.58
  578.5 14.0 %first_grads.1 = bf16[2560,1600]{1,0:T(8,128)(2,1)} custom-call(bf16[768,2560]{1,0:T(8,128)(2,1)} %get-tuple-element.188.normal_ref, bf16[960,768]{1,0:T(8,128)(2,1)S(1)} %copy-done.3, bf16[768,2560]{1,0:T(8,128)(2,1)} %get-tuple-element.184.residual_ref.residual_grad_ref, bf16[640,768]{1,0:T(8,128)(2,1)S(1)} %copy-done.4), custom_call_target="tpu_custom_call" | custom-call | flops 6291456000 | bytes 18513920 | tf_op jit(solution)/shard_map/first_grads/pallas_call | solution.py:791
  592.5 0.0 reduce-scatter.5.cloned.1.call-update
  592.5 0.9 copy-done.18
  593.4 0.1 stack.10
  593.5 109.3 %back_two.1 = (bf16[768,2560]{1,0:T(8,128)(2,1)}, f32[8,2560]{1,0:T(8,128)}) custom-call(bf16[960,768]{1,0:T(8,128)(2,1)} %get-tuple-element.45.proj_ref, bf16[2560,1600]{1,0:T(8,128)(2,1)} %all-gather.6.cloned.1.call-done.weight_ref, bf16[768,2560]{1,0:T(8,128)(2,1)} %bitcast.105, bf16[768,2560]{1,0:T(8,128)(2,1)} %get-tuple-element.184.residual_ref.residual_grad_ref, ...), custom_call_target="tpu_custom_call" | custom-call | flops 1966080 | bytes 157286400 | tf_op jit(solution)/shard_map/back_two/pallas_call | solution.py:700
  702.8 0.9 reduce_sum.48
  703.7 0.1 stack.9
  703.8 0.7 pad.4.x_ref
  704.5 15.8 %gain_sum.1 = f32[8,384]{1,0:T(8,128)} custom-call(f32[8,8,384]{2,1,0:T(8,128)} %pad.4.x_ref), custom_call_target="tpu_custom_call" | custom-call | tf_op jit(solution)/shard_map/gain_sum/pallas_call | solution.py:868
  720.3 7.3 convert.27
  727.6 2.1 multiply_subtract_fusion.4
  729.7 0.0 slice-start.3
  729.7 6.6 fusion.45
  736.5 7.0 fusion.48
  743.5 4.5 fusion.54
  748.1 3.0 fusion.51
  (81 shorter events, 0.3 us)
Async XLA Ops:
  7.2 61.6 %all-gather.6.cloned.1.call-start = ((), (), s32[]{:S(2)}) async-start(), calls=%async_computation.3 | async-start | bytes 9584640 | tf_op jit(solution)/shard_map/all_gather | solution.py:926
  10.9 3.0 copy-start.7
  10.9 247.3 %all-gather.4.cloned.1.call-start = ((), (), s32[]{:S(2)}) async-start(), calls=%async_computation.2 | async-start | bytes 30965760 | tf_op jit(solution)/shard_map/all_gather | solution.py:928
  14.1 2.2 copy-start.25
  14.1 3.0 copy-start.20
  16.1 14.9 %copy-start.24 = (s32[3,1]{0,1:T(1,128)S(1)}, s32[3,1]{0,1:T(1,128)}, u32[]{:S(2)}) copy-start(s32[3,1]{0,1:T(1,128)} %param.21) | copy-start | bytes 40
  16.2 576.3 %reduce-scatter.3.cloned.1.call-start = ((), (), s32[]{:S(2)}) async-start(), calls=%async_computation.4 | async-start | bytes 30965760 | tf_op jit(solution)/shard_map/reduce_scatter | solution.py:1000
  27.5 6.2 copy-start.17
  137.4 100.6 %copy-start.5 = (bf16[3,1,256,2560]{3,2,1,0:T(8,128)(2,1)S(1)}, bf16[3,1,256,2560]{3,2,1,0:T(8,128)(2,1)}, u32[]{:S(2)}) copy-start(bf16[3,1,256,2560]{3,2,1,0:T(8,128)(2,1)} %param.19) | copy-start | bytes 11796484
  238.0 4.5 copy-start
  242.6 8.2 %copy-start.1 = (bf16[768,2560]{1,0:T(8,128)(2,1)S(1)}, bf16[768,2560]{1,0:T(8,128)(2,1)}, u32[]{:S(2)}) copy-start(bf16[768,2560]{1,0:T(8,128)(2,1)} %copy-done) | copy-start | bytes 11796484
  242.6 8.2 %copy-start.6 = (bf16[3,1,256,2560]{3,2,1,0:T(8,128)(2,1)S(1)}, bf16[3,1,256,2560]{3,2,1,0:T(8,128)(2,1)}, u32[]{:S(2)}) copy-start(bf16[3,1,256,2560]{3,2,1,0:T(8,128)(2,1)} %param.19) | copy-start | bytes 11796484
  258.3 13.5 %copy-start.10 = (bf16[3,256,2560]{2,1,0:T(8,128)(2,1)S(1)}, bf16[3,256,2560]{2,1,0:T(8,128)(2,1)}, u32[]{:S(2)}) copy-start(bf16[3,256,2560]{2,1,0:T(8,128)(2,1)} %multiply_convert_fusion.1) | copy-start | bytes 11796484
  298.8 3.9 copy-start.2
  336.3 0.7 copy-start.19
  336.4 407.1 %reduce-scatter.5.cloned.1.call-start = ((), (), s32[]{:S(2)}) async-start(), calls=%async_computation.5 | async-start | bytes 9584640 | tf_op jit(solution)/shard_map/reduce_scatter | solution.py:1028
  572.7 5.8 copy-start.3
  572.7 5.8 copy-start.4
  592.5 0.9 copy-start.18
  593.5 134.1 %copy-start.21 = (f32[2,320]{1,0:T(2,128)S(1)}, f32[2,320]{1,0:T(2,128)}, u32[]{:S(2)}) copy-start(f32[2,320]{1,0:T(2,128)} %param.35) | copy-start | bytes 7684
  593.5 134.1 %copy-start.22 = (f32[2,320]{1,0:T(2,128)S(1)}, f32[2,320]{1,0:T(2,128)}, u32[]{:S(2)}) copy-start(f32[2,320]{1,0:T(2,128)} %param.37) | copy-start | bytes 7684
  593.5 134.1 %copy-start.23 = (f32[2,320]{1,0:T(2,128)S(1)}, f32[2,320]{1,0:T(2,128)}, u32[]{:S(2)}) copy-start(f32[2,320]{1,0:T(2,128)} %param.36) | copy-start | bytes 7684
  593.5 136.2 %copy-start.13 = (f32[1792,320]{0,1:T(8,128)S(1)}, f32[1792,320]{0,1:T(8,128)}, u32[]{:S(2)}) copy-start(f32[1792,320]{0,1:T(8,128)} %param.34) | copy-start | bytes 6881284
  720.2 9.5 %copy-start.8 = (f32[1792,320]{0,1:T(8,128)S(1)}, f32[1792,320]{0,1:T(8,128)}, u32[]{:S(2)}) copy-start(f32[1792,320]{0,1:T(8,128)} %param.32) | copy-start | bytes 6881284
  720.2 16.1 %slice-start = ((s8[4587520]{0:T(1024)(128)(4,1)}), s8[4194304]{0:T(1024)(128)(4,1)S(1)}, s32[]{:S(2)}) async-start(s8[4587520]{0:T(1024)(128)(4,1)} %bitcast.106), calls=%async_computation.6 | async-start | bytes 8388608
  720.3 16.1 %slice-start.2 = ((s8[4587520]{0:T(1024)(128)(4,1)}), s8[4194304]{0:T(1024)(128)(4,1)S(1)}, s32[]{:S(2)}) async-start(s8[4587520]{0:T(1024)(128)(4,1)} %bitcast.109), calls=%async_computation.8 | async-start | bytes 8388608
  720.3 16.1 %slice-start.4 = ((s8[4587520]{0:T(1024)(128)(4,1)}), s8[4194304]{0:T(1024)(128)(4,1)S(1)}, s32[]{:S(2)}) async-start(s8[4587520]{0:T(1024)(128)(4,1)} %bitcast.111), calls=%async_computation.10 | async-start | bytes 8388608
  729.7 6.7 slice-start.1
  729.7 6.7 slice-start.3
  729.7 6.7 slice-start.5
  729.7 6.7 copy-start.11
  736.4 7.1 copy-start.9
  736.4 7.0 copy-start.14
  743.5 4.6 copy-start.12
  743.5 4.6 copy-start.15
  743.5 4.6 copy-start.16
Sparse Core Ops, SparseCore 0:
  11.1 57.6 all-gather.5
  70.6 155.9 all-gather.3
  336.5 184.5 reduce-scatter.2
  592.6 72.5 reduce-scatter.4

commit v3 on v2

--- a/solution.py
+++ b/solution.py
@@ -177,36 +177,8 @@
     return [VMEM((rows, width), jnp.bfloat16)] + [pltpu.SemaphoreType.DMA((2, chunks))] * 4
 
 
-def line_body(n, segments, p_ref, o_ref, inbox, *sems):
-    z = lax.axis_index("tp")
-    pl.semaphore_wait(pltpu.get_barrier_semaphore(), line_greet(n, z))
-
-    def finish(segment, rows, total):
-        o_ref[rows, :] = total.astype(jnp.bfloat16)
-
-    line = Line(n, z, segments, p_ref.shape[0] // segments, p_ref, inbox, o_ref, sems, finish)
-    line.run(0, line.ticks)
-    line.drain()
-
-
 def line_cost(rows, width):
     return pl.CostEstimate(flops=rows * width, bytes_accessed=80 * rows * width, transcendentals=0)
-
-
-def line_sum(part, n, segments, ident):
-    rows, width = part.shape
-    return pl.pallas_call(
-        functools.partial(line_body, n, segments),
-        out_shape=jax.ShapeDtypeStruct((rows, width), jnp.bfloat16),
-        in_specs=[pl.BlockSpec(memory_space=VMEM)],
-        out_specs=pl.BlockSpec(memory_space=VMEM),
-        scratch_shapes=line_scratch(rows, width, segments, rows // segments),
-        compiler_params=pltpu.CompilerParams(
-            collective_id=ident, has_side_effects=True, vmem_limit_bytes=48 * 2**20
-        ),
-        cost_estimate=line_cost(rows, width),
-        name="line_sum",
-    )(part)
 
 
 def mean_of(values):
@@ -224,17 +196,6 @@
     return root * (scaled - standard * mean_of(scaled * standard))
 
 
-def greet(n):
-    me = lax.axis_index("ctx")
-    barrier = pltpu.get_barrier_semaphore()
-    for step in range(1, n):
-        pl.semaphore_signal(
-            barrier, inc=1, device_id={"ctx": lax.rem(me + step, n)}, device_id_type=MESH
-        )
-    pl.semaphore_wait(barrier, n - 1)
-    return me
-
-
 def turn(first, second, cosine, sine):
     return jnp.concatenate([first * cosine - second * sine, second * cosine + first * sine], 0)
 
@@ -248,32 +209,219 @@
     return jnp.where(allowed, 0.0, neg_big)
 
 
-def attend_body(
+def cut(rows, parts):
+    tiles = rows // 16
+    ends = [tiles * i // parts * 16 for i in range(parts + 1)]
+    return [(low, high - low) for low, high in zip(ends[:-1], ends[1:])]
+
+
+class Gather:
+    def __init__(self, source, whole, low, length, block_rows, fsdp, n, sems):
+        self.source, self.whole = source, whole
+        self.low, self.length, self.block_rows = low, length, block_rows
+        self.fsdp, self.n = fsdp, n
+        self.f, self.me = lax.axis_index("fsdp"), lax.axis_index("ctx")
+        self.across = lax.rem(self.me + n // 2, n)
+        self.other = self.me + 1 - 2 * lax.rem(self.me, 2)
+        self.sems = sems
+        self.first = length // 32 * 16
+
+    def at(self, f, ctx, low=0, length=None):
+        start = (f * self.n + ctx) * self.block_rows + self.low + low
+        return self.whole.at[
+            pl.ds(pl.multiple_of(start, 16), self.length if length is None else length)
+        ]
+
+    def copy(self, kind, source, target, where):
+        return pltpu.make_async_remote_copy(
+            src_ref=source,
+            dst_ref=target,
+            send_sem=self.sems.at[0, kind],
+            recv_sem=self.sems.at[1, kind],
+            device_id=where,
+            device_id_type=MESH,
+        )
+
+    def own(self):
+        return self.source.at[pl.ds(self.low, self.length)]
+
+    def ahead(self, j):
+        return lax.rem(self.f + j, self.fsdp)
+
+    def behind(self, j):
+        return lax.rem(self.f + self.fsdp - j, self.fsdp)
+
+    def to_across(self):
+        return self.copy(0, self.own(), self.at(self.f, self.me), {"ctx": self.across})
+
+    def to_other(self):
+        return self.copy(1, self.own(), self.at(self.f, self.me), {"ctx": self.other})
+
+    def across_to_other(self):
+        at = self.at(self.f, self.across)
+        return self.copy(2, at, at, {"ctx": self.other})
+
+    def to_ahead(self, j):
+        return self.copy(3 * j, self.own(), self.at(self.f, self.me), {"fsdp": self.ahead(j)})
+
+    def behind_to_other(self, j):
+        at = self.at(self.behind(j), self.me)
+        return self.copy(3 * j + 1, at, at, {"ctx": self.other})
+
+    def corner_to_other(self, j):
+        at = self.at(self.behind(j), self.across)
+        return self.copy(3 * j + 2, at, at, {"ctx": self.other})
+
+    def across_to_ahead(self, j):
+        at = self.at(self.f, self.across, 0, self.first)
+        return self.copy(3 * self.fsdp + 2 * j - 2, at, at, {"fsdp": self.ahead(j)})
+
+    def behind_to_across(self, j):
+        at = self.at(self.behind(j), self.me, self.first, self.length - self.first)
+        return self.copy(3 * self.fsdp + 2 * j - 1, at, at, {"ctx": self.across})
+
+    def local(self):
+        return pltpu.make_async_copy(self.own(), self.at(self.f, self.me), self.sems.at[2, 0])
+
+    def start(self):
+        self.to_across().start()
+        for j in range(1, self.fsdp):
+            self.to_ahead(j).start()
+        self.to_other().start()
+        self.local().start()
+
+    def forward(self):
+        self.to_across().wait_recv()
+        for j in range(1, self.fsdp):
+            self.across_to_ahead(j).start()
+        self.across_to_other().start()
+        for j in range(1, self.fsdp):
+            self.to_ahead(j).wait_recv()
+            self.behind_to_across(j).start()
+            self.behind_to_other(j).start()
+
+    def corner(self):
+        for j in range(1, self.fsdp):
+            self.across_to_ahead(j).wait_recv()
+            self.behind_to_across(j).wait_recv()
+            self.corner_to_other(j).start()
+
+    def finish(self):
+        self.local().wait()
+        self.to_other().wait_recv()
+        self.across_to_other().wait_recv()
+        for j in range(1, self.fsdp):
+            self.behind_to_other(j).wait_recv()
+            self.corner_to_other(j).wait_recv()
+
+    def drain(self):
+        self.to_across().wait_send()
+        self.to_other().wait_send()
+        self.across_to_other().wait_send()
+        for j in range(1, self.fsdp):
+            self.to_ahead(j).wait_send()
+            self.behind_to_other(j).wait_send()
+            self.corner_to_other(j).wait_send()
+            self.across_to_ahead(j).wait_send()
+            self.behind_to_across(j).wait_send()
+
+
+def gather_sems(fsdp):
+    return pltpu.SemaphoreType.DMA((3, 5 * fsdp - 2))
+
+
+FIRST_PIECES = 2
+SECOND_PIECES = 4
+
+
+def front_body(
     n,
+    tp,
+    fsdp,
     groups,
-    proj_ref,
+    out_width,
+    token_ref,
+    first_ref,
+    second_ref,
     cos_ref,
     sin_ref,
     key_pos_ref,
     query_pos_ref,
     length_ref,
+    first_whole,
+    second_whole,
+    normal_ref,
+    gain_ref,
     q_ref,
     kv_ref,
     full_ref,
     low_ref,
     log_ref,
+    residual_ref,
+    out_ref,
+    proj,
     bias,
+    parts,
     send_sem,
     recv_sem,
+    first_sems,
+    second_sems,
+    inbox,
+    *sems,
 ):
-    me = greet(n)
+    z = lax.axis_index("tp")
+    f = lax.axis_index("fsdp")
+    me = lax.axis_index("ctx")
+    peers = line_greet(tp, z)
+    barrier = pltpu.get_barrier_semaphore()
+    for step in range(1, n):
+        pl.semaphore_signal(
+            barrier, inc=1, device_id={"ctx": lax.rem(me + step, n)}, device_id_type=MESH
+        )
+    for step in range(1, fsdp):
+        pl.semaphore_signal(
+            barrier, inc=1, device_id={"fsdp": lax.rem(f + step, fsdp)}, device_id_type=MESH
+        )
+    pl.semaphore_wait(barrier, peers + n - 1 + fsdp - 1)
+
     seqs, _, rows = q_ref.shape
     dim = HEAD_DIMENSION
     half = dim // 2
     group_width = (GROUP + 2) * dim
-
-    def block(m, col):
-        return proj_ref[m, col : col + half, :], proj_ref[m, col + half : col + dim, :]
+    in_width = groups * group_width
+    heads = groups * GROUP
+    width = token_ref.shape[1]
+    tile = 512 if width % 512 == 0 else width
+
+    def gathers(source, whole, pieces, sems):
+        block = source.shape[0]
+        return [
+            Gather(source, whole, low, length, block, fsdp, n, sems.at[i])
+            for i, (low, length) in enumerate(cut(block, pieces))
+        ]
+
+    first = gathers(first_ref, first_whole, FIRST_PIECES, first_sems)
+    second = gathers(second_ref, second_whole, SECOND_PIECES, second_sems)
+    for piece in first:
+        piece.start()
+    for piece in first:
+        piece.forward()
+    for piece in first:
+        piece.corner()
+    second[0].start()
+    for piece in first:
+        piece.finish()
+
+    columns = out_width + in_width
+    base = columns // 128 * 128
+    turned = first_whole[:, base : base + 128].astype(jnp.float32).T
+    gain_ref[...] = turned[columns - base : columns - base + 8]
+
+    def columns_of(m):
+        return pl.ds(pl.multiple_of(m * rows, 128), rows)
+
+    def rows_of(m):
+        return pl.ds(pl.multiple_of(m * rows, CHUNK), rows)
 
     def copy(m, step):
         return pltpu.make_async_remote_copy(
@@ -285,68 +433,132 @@
             device_id_type=MESH,
         )
 
-    def spread(m, carry):
+    def project(m, carry):
+        values = token_ref[rows_of(m), :].astype(jnp.float32)
+        root = lax.rsqrt(mean_of(values * values) + norm_eps)
+        normal_ref[rows_of(m), :] = (values * root * gain_ref[0:1, :]).astype(jnp.bfloat16)
+        proj[m] = jnp.dot(
+            normal_ref[rows_of(m), :],
+            first_whole[:, out_width : out_width + in_width],
+            preferred_element_type=jnp.float32,
+        ).T
         for g in range(groups):
             col = g * group_width + GROUP * dim
-            kv_ref[m, me, g, :dim, :] = turn(*block(m, col), cos_ref[m], sin_ref[m]).astype(
-                jnp.bfloat16
-            )
-            kv_ref[m, me, g, dim:, :] = proj_ref[m, col + dim : col + 2 * dim, :].astype(
-                jnp.bfloat16
-            )
+            kv_ref[m, me, g, :dim, :] = turn(
+                proj[m, col : col + half, :],
+                proj[m, col + half : col + dim, :],
+                cos_ref[m],
+                sin_ref[m],
+            ).astype(jnp.bfloat16)
+            kv_ref[m, me, g, dim:, :] = proj[m, col + dim : col + 2 * dim, :].astype(jnp.bfloat16)
         for step in range(1, n):
             copy(m, step).start()
         return carry
 
-    lax.fori_loop(0, seqs, spread, 0)
-
-    def sequence(m, carry):
-        for g in range(groups):
-            for h in range(GROUP):
-                low = (g * GROUP + h) * dim
-                q_ref[m, low : low + dim, :] = turn(
-                    *block(m, g * group_width + h * dim), cos_ref[m], sin_ref[m]
-                ).astype(jnp.bfloat16)
+    lax.fori_loop(0, seqs, project, 0)
+    for piece in second[1:]:
+        piece.start()
+
+    def finish(segment, at, total):
+        values = token_ref[at, :].astype(jnp.float32) + total
+        residual_ref[at, :] = values
+        root = lax.rsqrt(mean_of(values * values) + norm_eps)
+        out_ref[at, :] = (values * root * gain_ref[1:2, :]).astype(jnp.bfloat16)
+
+    line = Line(tp, z, seqs, rows, parts, inbox, out_ref, sems, finish)
+
+    def head(m, at):
+        g = at // GROUP
+        h = at % GROUP
+        low = pl.ds(pl.multiple_of(at * dim, 16), dim)
+        col = pl.multiple_of(g * group_width + h * dim, 8)
+        query = turn(
+            proj[m, pl.ds(col, half), :],
+            proj[m, pl.ds(pl.multiple_of(col + half, 8), half), :],
+            cos_ref[m],
+            sin_ref[m],
+        ).astype(jnp.bfloat16)
+        q_ref[m, low, :] = query
+        scores = [
+            lax.dot_general(
+                kv_ref[m, j, g, :dim, :],
+                query,
+                (((0,), (0,)), ((), ())),
+                preferred_element_type=jnp.float32,
+            )
+            * (log2_e * dim**-0.5)
+            + bias[j * rows : (j + 1) * rows, :]
+            for j in range(n)
+        ]
+        top = functools.reduce(jnp.maximum, [jnp.max(s, axis=0, keepdims=True) for s in scores])
+        total = jnp.zeros_like(top)
+        out = jnp.zeros((dim, rows), jnp.float32)
+        for j in range(n):
+            weights = jnp.exp2(scores[j] - top)
+            total += jnp.sum(weights, axis=0, keepdims=True)
+            out += jnp.dot(
+                kv_ref[m, j, g, dim:, :],
+                weights.astype(jnp.bfloat16),
+                preferred_element_type=jnp.float32,
+            )
+        out = out / total
+        full_ref[m, low, :] = out
+        low_ref[low, columns_of(m)] = out.astype(jnp.bfloat16)
+        log_ref[m, at] = top + jnp.log2(total)
+
+    def ready(m):
         bias[...] = mask_bias(key_pos_ref[m], query_pos_ref[m], length_ref[m])
         for step in range(1, n):
             copy(m, step).wait_recv()
-        for g in range(groups):
-            for h in range(GROUP):
-                low = (g * GROUP + h) * dim
-                query = q_ref[m, low : low + dim, :]
-                scores = [
-                    lax.dot_general(
-                        kv_ref[m, j, g, :dim, :],
-                        query,
-                        (((0,), (0,)), ((), ())),
-                        preferred_element_type=jnp.float32,
-                    )
-                    * (log2_e * dim**-0.5)
-                    + bias[j * rows : (j + 1) * rows, :]
-                    for j in range(n)
-                ]
-                top = functools.reduce(
-                    jnp.maximum, [jnp.max(s, axis=0, keepdims=True) for s in scores]
-                )
-                total = jnp.zeros_like(top)
-                out = jnp.zeros((dim, rows), jnp.float32)
-                for j in range(n):
-                    weights = jnp.exp2(scores[j] - top)
-                    total += jnp.sum(weights, axis=0, keepdims=True)
-                    out += jnp.dot(
-                        kv_ref[m, j, g, dim:, :],
-                        weights.astype(jnp.bfloat16),
-                        preferred_element_type=jnp.float32,
-                    )
-                out = out / total
-                full_ref[m, low : low + dim, :] = out
-                low_ref[low : low + dim, pl.ds(pl.multiple_of(m * rows, 128), rows)] = out.astype(
-                    jnp.bfloat16
-                )
-                log_ref[m, g * GROUP + h : g * GROUP + h + 1, :] = top + jnp.log2(total)
+
+    def product(m):
+        left = low_ref[:, columns_of(m)].T
+        for low in range(0, width, tile):
+            parts[rows_of(m), low : low + tile] = lax.dot_general(
+                left,
+                first_whole[low : low + tile, :out_width],
+                (((1,), (1,)), ((), ())),
+                preferred_element_type=jnp.float32,
+            ).astype(jnp.bfloat16)
+
+    def sequence(m, carry):
+        ready(m)
+
+        def item(at, inner):
+            line.tick((m - 1) * heads + at)
+            head(m, at)
+            return inner
+
+        lax.fori_loop(0, heads, item, 0)
+        product(m)
         return carry
 
-    lax.fori_loop(0, seqs, sequence, 0)
+    def opening(at, carry):
+        head(0, at)
+        return carry
+
+    ready(0)
+    lax.fori_loop(0, heads, opening, 0)
+    product(0)
+    second[0].forward()
+    lax.fori_loop(1, 2, sequence, 0)
+    second[1].forward()
+    lax.fori_loop(2, seqs, sequence, 0)
+    for piece in second[2:]:
+        piece.forward()
+    at = (seqs - 1) * heads
+    line.run(at, at + 4)
+    for piece in second[:2]:
+        piece.corner()
+    line.run(at + 4, at + 10)
+    for piece in second[2:]:
+        piece.corner()
+    line.run(at + 10, line.ticks)
+    for piece in second:
+        piece.finish()
+    line.drain()
+    for piece in first + second:
+        piece.drain()
 
     def drain(m, carry):
         for step in range(1, n):
@@ -356,33 +568,50 @@
     lax.fori_loop(0, seqs, drain, 0)
 
 
-def attend(projected, cosine, sine, key_pos, query_pos, lengths, n, ident):
-    seqs, width, rows = projected.shape
-    groups = width // ((GROUP + 2) * HEAD_DIMENSION)
+def front(tokens, first_pack, second_pack, where, seqs, out_width, in_width, n, tp, fsdp, ident):
+    all_rows, model_width = tokens.shape
+    rows = all_rows // seqs
+    groups = in_width // ((GROUP + 2) * HEAD_DIMENSION)
     heads = groups * GROUP
+    shards = n * fsdp
+    dim = HEAD_DIMENSION
     shape = jax.ShapeDtypeStruct
+    low, wide = jnp.bfloat16, jnp.float32
     vmem = pl.BlockSpec(memory_space=VMEM)
+    hbm = pl.BlockSpec(memory_space=pl.ANY)
     return pl.pallas_call(
-        functools.partial(attend_body, n, groups),
+        functools.partial(front_body, n, tp, fsdp, groups, out_width),
         out_shape=(
-            shape((seqs, heads * HEAD_DIMENSION, rows), jnp.bfloat16),
-            shape((seqs, n, groups, 2 * HEAD_DIMENSION, rows), jnp.bfloat16),
-            shape((seqs, heads * HEAD_DIMENSION, rows), jnp.float32),
-            shape((heads * HEAD_DIMENSION, seqs * rows), jnp.bfloat16),
-            shape((seqs, heads, rows), jnp.float32),
+            shape((shards * first_pack.shape[0], first_pack.shape[1]), low),
+            shape((shards * second_pack.shape[0], second_pack.shape[1]), low),
+            shape((all_rows, model_width), low),
+            shape((8, model_width), wide),
+            shape((seqs, heads * dim, rows), low),
+            shape((seqs, n, groups, 2 * dim, rows), low),
+            shape((seqs, heads * dim, rows), wide),
+            shape((heads * dim, all_rows), low),
+            shape((seqs, heads, 1, rows), wide),
+            shape((all_rows, model_width), wide),
+            shape((all_rows, model_width), low),
         ),
-        in_specs=[vmem] * 6,
-        out_specs=(vmem,) * 5,
+        in_specs=[vmem, hbm, hbm] + [vmem] * 5,
+        out_specs=(vmem, hbm) + (vmem,) * 9,
         scratch_shapes=[
-            VMEM((n * rows, rows), jnp.float32),
+            VMEM((seqs, in_width, rows), wide),
+            VMEM((n * rows, rows), wide),
+            VMEM((all_rows, model_width), low),
             pltpu.SemaphoreType.DMA((seqs, n - 1)),
             pltpu.SemaphoreType.DMA((seqs, n - 1)),
-        ],
+            pltpu.SemaphoreType.DMA((FIRST_PIECES, 3, 5 * fsdp - 2)),
+            pltpu.SemaphoreType.DMA((SECOND_PIECES, 3, 5 * fsdp - 2)),
+        ]
+        + line_scratch(all_rows, model_width, seqs, rows),
         compiler_params=pltpu.CompilerParams(
-            collective_id=ident, has_side_effects=True, vmem_limit_bytes=56 * 2**20
+            collective_id=ident, has_side_effects=True, vmem_limit_bytes=60 * 2**20
         ),
-        name="attend",
-    )(projected, cosine, sine, key_pos, query_pos, lengths)
+        cost_estimate=line_cost(all_rows, model_width),
+        name="front",
+    )(tokens, first_pack, second_pack, *where)
 
 
 def back_one_body(
@@ -650,6 +879,7 @@
 def back_two_body(
     tp,
     seqs,
+    skip,
     proj_ref,
     weight_ref,
     token_ref,
@@ -665,7 +895,6 @@
     pl.semaphore_wait(pltpu.get_barrier_semaphore(), line_greet(tp, z))
     gain_sums[...] = jnp.zeros_like(gain_sums)
     rows = token_ref.shape[0] // seqs
-    skip = weight_ref.shape[1] - proj_ref.shape[0]
     width = weight_ref.shape[0]
     tile = 512 if width % 512 == 0 else width
 
@@ -681,7 +910,7 @@
         for low in range(0, width, tile):
             parts[m * rows : (m + 1) * rows, low : low + tile] = lax.dot_general(
                 left,
-                weight_ref[low : low + tile, skip:],
+                weight_ref[low : low + tile, skip : skip + proj_ref.shape[0]],
                 (((1,), (1,)), ((), ())),
                 preferred_element_type=jnp.float32,
             ).astype(jnp.bfloat16)
@@ -693,12 +922,12 @@
     line.drain()
 
 
-def back_two(projected, first_whole, tokens, residual_grad, gains, seqs, tp, ident):
+def back_two(projected, first_whole, tokens, residual_grad, gains, skip, seqs, tp, ident):
     rows, width = tokens.shape
     vmem = pl.BlockSpec(memory_space=VMEM)
     shape = jax.ShapeDtypeStruct
     return pl.pallas_call(
-        functools.partial(back_two_body, tp, seqs),
+        functools.partial(back_two_body, tp, seqs, skip),
         out_shape=(shape((rows, width), jnp.bfloat16), shape((8, width), jnp.float32)),
         in_specs=[vmem] * 5,
         out_specs=(vmem,) * 2,
@@ -710,6 +939,86 @@
         cost_estimate=line_cost(rows, width),
         name="back_two",
     )(projected, first_whole, tokens, residual_grad, gains)
+
+
+def hidden_body(
+    normal_ref, grad_out_ref, gate_ref, up_ref, down_ref, inner_ref, grad_gate_ref, grad_up_ref
+):
+    def product(left, right):
+        return jnp.dot(left[...], right[...], preferred_element_type=jnp.float32)
+
+    gate = product(normal_ref, gate_ref)
+    up = product(normal_ref, up_ref)
+    grad_inner = product(grad_out_ref, down_ref)
+    sigmoid = jax.nn.sigmoid(gate)
+    silu = gate * sigmoid
+    inner_ref[...] = (silu * up).astype(jnp.bfloat16)
+    grad_gate_ref[...] = (
+        grad_inner * up * sigmoid * (1.0 + gate * (1.0 - sigmoid))
+    ).astype(jnp.bfloat16)
+    grad_up_ref[...] = (grad_inner * silu).astype(jnp.bfloat16)
+
+
+def hidden_units(normal, grad_out, whole, tile=256):
+    rows, width = normal.shape
+    columns = whole.shape[1]
+    units = columns // 3
+    steps = units // tile
+    vmem = pl.BlockSpec(memory_space=VMEM)
+    return pl.pallas_call(
+        hidden_body,
+        grid=(steps,),
+        out_shape=(jax.ShapeDtypeStruct((rows, units), jnp.bfloat16),) * 3,
+        in_specs=[vmem, vmem]
+        + [
+            pl.BlockSpec((width, tile), functools.partial(lambda k, i: (0, k * steps + i), k))
+            for k in range(3)
+        ],
+        out_specs=[pl.BlockSpec((rows, tile), lambda i: (0, i))] * 3,
+        compiler_params=pltpu.CompilerParams(vmem_limit_bytes=56 * 2**20),
+        cost_estimate=pl.CostEstimate(
+            flops=2 * rows * width * columns,
+            bytes_accessed=2 * (rows + width) * columns,
+            transcendentals=rows * units,
+        ),
+        name="hidden_units",
+    )(normal, grad_out, whole, whole, whole)
+
+
+def leave_body(inner_ref, grad_gate_ref, grad_up_ref, weight_ref, normal_ref, mixed_ref):
+    units = inner_ref.shape[1]
+
+    def product(left, k):
+        return lax.dot_general(
+            left[...],
+            weight_ref[:, k * units : (k + 1) * units],
+            (((1,), (1,)), ((), ())),
+            preferred_element_type=jnp.float32,
+        )
+
+    normal_ref[...] = (product(grad_gate_ref, 0) + product(grad_up_ref, 1)).astype(jnp.bfloat16)
+    mixed_ref[...] = product(inner_ref, 2).astype(jnp.bfloat16)
+
+
+def leave(inner, grad_gate, grad_up, whole, tile=256):
+    rows, units = inner.shape
+    width, columns = whole.shape
+    low = jnp.bfloat16
+    vmem = pl.BlockSpec(memory_space=VMEM)
+    return pl.pallas_call(
+        leave_body,
+        grid=(width // tile,),
+        out_shape=(jax.ShapeDtypeStruct((rows, width), low),) * 2,
+        in_specs=[vmem] * 3 + [pl.BlockSpec((tile, columns), lambda i: (i, 0))],
+        out_specs=[pl.BlockSpec((rows, tile), lambda i: (0, i))] * 2,
+        compiler_params=pltpu.CompilerParams(vmem_limit_bytes=56 * 2**20),
+        cost_estimate=pl.CostEstimate(
+            flops=2 * rows * width * columns,
+            bytes_accessed=2 * (rows + width) * columns,
+            transcendentals=0,
+        ),
+        name="leave",
+    )(inner, grad_gate, grad_up, whole)
 
 
 def grads_body(rows_last, left_ref, right_ref, *rest):
@@ -921,15 +1230,19 @@
     in_width = attention_input_weight.shape[1]
     shards = ("fsdp", "ctx")
 
-    first_pack = jnp.concatenate([attend_out.T, attention_input_weight], 1).astype(low)
+    own = attention_input_weight.shape[0]
+    used = out_width + in_width + 2
+    padded = -(-used // 128) * 128
+    first_pack = jnp.concatenate(
+        [
+            attend_out.T,
+            attention_input_weight,
+            norm_gains.T,
+            jnp.zeros((own, padded - used), jnp.float32),
+        ],
+        1,
+    ).astype(low)
     second_pack = jnp.concatenate([gate_up, down_weight.T], 1).astype(low)
-    first_whole = lax.all_gather(first_pack, shards, axis=0, tiled=True)
-    gains = lax.all_gather(norm_gains.astype(low), shards, axis=1, tiled=True).astype(jnp.float32)
-    second_whole = lax.all_gather(second_pack, shards, axis=0, tiled=True)
-    out_proj = first_whole[:, :out_width]
-    in_proj = first_whole[:, out_width:]
-    pair_proj = second_whole[:, : 2 * hidden]
-    down_proj = second_whole[:, 2 * hidden :]
 
     orders = span_order.reshape(seqs, 2 * ctx_size)
     lengths = seq_lengths.reshape(seqs)
@@ -949,69 +1262,60 @@
     length_row = jnp.broadcast_to(lengths[:, None, None], query_pos.shape)
     where = (cosine, sine, key_pos, query_pos, length_row)
 
-    layer_inputs = tokens.reshape(seqs, row_count, model_width).astype(jnp.float32)
-    first_root = lax.rsqrt(jnp.mean(layer_inputs * layer_inputs, -1, keepdims=True) + norm_eps)
-    first_standard = layer_inputs * first_root
-    first_normal = (first_standard * gains[0]).astype(low)
-    projected = dot("dc,mrd->mcr", in_proj, first_normal)
-    queries, key_values, attended_full, attended, log_total = attend(
-        projected, *where, ctx_size, 1
+    all_rows = seqs * row_count
+    token_rows = tokens.reshape(all_rows, model_width)
+    (
+        first_whole,
+        second_whole,
+        first_normal,
+        gains,
+        queries,
+        key_values,
+        attended_full,
+        attended,
+        log_total,
+        residual,
+        second_normal,
+    ) = front(
+        token_rows,
+        first_pack,
+        second_pack,
+        where,
+        seqs,
+        out_width,
+        in_width,
+        ctx_size,
+        tp_size,
+        lax.axis_size("fsdp"),
+        1,
     )
 
-    all_rows = seqs * row_count
-
-    def over_tp(part, ident):
-        flat = part.astype(low).reshape(all_rows, model_width)
-        return line_sum(flat, tp_size, seqs, ident).reshape(part.shape).astype(jnp.float32)
-
-    residual = layer_inputs + over_tp(
-        dot("cr,dc->rd", attended, out_proj).reshape(layer_inputs.shape), 2
-    )
-
-    second_root = lax.rsqrt(jnp.mean(residual * residual, -1, keepdims=True) + norm_eps)
-    second_standard = residual * second_root
-    second_normal = (second_standard * gains[1]).astype(low)
-    gate = dot("mrd,dc->mrc", second_normal, pair_proj[:, :hidden])
-    up = dot("mrd,dc->mrc", second_normal, pair_proj[:, hidden:])
-    sigmoid = jax.nn.sigmoid(gate)
-    silu = gate * sigmoid
-    inner = (silu * up).astype(low)
     keep = (pos_here < lengths[:, None]).astype(jnp.float32)[..., None]
     grad_out = out_cotangent.reshape(seqs, row_count, model_width).astype(jnp.float32) * keep
-    grad_out_low = grad_out.astype(low)
-    grad_inner = dot("mrd,dc->mrc", grad_out_low, down_proj)
-    grad_gate = (grad_inner * up * sigmoid * (1.0 + gate * (1.0 - sigmoid))).astype(low)
-    grad_up = (grad_inner * silu).astype(low)
-    grad_pair = jnp.concatenate([grad_gate, grad_up], -1)
-    pair_flat = grad_pair.reshape(all_rows, 2 * hidden)
-    second_grads = grads_into(
-        None, 3 * hidden, 0, second_normal.reshape(all_rows, model_width), pair_flat, False, 256
-    )
-    second_grads = grads_into(
-        second_grads,
-        3 * hidden,
-        2 * hidden,
-        grad_out_low.reshape(all_rows, model_width),
-        inner.reshape(all_rows, hidden),
-        False,
-        256,
-    )
-    grad_pair, second_grads = lax.optimization_barrier((grad_pair, second_grads))
+    grad_out = grad_out.astype(low).reshape(all_rows, model_width)
+    inner, grad_gate, grad_up = hidden_units(second_normal, grad_out, second_whole)
+    second_grads = None
+    for at, (left, right) in enumerate(
+        ((second_normal, grad_gate), (second_normal, grad_up), (grad_out, inner))
+    ):
+        second_grads = grads_into(
+            second_grads, 3 * hidden, at * hidden, left, right, False, 256
+        )
+    inner, second_grads = lax.optimization_barrier((inner, second_grads))
     second_share = lax.psum_scatter(second_grads, shards, scatter_dimension=0, tiled=True)
-    normal_part = dot("mrc,dc->mrd", grad_pair, pair_proj).astype(low)
-    mixed_part = dot("mrc,dc->mrd", inner, down_proj).astype(low)
+    normal_part, mixed_part = leave(inner, grad_gate, grad_up, second_whole)
 
     back, grad_projected, second_gain = back_one(
-        normal_part.reshape(all_rows, model_width),
-        mixed_part.reshape(all_rows, model_width),
-        residual.reshape(all_rows, model_width),
-        grad_out_low.reshape(all_rows, model_width),
+        normal_part,
+        mixed_part,
+        residual,
+        grad_out,
         gains,
         first_whole,
         queries,
         key_values,
         attended_full,
-        log_total[:, :, None, :],
+        log_total,
         where,
         ctx_size,
         tp_size,
@@ -1020,7 +1324,7 @@
     grad_residual_low = back[:all_rows]
     mixed = back[all_rows:]
     first_grads = first_grads_of(
-        first_normal.reshape(all_rows, model_width), grad_projected, grad_residual_low, attended
+        first_normal, grad_projected, grad_residual_low, attended
     )
     grad_projected, first_grads, second_share = lax.optimization_barrier(
         (grad_projected, first_grads, second_share)
@@ -1029,9 +1333,10 @@
     input_grad, first_gain = back_two(
         grad_projected,
         first_whole,
-        tokens.reshape(all_rows, model_width),
+        token_rows,
         grad_residual_low,
         gains,
+        out_width,
         seqs,
         tp_size,
         5,

time: 765 us -> 733 us (0.958)
  Pallas kernels: 524 us -> 650 us
  matrix products: 93.1 us -> 0 us
  waiting for transfers between devices: 30.4 us -> 0.04 us
  other arithmetic: 73.8 us -> 47.5 us
  blocking collectives: 10.3 us -> 0 us
    pallas_call x3 -> x4, Pallas kernels: 261 us -> 385 us  [the longest x1 216 us: front(): pl.pallas_call(functools.partial(front_body, n, tp, fsdp, groups, out_wid...]
    dot_general x7 -> x0, matrix products: 93.1 us -> none  [dot(): return jnp.einsum(spec, left, right, preferred_element_type=jnp.float32)]
    all_gather x2 -> x0, waiting for transfers between devices: 30.3 us -> none  [the longest x1 30.3 us: on_device(): first_whole = lax.all_gather(first_pack, shards, axis=0, tiled=True)]
    all_gather x1 -> x0, blocking collectives: 10.3 us -> none  [on_device(): lax.all_gather(norm_gains.astype(low), shards, axis=1, tiled=True)]
    convert_element_type x4 -> x1, other arithmetic: 13 us -> 2.68 us  [on_device(): grad_out = grad_out.astype(low).reshape(all_rows, model_width)]
    pallas_call x2 -> x3, Pallas kernels: 33.7 us -> 39.4 us  [grads_into(): pl.pallas_call(functools.partial(grads_body, rows_last), grid=(n // tile,...]
  transfers between devices with their start and end apart: 4 -> 2, of which waited for: 1 -> 0; matrix products, arithmetic and copies ran while one was open for 16% -> 4% of each run, Pallas kernels for 65% -> 50%
where the time goes in v3:
time: 733 us; the launch traced here: 729 us
  Pallas kernels  650 us (89%)
  other arithmetic  47.5 us (6%)
  local copies, waits for them, and re-layouts  16.6 us (2%)
  between operations  14.6 us (2%)
    pallas_call x1, Pallas kernels, front(): pl.pallas_call(functools.partial(front_body, n, tp, fsdp, groups, out_wid...  216 us
    pallas_call x1, Pallas kernels, back_one(): pl.pallas_call(functools.partial(back_one_body, n, tp, groups), out_shape...  201 us
    pallas_call x1, Pallas kernels, back_two(): pl.pallas_call(functools.partial(back_two_body, tp, seqs, skip), out_shap...  109 us
    pallas_call x3, Pallas kernels, grads_into(): pl.pallas_call(functools.partial(grads_body, rows_last), grid=(n // tile,...  39.4 us
    pallas_call x1, Pallas kernels, leave(): pl.pallas_call(leave_body, grid=(width // tile,), out_shape=(jax.ShapeDty...  30.3 us
    pallas_call x1, Pallas kernels, hidden_units(): pl.pallas_call(hidden_body, grid=(steps,), out_shape=(jax.ShapeDtypeStruc...  29.1 us
    convert_element_type x4, other arithmetic, on_device(): results.append(updated[2].astype(low))  20.5 us
  transfers between devices with their start and end apart: 2, of which 0 were waited for; matrix products, arithmetic and copies ran while one was open for 4% of the time, Pallas kernels for 50%

profile of v3, /device:TPU:0, one launch (start us, length us, event | category | flops | bytes accessed | tf_op | source)
XLA Modules:
  0.0 729.2 jit_solution(17754384098581922331)
XLA Ops:
  7.2 0.0 copy-start.5
  7.2 0.0 reduce-scatter.3.cloned.1.call-start
  7.3 0.8 copy.55
  8.1 0.1 select_reduce_fusion
  8.3 0.1 dynamic-slice
  8.3 0.7 compare_convert_fusion
  9.1 0.6 broadcast_in_dim.47.query_pos_ref
  9.6 0.7 convert.27
  10.3 0.2 copy.49
  10.5 1.9 convert_bitcast_fusion.1
  12.4 2.3 convert.26
  14.7 0.1 convert_bitcast_fusion
  14.8 1.7 copy.50
  16.5 2.8 broadcast_add_fusion.key_pos_ref
  19.2 2.5 convert.28
  21.8 1.2 multiply_sine_fusion
  23.0 2.0 pad_maximum_fusion.second_ref
  24.9 1.4 copy-done.7
  26.3 2.7 fusion.grad_out_ref.left_ref
  29.0 2.0 concatenate.9.first_ref
  31.0 0.6 broadcast_in_dim.49.length_ref
  31.6 216.0 %front.1 = (bf16[2560,1664]{1,0:T(8,128)(2,1)}, bf16[2560,5376]{1,0:T(8,128)(2,1)}, bf16[768,2560]{1,0:T(8,128)(2,1)}, f32[8,2560]{1,0:T(8,128)}, bf16[3,640,256...) custom-call(bf16[768,2560]{1,0:T(8,128)(2,1)} %bitcast.41, ...), custom_call_target="tpu_custom_call" | custom-call | flops 1966080 | bytes 157286400 | tf_op jit(solution)/shard_map/front/pallas_call | solution.py:582
  247.6 29.1 %hidden_units.1 = (bf16[768,1792]{1,0:T(8,128)(2,1)}, bf16[768,1792]{1,0:T(8,128)(2,1)}, bf16[768,1792]{1,0:T(8,128)(2,1)}) custom-call(bf16[768,2560]{1,0:T(8,128)(2,1)} %get-tuple-element.47.normal_ref.left_ref, bf16[768,2560]{1,0:T(8,128)(2,1)} %fusion.grad_out_ref.left_ref, bf16[2560,5376]{1,0:T(8,128)(2,1)} %get-tuple-element.48.gate_ref.up_ref.down_ref.weight_ref, ...), custom_call_target="tpu_custom_call" | custom-call | flops 21139292160 | bytes 35782656 | tf_op jit(solution)/shard_map/hidden_units/pallas_call | solution.py:968
  276.7 1.8 copy-done
  278.5 13.3 %weight_grads.3.rest_0_ = bf16[2560,5376]{1,0:T(8,128)(2,1)} custom-call(bf16[768,2560]{1,0:T(8,128)(2,1)} %get-tuple-element.47.normal_ref.left_ref, bf16[768,1792]{1,0:T(8,128)(2,1)S(1)} %copy-done), custom_call_target="tpu_custom_call" | custom-call | flops 7046430720 | bytes 15859712 | tf_op jit(solution)/shard_map/weight_grads/pallas_call | solution.py:1058
  291.8 13.2 %weight_grads.4.rest_0_ = bf16[2560,5376]{1,0:T(8,128)(2,1)} custom-call(bf16[768,2560]{1,0:T(8,128)(2,1)} %get-tuple-element.47.normal_ref.left_ref, bf16[768,1792]{1,0:T(8,128)(2,1)S(1)} %copy-done.2, bf16[2560,5376]{1,0:T(8,128)(2,1)} %weight_grads.3.rest_0_), custom_call_target="tpu_custom_call", output_to_operand_aliasing={{}: (2, {})} | custom-call | flops 7046430720 | bytes 15859712 | tf_op jit(solution)/shard_map/weight_grads/pallas_call | solution.py:1058
  304.9 0.0 copy-done.1
  304.9 13.0 %weight_grads.5 = bf16[2560,5376]{1,0:T(8,128)(2,1)} custom-call(bf16[768,2560]{1,0:T(8,128)(2,1)} %fusion.grad_out_ref.left_ref, bf16[768,1792]{1,0:T(8,128)(2,1)S(1)} %copy-done.1, bf16[2560,5376]{1,0:T(8,128)(2,1)} %weight_grads.4.rest_0_), custom_call_target="tpu_custom_call", output_to_operand_aliasing={{}: (2, {})} | custom-call | flops 7046430720 | bytes 15859712 | tf_op jit(solution)/shard_map/weight_grads/pallas_call | solution.py:1058
  317.9 0.0 reduce-scatter.3.cloned.1.call-update
  317.9 0.0 reduce-scatter.5.cloned.1.call-start
  318.0 30.3 %leave.1 = (bf16[768,2560]{1,0:T(8,128)(2,1)}, bf16[768,2560]{1,0:T(8,128)(2,1)}) custom-call(bf16[768,1792]{1,0:T(8,128)(2,1)} %get-tuple-element.52.right_ref.inner_ref, bf16[768,1792]{1,0:T(8,128)(2,1)} %get-tuple-element.51.right_ref.grad_gate_ref, bf16[768,1792]{1,0:T(8,128)(2,1)} %get-tuple-element.50.right_ref.grad_up_ref, ...), custom_call_target="tpu_custom_call" | custom-call | flops 21139292160 | bytes 35782656 | tf_op jit(solution)/shard_map/leave/pallas_call | solution.py:1008
  348.3 200.6 %back_one.1 = (bf16[1536,2560]{1,0:T(8,128)(2,1)}, bf16[960,768]{1,0:T(8,128)(2,1)}, f32[8,2560]{1,0:T(8,128)}) custom-call(bf16[768,2560]{1,0:T(8,128)(2,1)} %get-tuple-element.53.normal_ref, bf16[768,2560]{1,0:T(8,128)(2,1)} %get-tuple-element.54.mixed_ref, f32[768,2560]{1,0:T(8,128)} %get-tuple-element.55.residual_ref, ...), custom_call_target="tpu_custom_call" | custom-call | flops 3932160 | bytes 314572800 | tf_op jit(solution)/shard_map/back_one/pallas_call | solution.py:837
  548.9 5.8 fusion.31
  554.7 0.0 copy-done.4
  554.7 14.0 %first_grads.1 = bf16[2560,1600]{1,0:T(8,128)(2,1)} custom-call(bf16[768,2560]{1,0:T(8,128)(2,1)} %get-tuple-element.64.normal_ref, bf16[960,768]{1,0:T(8,128)(2,1)S(1)} %copy-done.3, bf16[768,2560]{1,0:T(8,128)(2,1)} %get-tuple-element.157.residual_ref.residual_grad_ref, bf16[640,768]{1,0:T(8,128)(2,1)S(1)} %copy-done.4), custom_call_target="tpu_custom_call" | custom-call | flops 6291456000 | bytes 18513920 | tf_op jit(solution)/shard_map/first_grads/pallas_call | solution.py:1100
  568.7 0.0 reduce-scatter.5.cloned.1.call-update
  568.7 0.9 copy-done.16
  569.6 0.1 stack.10
  569.7 0.0 copy-start.18
  569.7 0.0 copy-start.19
  569.7 109.5 %back_two.1 = (bf16[768,2560]{1,0:T(8,128)(2,1)}, f32[8,2560]{1,0:T(8,128)}) custom-call(bf16[960,768]{1,0:T(8,128)(2,1)} %get-tuple-element.67.proj_ref, bf16[2560,1664]{1,0:T(8,128)(2,1)} %get-tuple-element.57.weight_ref, bf16[768,2560]{1,0:T(8,128)(2,1)} %bitcast.42, bf16[768,2560]{1,0:T(8,128)(2,1)} %get-tuple-element.157.residual_ref.residual_grad_ref, ...), custom_call_target="tpu_custom_call" | custom-call | flops 1966080 | bytes 157286400 | tf_op jit(solution)/shard_map/back_two/pallas_call | solution.py:929
  679.2 0.9 reduce_sum.28
  680.1 0.1 stack.9
  680.2 0.7 pad.4.x_ref
  680.9 11.6 %gain_sum.1 = f32[8,384]{1,0:T(8,128)} custom-call(f32[8,8,384]{2,1,0:T(8,128)} %pad.4.x_ref), custom_call_target="tpu_custom_call" | custom-call | tf_op jit(solution)/shard_map/gain_sum/pallas_call | solution.py:1177
  692.5 0.0 slice-start
  692.5 0.0 slice-start.2
  692.5 0.0 slice-start.4
  692.5 7.3 %convert.32 = f32[3,1,256,2560]{3,2,1,0:T(8,128)} convert(bf16[3,1,256,2560]{3,2,1,0:T(8,128)(2,1)} %bitcast.47) | non-fusion elementwise | flops 1966080 | bytes 11796480
  699.9 1.6 multiply_subtract_fusion.4
  701.5 7.2 fusion.19
  708.7 0.0 slice-done.1
  708.7 0.0 slice-done.3
  708.8 0.0 slice-done.5
  708.8 0.0 copy-done.8
  708.8 0.0 copy-start.9
  708.8 0.0 copy-start.15
  708.8 7.0 fusion.22
  715.9 0.0 copy-done.15
  715.9 0.0 copy-start.12
  715.9 0.0 copy-start.13
  715.9 3.4 fusion.25
  719.3 0.0 copy-done.6
  719.3 2.9 fusion.28
  (48 shorter events, 0.2 us)
Async XLA Ops:
  7.2 7.5 %copy-start.5 = (f32[1792,320]{0,1:T(8,128)S(1)}, f32[1792,320]{0,1:T(8,128)}, u32[]{:S(2)}) copy-start(f32[1792,320]{0,1:T(8,128)} %param.32) | copy-start | bytes 6881284
  7.2 561.5 %reduce-scatter.3.cloned.1.call-start = ((), (), s32[]{:S(2)}) async-start(), calls=%async_computation.2 | async-start | bytes 30965760 | tf_op jit(solution)/shard_map/reduce_scatter | solution.py:1305
  23.0 3.4 copy-start.7
  26.3 2.7 copy-start.10
  26.3 2.7 copy-start.11
  29.0 2.0 copy-start.20
  276.7 1.8 copy-start
  278.5 13.3 %copy-start.2 = (bf16[768,1792]{1,0:T(8,128)(2,1)S(1)}, bf16[768,1792]{1,0:T(8,128)(2,1)}, u32[]{:S(2)}) copy-start(bf16[768,1792]{1,0:T(8,128)(2,1)} %get-tuple-element.50.right_ref.grad_up_ref) | copy-start | bytes 8257540
  291.8 13.2 %copy-start.1 = (bf16[768,1792]{1,0:T(8,128)(2,1)S(1)}, bf16[768,1792]{1,0:T(8,128)(2,1)}, u32[]{:S(2)}) copy-start(bf16[768,1792]{1,0:T(8,128)(2,1)} %get-tuple-element.52.right_ref.inner_ref) | copy-start | bytes 8257540
  317.9 397.9 %reduce-scatter.5.cloned.1.call-start = ((), (), s32[]{:S(2)}) async-start(), calls=%async_computation.3 | async-start | bytes 9584640 | tf_op jit(solution)/shard_map/reduce_scatter | solution.py:1332
  548.9 5.8 copy-start.3
  548.9 5.8 copy-start.4
  568.7 0.9 copy-start.16
  569.7 130.2 %copy-start.17 = (f32[2,320]{1,0:T(2,128)S(1)}, f32[2,320]{1,0:T(2,128)}, u32[]{:S(2)}) copy-start(f32[2,320]{1,0:T(2,128)} %param.35) | copy-start | bytes 7684
  569.7 130.2 %copy-start.18 = (f32[2,320]{1,0:T(2,128)S(1)}, f32[2,320]{1,0:T(2,128)}, u32[]{:S(2)}) copy-start(f32[2,320]{1,0:T(2,128)} %param.37) | copy-start | bytes 7684
  569.7 130.2 %copy-start.19 = (f32[2,320]{1,0:T(2,128)S(1)}, f32[2,320]{1,0:T(2,128)}, u32[]{:S(2)}) copy-start(f32[2,320]{1,0:T(2,128)} %param.36) | copy-start | bytes 7684
  692.5 16.2 %slice-start = ((s8[4587520]{0:T(1024)(128)(4,1)}), s8[4194304]{0:T(1024)(128)(4,1)S(1)}, s32[]{:S(2)}) async-start(s8[4587520]{0:T(1024)(128)(4,1)} %bitcast.39), calls=%async_computation.4 | async-start | bytes 8388608
  692.5 16.2 %slice-start.2 = ((s8[4587520]{0:T(1024)(128)(4,1)}), s8[4194304]{0:T(1024)(128)(4,1)S(1)}, s32[]{:S(2)}) async-start(s8[4587520]{0:T(1024)(128)(4,1)} %bitcast.43), calls=%async_computation.6 | async-start | bytes 8388608
  692.5 16.2 %slice-start.4 = ((s8[4587520]{0:T(1024)(128)(4,1)}), s8[4194304]{0:T(1024)(128)(4,1)S(1)}, s32[]{:S(2)}) async-start(s8[4587520]{0:T(1024)(128)(4,1)} %bitcast.45), calls=%async_computation.8 | async-start | bytes 8388608
  701.5 7.3 slice-start.1
  701.5 7.3 slice-start.3
  701.5 7.3 slice-start.5
  701.5 7.3 %copy-start.8 = (bf16[320,5376]{1,0:T(8,128)(2,1)S(1)}, bf16[320,5376]{1,0:T(8,128)(2,1)}, u32[]{:S(2)}) copy-start(bf16[320,5376]{1,0:T(8,128)(2,1)} %reduce-scatter.3.cloned.1.call-done) | copy-start | bytes 10321924
  708.8 7.1 copy-start.9
  708.8 7.0 copy-start.15
  715.8 3.4 copy-start.6
  715.9 3.4 copy-start.12
  715.9 3.4 copy-start.13
  715.9 3.4 copy-start.14
Sparse Core Ops, SparseCore 0:
  318.1 178.4 reduce-scatter.2
  568.8 72.6 reduce-scatter.4

commit v4 on v3

--- a/solution.py
+++ b/solution.py
@@ -204,9 +204,20 @@
     return jnp.concatenate([first * cosine + second * sine, second * cosine - first * sine], 0)
 
 
-def mask_bias(key_position, query_position, length):
-    allowed = (key_position <= query_position) & (key_position < length)
-    return jnp.where(allowed, 0.0, neg_big)
+def fill_bias(bias, order_ref, length_ref, m, me, n):
+    rows = bias.shape[1]
+    span = rows // 2
+    lane = lax.broadcasted_iota(jnp.int32, (1, rows), 1)
+    query = jnp.where(
+        lane < span,
+        order_ref[m, 2 * me] * span + lane,
+        order_ref[m, 2 * me + 1] * span + lane - span,
+    )
+    within = lax.broadcasted_iota(jnp.int32, (span, rows), 0)
+    for block in range(2 * n):
+        key = order_ref[m, block] * span + within
+        allowed = (key <= query) & (key < length_ref[m])
+        bias[block * span : (block + 1) * span, :] = jnp.where(allowed, 0.0, neg_big)
 
 
 def cut(rows, parts):
@@ -224,7 +235,7 @@
         self.across = lax.rem(self.me + n // 2, n)
         self.other = self.me + 1 - 2 * lax.rem(self.me, 2)
         self.sems = sems
-        self.first = length // 32 * 16
+        self.first = max(16, min(length - 16, length * 6 // 160 * 16))
 
     def at(self, f, ctx, low=0, length=None):
         start = (f * self.n + ctx) * self.block_rows + self.low + low
@@ -284,17 +295,29 @@
         return pltpu.make_async_copy(self.own(), self.at(self.f, self.me), self.sems.at[2, 0])
 
     def start(self):
+        self.start_across()
+        self.start_ahead()
+
+    def start_across(self):
         self.to_across().start()
+
+    def start_ahead(self):
         for j in range(1, self.fsdp):
             self.to_ahead(j).start()
         self.to_other().start()
         self.local().start()
 
     def forward(self):
+        self.forward_across()
+        self.forward_behind()
+
+    def forward_across(self):
         self.to_across().wait_recv()
         for j in range(1, self.fsdp):
             self.across_to_ahead(j).start()
         self.across_to_other().start()
+
+    def forward_behind(self):
         for j in range(1, self.fsdp):
             self.to_ahead(j).wait_recv()
             self.behind_to_across(j).start()
@@ -330,27 +353,25 @@
     return pltpu.SemaphoreType.DMA((3, 5 * fsdp - 2))
 
 
-FIRST_PIECES = 2
-SECOND_PIECES = 4
-
-
 def front_body(
     n,
     tp,
     fsdp,
     groups,
-    out_width,
     token_ref,
-    first_ref,
-    second_ref,
+    in_ref,
+    tail_ref,
+    out_weight_ref,
+    gate_up_ref,
+    down_ref,
     cos_ref,
     sin_ref,
-    key_pos_ref,
-    query_pos_ref,
+    order_ref,
     length_ref,
-    first_whole,
-    second_whole,
-    normal_ref,
+    in_whole_ref,
+    out_whole_ref,
+    pair_whole_ref,
+    normal_out_ref,
     gain_ref,
     q_ref,
     kv_ref,
@@ -359,13 +380,23 @@
     log_ref,
     residual_ref,
     out_ref,
+    in_whole,
+    out_whole,
+    normal_ref,
+    in_pack,
+    out_pack,
+    pair_pack,
+    staged,
     proj,
     bias,
     parts,
+    load_sem,
+    save_sem,
     send_sem,
     recv_sem,
-    first_sems,
-    second_sems,
+    in_sems,
+    out_sems,
+    pair_sems,
     inbox,
     *sems,
 ):
@@ -382,7 +413,6 @@
         pl.semaphore_signal(
             barrier, inc=1, device_id={"fsdp": lax.rem(f + step, fsdp)}, device_id_type=MESH
         )
-    pl.semaphore_wait(barrier, peers + n - 1 + fsdp - 1)
 
     seqs, _, rows = q_ref.shape
     dim = HEAD_DIMENSION
@@ -392,30 +422,69 @@
     heads = groups * GROUP
     width = token_ref.shape[1]
     tile = 512 if width % 512 == 0 else width
-
-    def gathers(source, whole, pieces, sems):
-        block = source.shape[0]
+    block = in_ref.shape[0]
+    pair_width = gate_up_ref.shape[1]
+    whole_tiles = in_width // 128 * 128
+
+    ranges = cut(block, pair_sems.shape[0])
+
+    def loads(i):
+        low, length = ranges[i]
+        return [
+            pltpu.make_async_copy(
+                source.at[pl.ds(low, length)],
+                staged.at[i % 2, pl.ds(0, length), pl.ds(first, source.shape[1])],
+                load_sem.at[i % 2, at],
+            )
+            for at, (source, first) in enumerate(((gate_up_ref, 0), (down_ref, pair_width)))
+        ]
+
+    for load in loads(0):
+        load.start()
+    in_pack[:, :whole_tiles] = in_ref[:, :whole_tiles].astype(jnp.bfloat16)
+    in_pack[:, whole_tiles:] = tail_ref[...]
+    out_pack[...] = out_weight_ref[...].astype(jnp.bfloat16)
+    pl.semaphore_wait(barrier, peers + n - 1 + fsdp - 1)
+
+    def gathers(source, whole, sems):
         return [
             Gather(source, whole, low, length, block, fsdp, n, sems.at[i])
-            for i, (low, length) in enumerate(cut(block, pieces))
+            for i, (low, length) in enumerate(cut(block, sems.shape[0]))
         ]
 
-    first = gathers(first_ref, first_whole, FIRST_PIECES, first_sems)
-    second = gathers(second_ref, second_whole, SECOND_PIECES, second_sems)
+    first = gathers(in_pack, in_whole, in_sems)
+    outer = gathers(out_pack, out_whole, out_sems)
+    pair = gathers(pair_pack, pair_whole_ref, pair_sems)
     for piece in first:
         piece.start()
+    for i, (low, length) in enumerate(ranges):
+        if i + 1 < len(ranges):
+            for load in loads(i + 1):
+                load.start()
+        for load in loads(i):
+            load.wait()
+        pair_pack[low : low + length, :] = staged[i % 2, :length, :].astype(jnp.bfloat16)
     for piece in first:
         piece.forward()
+    for piece in outer:
+        piece.start()
     for piece in first:
         piece.corner()
-    second[0].start()
     for piece in first:
         piece.finish()
-
-    columns = out_width + in_width
-    base = columns // 128 * 128
-    turned = first_whole[:, base : base + 128].astype(jnp.float32).T
-    gain_ref[...] = turned[columns - base : columns - base + 8]
+    for piece in outer:
+        piece.forward()
+    for piece in pair:
+        piece.start_ahead()
+    saves = [
+        pltpu.make_async_copy(in_whole, in_whole_ref, save_sem.at[0]),
+        pltpu.make_async_copy(normal_ref, normal_out_ref, save_sem.at[1]),
+        pltpu.make_async_copy(out_whole, out_whole_ref, save_sem.at[2]),
+    ]
+    saves[0].start()
+
+    turned = in_whole[:, whole_tiles : whole_tiles + 128].astype(jnp.float32).T
+    gain_ref[...] = turned[in_width - whole_tiles : in_width - whole_tiles + 8]
 
     def columns_of(m):
         return pl.ds(pl.multiple_of(m * rows, 128), rows)
@@ -439,7 +508,7 @@
         normal_ref[rows_of(m), :] = (values * root * gain_ref[0:1, :]).astype(jnp.bfloat16)
         proj[m] = jnp.dot(
             normal_ref[rows_of(m), :],
-            first_whole[:, out_width : out_width + in_width],
+            in_whole[:, :in_width],
             preferred_element_type=jnp.float32,
         ).T
         for g in range(groups):
@@ -456,12 +525,13 @@
         return carry
 
     lax.fori_loop(0, seqs, project, 0)
-    for piece in second[1:]:
-        piece.start()
+    for piece in pair:
+        piece.start_across()
+    saves[1].start()
 
     def finish(segment, at, total):
         values = token_ref[at, :].astype(jnp.float32) + total
-        residual_ref[at, :] = values
+        residual_ref[at, :] = values.astype(jnp.bfloat16)
         root = lax.rsqrt(mean_of(values * values) + norm_eps)
         out_ref[at, :] = (values * root * gain_ref[1:2, :]).astype(jnp.bfloat16)
 
@@ -507,7 +577,7 @@
         log_ref[m, at] = top + jnp.log2(total)
 
     def ready(m):
-        bias[...] = mask_bias(key_pos_ref[m], query_pos_ref[m], length_ref[m])
+        fill_bias(bias, order_ref, length_ref, m, me, n)
         for step in range(1, n):
             copy(m, step).wait_recv()
 
@@ -516,7 +586,7 @@
         for low in range(0, width, tile):
             parts[rows_of(m), low : low + tile] = lax.dot_general(
                 left,
-                first_whole[low : low + tile, :out_width],
+                out_whole[low : low + tile, :],
                 (((1,), (1,)), ((), ())),
                 preferred_element_type=jnp.float32,
             ).astype(jnp.bfloat16)
@@ -539,26 +609,43 @@
 
     ready(0)
     lax.fori_loop(0, heads, opening, 0)
+    for piece in outer:
+        piece.corner()
+    for piece in outer:
+        piece.finish()
+    saves[2].start()
     product(0)
-    second[0].forward()
+    pair[0].forward_behind()
     lax.fori_loop(1, 2, sequence, 0)
-    second[1].forward()
+    for piece in pair[1:2]:
+        piece.forward_behind()
     lax.fori_loop(2, seqs, sequence, 0)
-    for piece in second[2:]:
-        piece.forward()
     at = (seqs - 1) * heads
-    line.run(at, at + 4)
-    for piece in second[:2]:
+    for piece in pair[2:3]:
+        piece.forward_behind()
+    pair[0].forward_across()
+    line.run(at, at + 2)
+    for piece in pair[3:]:
+        piece.forward_behind()
+    line.run(at + 2, at + 4)
+    for piece in pair[1:2]:
+        piece.forward_across()
+    line.run(at + 4, at + 10)
+    for piece in pair[2:3]:
+        piece.forward_across()
+    line.run(at + 10, at + 16)
+    for piece in pair[3:]:
+        piece.forward_across()
+    line.run(at + 16, line.ticks)
+    for piece in pair:
         piece.corner()
-    line.run(at + 4, at + 10)
-    for piece in second[2:]:
-        piece.corner()
-    line.run(at + 10, line.ticks)
-    for piece in second:
+    for piece in pair:
         piece.finish()
     line.drain()
-    for piece in first + second:
+    for piece in first + outer + pair:
         piece.drain()
+    for save in saves:
+        save.wait()
 
     def drain(m, carry):
         for step in range(1, n):
@@ -568,22 +655,34 @@
     lax.fori_loop(0, seqs, drain, 0)
 
 
-def front(tokens, first_pack, second_pack, where, seqs, out_width, in_width, n, tp, fsdp, ident):
+def front(
+    tokens, in_weight, tail, out_weight, gate_up, down, where, seqs, n, tp, fsdp, ident
+):
     all_rows, model_width = tokens.shape
     rows = all_rows // seqs
+    block, in_width = in_weight.shape
     groups = in_width // ((GROUP + 2) * HEAD_DIMENSION)
     heads = groups * GROUP
     shards = n * fsdp
     dim = HEAD_DIMENSION
+    padded = in_width // 128 * 128 + tail.shape[1]
+    out_width = out_weight.shape[1]
+    pair_width = gate_up.shape[1] + down.shape[1]
+    pieces = min(4, block // 32)
+    longest = max(length for _, length in cut(block, pieces))
     shape = jax.ShapeDtypeStruct
     low, wide = jnp.bfloat16, jnp.float32
     vmem = pl.BlockSpec(memory_space=VMEM)
     hbm = pl.BlockSpec(memory_space=pl.ANY)
+    smem = pl.BlockSpec(memory_space=pltpu.SMEM)
+    dma = pltpu.SemaphoreType.DMA
+    gather_sems = (3, 5 * fsdp - 2)
     return pl.pallas_call(
-        functools.partial(front_body, n, tp, fsdp, groups, out_width),
+        functools.partial(front_body, n, tp, fsdp, groups),
         out_shape=(
-            shape((shards * first_pack.shape[0], first_pack.shape[1]), low),
-            shape((shards * second_pack.shape[0], second_pack.shape[1]), low),
+            shape((shards * block, padded), low),
+            shape((shards * block, out_width), low),
+            shape((shards * block, pair_width), low),
             shape((all_rows, model_width), low),
             shape((8, model_width), wide),
             shape((seqs, heads * dim, rows), low),
@@ -591,19 +690,29 @@
             shape((seqs, heads * dim, rows), wide),
             shape((heads * dim, all_rows), low),
             shape((seqs, heads, 1, rows), wide),
-            shape((all_rows, model_width), wide),
+            shape((all_rows, model_width), low),
             shape((all_rows, model_width), low),
         ),
-        in_specs=[vmem, hbm, hbm] + [vmem] * 5,
-        out_specs=(vmem, hbm) + (vmem,) * 9,
+        in_specs=[vmem] * 4 + [hbm] * 2 + [vmem] * 2 + [smem] * 2,
+        out_specs=(hbm,) * 4 + (vmem,) * 8,
         scratch_shapes=[
+            VMEM((shards * block, padded), low),
+            VMEM((shards * block, out_width), low),
+            VMEM((all_rows, model_width), low),
+            VMEM((block, padded), low),
+            VMEM((block, out_width), low),
+            VMEM((block, pair_width), low),
+            VMEM((2, longest, pair_width), wide),
             VMEM((seqs, in_width, rows), wide),
             VMEM((n * rows, rows), wide),
             VMEM((all_rows, model_width), low),
-            pltpu.SemaphoreType.DMA((seqs, n - 1)),
-            pltpu.SemaphoreType.DMA((seqs, n - 1)),
-            pltpu.SemaphoreType.DMA((FIRST_PIECES, 3, 5 * fsdp - 2)),
-            pltpu.SemaphoreType.DMA((SECOND_PIECES, 3, 5 * fsdp - 2)),
+            dma((2, 2)),
+            dma((3,)),
+            dma((seqs, n - 1)),
+            dma((seqs, n - 1)),
+            dma((min(2, pieces),) + gather_sems),
+            dma((1,) + gather_sems),
+            dma((pieces,) + gather_sems),
         ]
         + line_scratch(all_rows, model_width, seqs, rows),
         compiler_params=pltpu.CompilerParams(
@@ -611,13 +720,14 @@
         ),
         cost_estimate=line_cost(all_rows, model_width),
         name="front",
-    )(tokens, first_pack, second_pack, *where)
+    )(tokens, in_weight, tail, out_weight, gate_up, down, *where)
 
 
 def back_one_body(
     n,
     tp,
     groups,
+    late,
     normal_ref,
     mixed_ref,
     residual_ref,
@@ -630,8 +740,7 @@
     log_ref,
     cos_ref,
     sin_ref,
-    key_pos_ref,
-    query_pos_ref,
+    order_ref,
     length_ref,
     out_ref,
     proj_ref,
@@ -655,7 +764,9 @@
     all_rows = seqs * rows
     loads = [
         pltpu.make_async_copy(normal_ref, parts.at[pl.ds(0, all_rows)], load_sem.at[0]),
-        pltpu.make_async_copy(mixed_ref, parts.at[pl.ds(all_rows, all_rows)], load_sem.at[1]),
+        pltpu.make_async_copy(
+            mixed_ref, parts.at[pl.ds(all_rows, late * rows)], load_sem.at[1]
+        ),
         pltpu.make_async_copy(
             weight_ref.at[:, pl.ds(0, out_proj.shape[1])], out_proj, load_sem.at[2]
         ),
@@ -680,15 +791,19 @@
     def finish(segment, at, total):
         @pl.when(segment < seqs)
         def _():
-            grad = norm_back(total, residual_ref[at, :], gain_ref[1:2, :], gain_sums)
+            grad = norm_back(
+                total, residual_ref[at, :].astype(jnp.float32), gain_ref[1:2, :], gain_sums
+            )
             out_ref[at, :] = (grad_out_ref[at, :].astype(jnp.float32) + grad).astype(jnp.bfloat16)
 
         @pl.when(segment >= seqs)
         def _():
-            start = pl.multiple_of(at.start - all_rows, CHUNK)
-            out_ref[at, :] = (residual_ref[pl.ds(start, CHUNK), :] + total).astype(jnp.bfloat16)
-
-    line = Line(tp, z, 2 * seqs, rows, parts, inbox, out_ref, sems, finish)
+            start = pl.multiple_of(at.start - late * rows, CHUNK)
+            out_ref[at, :] = (
+                residual_ref[pl.ds(start, CHUNK), :].astype(jnp.float32) + total
+            ).astype(jnp.bfloat16)
+
+    line = Line(tp, z, seqs + late, rows, parts, inbox, out_ref, sems, finish)
 
     def copy(m, step):
         to = lax.rem(me + step, n)
@@ -713,7 +828,7 @@
             )
             .T.astype(jnp.bfloat16)
         )
-        bias[...] = mask_bias(key_pos_ref[m], query_pos_ref[m], length_ref[m])
+        fill_bias(bias, order_ref, length_ref, m, me, n)
 
     def head(m, at):
         g = at // GROUP
@@ -818,7 +933,7 @@
     residual,
     grad_out,
     gains,
-    first_whole,
+    out_whole,
     queries,
     key_values,
     full,
@@ -831,20 +946,23 @@
     seqs, width, rows = queries.shape
     groups = key_values.shape[2]
     all_rows, model_width = normal_part.shape
+    late = mixed_part.shape[0] // rows
+    line_rows = all_rows + late * rows
     vmem = pl.BlockSpec(memory_space=VMEM)
     hbm = pl.BlockSpec(memory_space=pl.ANY)
+    smem = pl.BlockSpec(memory_space=pltpu.SMEM)
     shape = jax.ShapeDtypeStruct
     return pl.pallas_call(
-        functools.partial(back_one_body, n, tp, groups),
+        functools.partial(back_one_body, n, tp, groups, late),
         out_shape=(
-            shape((2 * all_rows, model_width), jnp.bfloat16),
+            shape((line_rows, model_width), jnp.bfloat16),
             shape((groups * (GROUP + 2) * HEAD_DIMENSION, all_rows), jnp.bfloat16),
             shape((8, model_width), jnp.float32),
         ),
-        in_specs=[hbm, hbm, vmem, vmem, vmem, hbm] + [vmem] * 9,
+        in_specs=[hbm, hbm, vmem, vmem, vmem, hbm] + [vmem] * 6 + [smem] * 2,
         out_specs=(vmem,) * 3,
         scratch_shapes=[
-            VMEM((2 * all_rows, model_width), jnp.bfloat16),
+            VMEM((line_rows, model_width), jnp.bfloat16),
             VMEM((model_width, width), jnp.bfloat16),
             VMEM((width, rows), jnp.bfloat16),
             VMEM((n, 2 * HEAD_DIMENSION, rows), jnp.float32),
@@ -855,11 +973,11 @@
             pltpu.SemaphoreType.DMA((seqs, n - 1)),
             pltpu.SemaphoreType.DMA((seqs, n - 1)),
         ]
-        + line_scratch(2 * all_rows, model_width, 2 * seqs, rows),
+        + line_scratch(line_rows, model_width, seqs + late, rows),
         compiler_params=pltpu.CompilerParams(
             collective_id=ident, has_side_effects=True, vmem_limit_bytes=60 * 2**20
         ),
-        cost_estimate=line_cost(2 * all_rows, model_width),
+        cost_estimate=line_cost(line_rows, model_width),
         name="back_one",
     )(
         normal_part,
@@ -867,7 +985,7 @@
         residual,
         grad_out,
         gains,
-        first_whole,
+        out_whole,
         queries,
         key_values,
         full,
@@ -985,92 +1103,184 @@
     )(normal, grad_out, whole, whole, whole)
 
 
-def leave_body(inner_ref, grad_gate_ref, grad_up_ref, weight_ref, normal_ref, mixed_ref):
-    units = inner_ref.shape[1]
-
-    def product(left, k):
-        return lax.dot_general(
-            left[...],
-            weight_ref[:, k * units : (k + 1) * units],
-            (((1,), (1,)), ((), ())),
+def mid_body(
+    tp,
+    seqs,
+    early,
+    normal_ref,
+    grad_out_ref,
+    inner_ref,
+    gate_ref,
+    up_ref,
+    residual_ref,
+    whole_ref,
+    grads_ref,
+    normal_part,
+    late_part,
+    out_ref,
+    residual,
+    turned,
+    staged,
+    weights,
+    parts,
+    load_sem,
+    weight_sem,
+    store_sem,
+    inbox,
+    *sems,
+):
+    z = lax.axis_index("tp")
+    load = pltpu.make_async_copy(
+        residual_ref.at[pl.ds(0, residual.shape[0])], residual, load_sem.at[0]
+    )
+    load.start()
+    rows, units = inner_ref.shape
+    width = normal_ref.shape[1]
+    tile = staged.shape[2]
+    pieces = width // tile
+    steps = units // tile
+    early_rows = parts.shape[0]
+    contract = (((1,), (1,)), ((), ()))
+
+    def fetch(at, first, columns):
+        slot = lax.rem(at, 2)
+        return pltpu.make_async_copy(
+            whole_ref.at[pl.ds(pl.multiple_of(at * tile, tile), tile), pl.ds(first, columns)],
+            weights.at[slot, :, pl.ds(0, columns)],
+            weight_sem.at[slot],
+        )
+
+    def columns_of(at):
+        return pl.ds(pl.multiple_of(at * tile, tile), tile)
+
+    fetch(0, 2 * units, units).start()
+    pl.semaphore_wait(pltpu.get_barrier_semaphore(), line_greet(tp, z))
+
+    def expand(at, carry):
+        @pl.when(at + 1 < pieces)
+        def _():
+            fetch(at + 1, 2 * units, units).start()
+
+        fetch(at, 2 * units, units).wait()
+        part = lax.dot_general(
+            inner_ref[...],
+            weights[lax.rem(at, 2), :, :units],
+            contract,
             preferred_element_type=jnp.float32,
+        ).astype(jnp.bfloat16)
+        parts[:, columns_of(at)] = part[:early_rows]
+        late_part[:, columns_of(at)] = part[early_rows:]
+        return carry
+
+    lax.fori_loop(0, pieces, expand, 0)
+    load.wait()
+    fetch(0, 0, 2 * units).start()
+    turned[...] = normal_ref[...].T
+
+    def finish(segment, at, total):
+        out_ref[at, :] = (residual[at, :].astype(jnp.float32) + total).astype(jnp.bfloat16)
+
+    line = Line(tp, z, early, rows // seqs, parts, inbox, out_ref, sems, finish)
+
+    def store(kind, at):
+        return pltpu.make_async_copy(
+            staged.at[lax.rem(kind * steps + at, 2)],
+            grads_ref.at[:, columns_of(kind * steps + at)],
+            store_sem.at[lax.rem(kind * steps + at, 2)],
         )
 
-    normal_ref[...] = (product(grad_gate_ref, 0) + product(grad_up_ref, 1)).astype(jnp.bfloat16)
-    mixed_ref[...] = product(inner_ref, 2).astype(jnp.bfloat16)
-
-
-def leave(inner, grad_gate, grad_up, whole, tile=256):
-    rows, units = inner.shape
-    width, columns = whole.shape
+    for kind, right in enumerate((gate_ref, up_ref, inner_ref)):
+        if kind == 2:
+            turned[...] = grad_out_ref[...].T
+
+        def gradient(at, carry):
+            line.tick(kind * steps + at)
+
+            @pl.when(kind * steps + at >= 2)
+            def _():
+                store(kind, at - 2).wait()
+
+            staged[lax.rem(kind * steps + at, 2)] = jnp.dot(
+                turned[...], right[:, columns_of(at)], preferred_element_type=jnp.float32
+            ).astype(jnp.bfloat16)
+            store(kind, at).start()
+            return carry
+
+        lax.fori_loop(0, steps, gradient, 0)
+
+    def leave(at, carry):
+        line.tick(3 * steps + at)
+
+        @pl.when(at + 1 < pieces)
+        def _():
+            fetch(at + 1, 0, 2 * units).start()
+
+        fetch(at, 0, 2 * units).wait()
+        slot = lax.rem(at, 2)
+        normal_part[:, columns_of(at)] = (
+            lax.dot_general(
+                gate_ref[...],
+                weights[slot, :, :units],
+                contract,
+                preferred_element_type=jnp.float32,
+            )
+            + lax.dot_general(
+                up_ref[...],
+                weights[slot, :, units:],
+                contract,
+                preferred_element_type=jnp.float32,
+            )
+        ).astype(jnp.bfloat16)
+        return carry
+
+    lax.fori_loop(0, pieces, leave, 0)
+    store(2, steps - 2).wait()
+    store(2, steps - 1).wait()
+    line.run(3 * steps + pieces, line.ticks)
+    line.drain()
+
+
+def mid(normal, grad_out, inner, grad_gate, grad_up, residual, whole, seqs, early, tp, ident):
+    all_rows, width = normal.shape
+    units = inner.shape[1]
+    columns = whole.shape[1]
+    rows = all_rows // seqs
+    tile = 256
     low = jnp.bfloat16
+    shape = jax.ShapeDtypeStruct
     vmem = pl.BlockSpec(memory_space=VMEM)
+    hbm = pl.BlockSpec(memory_space=pl.ANY)
     return pl.pallas_call(
-        leave_body,
-        grid=(width // tile,),
-        out_shape=(jax.ShapeDtypeStruct((rows, width), low),) * 2,
-        in_specs=[vmem] * 3 + [pl.BlockSpec((tile, columns), lambda i: (i, 0))],
-        out_specs=[pl.BlockSpec((rows, tile), lambda i: (0, i))] * 2,
-        compiler_params=pltpu.CompilerParams(vmem_limit_bytes=56 * 2**20),
+        functools.partial(mid_body, tp, seqs, early),
+        out_shape=(
+            shape((width, columns), low),
+            shape((all_rows, width), low),
+            shape(((seqs - early) * rows, width), low),
+            shape((early * rows, width), low),
+        ),
+        in_specs=[vmem] * 5 + [hbm] * 2,
+        out_specs=(hbm,) + (vmem,) * 3,
+        scratch_shapes=[
+            VMEM((early * rows, width), low),
+            VMEM((width, all_rows), low),
+            VMEM((2, width, tile), low),
+            VMEM((2, tile, 2 * units), low),
+            VMEM((early * rows, width), low),
+            pltpu.SemaphoreType.DMA((1,)),
+            pltpu.SemaphoreType.DMA((2,)),
+            pltpu.SemaphoreType.DMA((2,)),
+        ]
+        + line_scratch(early * rows, width, early, rows),
+        compiler_params=pltpu.CompilerParams(
+            collective_id=ident, has_side_effects=True, vmem_limit_bytes=60 * 2**20
+        ),
         cost_estimate=pl.CostEstimate(
-            flops=2 * rows * width * columns,
-            bytes_accessed=2 * (rows + width) * columns,
+            flops=4 * all_rows * width * columns,
+            bytes_accessed=40 * all_rows * width,
             transcendentals=0,
         ),
-        name="leave",
-    )(inner, grad_gate, grad_up, whole)
-
-
-def grads_body(rows_last, left_ref, right_ref, *rest):
-    out_ref, turned = rest[-2:]
-
-    @pl.when(pl.program_id(0) == 0)
-    def _():
-        turned[...] = left_ref[...].T
-
-    contract = (((1,), (1 if rows_last else 0,)), ((), ()))
-    width = turned.shape[0]
-    part = 512 if width % 512 == 0 else width
-    for low in range(0, width, part):
-        out_ref[low : low + part, :] = lax.dot_general(
-            turned[low : low + part, :],
-            right_ref[...],
-            contract,
-            preferred_element_type=jnp.float32,
-        ).astype(out_ref.dtype)
-
-
-def grads_into(buffer, columns, first, left, right, rows_last, tile):
-    rows, width = left.shape
-    n = right.shape[0] if rows_last else right.shape[1]
-    in_specs = [
-        pl.BlockSpec(memory_space=VMEM),
-        pl.BlockSpec((tile, rows), lambda i: (i, 0))
-        if rows_last
-        else pl.BlockSpec((rows, tile), lambda i: (0, i)),
-    ]
-    operands = [left, right]
-    aliases = {}
-    if buffer is not None:
-        in_specs.append(pl.BlockSpec(memory_space=pl.ANY))
-        operands.append(buffer)
-        aliases = {2: 0}
-    return pl.pallas_call(
-        functools.partial(grads_body, rows_last),
-        grid=(n // tile,),
-        out_shape=jax.ShapeDtypeStruct((width, columns), jnp.bfloat16),
-        in_specs=in_specs,
-        out_specs=pl.BlockSpec((width, tile), lambda i: (0, first // tile + i)),
-        scratch_shapes=[VMEM((width, rows), jnp.bfloat16)],
-        input_output_aliases=aliases,
-        compiler_params=pltpu.CompilerParams(vmem_limit_bytes=48 * 2**20),
-        cost_estimate=pl.CostEstimate(
-            flops=2 * rows * width * n,
-            bytes_accessed=2 * (rows * width + rows * n + width * n),
-            transcendentals=0,
-        ),
-        name="weight_grads",
-    )(*operands)
+        name="mid",
+    )(normal, grad_out, inner, grad_gate, grad_up, residual, whole)
 
 
 def first_grads_body(normal_ref, proj_ref, residual_ref, attended_ref, out_ref):
@@ -1080,7 +1290,7 @@
     contract = (((1,), (1,)), ((), ()))
     for low in range(0, width, tile):
         out_ref[low : low + tile, :split] = lax.dot_general(
-            residual_ref[:, low : low + tile].T,
+            residual_ref[: normal_ref.shape[0], low : low + tile].T,
             attended_ref[...],
             contract,
             preferred_element_type=jnp.float32,
@@ -1230,19 +1440,9 @@
     in_width = attention_input_weight.shape[1]
     shards = ("fsdp", "ctx")
 
-    own = attention_input_weight.shape[0]
-    used = out_width + in_width + 2
-    padded = -(-used // 128) * 128
-    first_pack = jnp.concatenate(
-        [
-            attend_out.T,
-            attention_input_weight,
-            norm_gains.T,
-            jnp.zeros((own, padded - used), jnp.float32),
-        ],
-        1,
-    ).astype(low)
-    second_pack = jnp.concatenate([gate_up, down_weight.T], 1).astype(low)
+    ahead = in_width // 128 * 128
+    tail = jnp.concatenate([attention_input_weight[:, ahead:], norm_gains.T], 1).astype(low)
+    tail = jnp.pad(tail, ((0, 0), (0, -tail.shape[1] % 128)))
 
     orders = span_order.reshape(seqs, 2 * ctx_size)
     lengths = seq_lengths.reshape(seqs)
@@ -1257,16 +1457,14 @@
     inverse = rope_base ** (-(jnp.arange(half_width, dtype=jnp.float32) * 2.0 / HEAD_DIMENSION))
     angles = pos_here.astype(jnp.float32)[:, None, :] * inverse[None, :, None]
     cosine, sine = jnp.cos(angles), jnp.sin(angles)
-    key_pos = pos_all[:, :, None]
-    query_pos = pos_here[:, None, :]
-    length_row = jnp.broadcast_to(lengths[:, None, None], query_pos.shape)
-    where = (cosine, sine, key_pos, query_pos, length_row)
+    where = (cosine, sine, orders, lengths)
 
     all_rows = seqs * row_count
     token_rows = tokens.reshape(all_rows, model_width)
     (
-        first_whole,
-        second_whole,
+        in_whole,
+        out_whole,
+        pair_whole,
         first_normal,
         gains,
         queries,
@@ -1278,12 +1476,13 @@
         second_normal,
     ) = front(
         token_rows,
-        first_pack,
-        second_pack,
+        attention_input_weight,
+        tail,
+        attend_out.T,
+        gate_up,
+        down_weight.T,
         where,
         seqs,
-        out_width,
-        in_width,
         ctx_size,
         tp_size,
         lax.axis_size("fsdp"),
@@ -1293,17 +1492,22 @@
     keep = (pos_here < lengths[:, None]).astype(jnp.float32)[..., None]
     grad_out = out_cotangent.reshape(seqs, row_count, model_width).astype(jnp.float32) * keep
     grad_out = grad_out.astype(low).reshape(all_rows, model_width)
-    inner, grad_gate, grad_up = hidden_units(second_normal, grad_out, second_whole)
-    second_grads = None
-    for at, (left, right) in enumerate(
-        ((second_normal, grad_gate), (second_normal, grad_up), (grad_out, inner))
-    ):
-        second_grads = grads_into(
-            second_grads, 3 * hidden, at * hidden, left, right, False, 256
-        )
-    inner, second_grads = lax.optimization_barrier((inner, second_grads))
+    inner, grad_gate, grad_up = hidden_units(second_normal, grad_out, pair_whole)
+    early = seqs - 1
+    second_grads, normal_part, mixed_part, mixed_early = mid(
+        second_normal,
+        grad_out,
+        inner,
+        grad_gate,
+        grad_up,
+        residual,
+        pair_whole,
+        seqs,
+        early,
+        tp_size,
+        2,
+    )
     second_share = lax.psum_scatter(second_grads, shards, scatter_dimension=0, tiled=True)
-    normal_part, mixed_part = leave(inner, grad_gate, grad_up, second_whole)
 
     back, grad_projected, second_gain = back_one(
         normal_part,
@@ -1311,7 +1515,7 @@
         residual,
         grad_out,
         gains,
-        first_whole,
+        out_whole,
         queries,
         key_values,
         attended_full,
@@ -1321,10 +1525,9 @@
         tp_size,
         4,
     )
-    grad_residual_low = back[:all_rows]
-    mixed = back[all_rows:]
+    mixed = jnp.concatenate([mixed_early, back[all_rows:]], 0)
     first_grads = first_grads_of(
-        first_normal, grad_projected, grad_residual_low, attended
+        first_normal, grad_projected, back, attended
     )
     grad_projected, first_grads, second_share = lax.optimization_barrier(
         (grad_projected, first_grads, second_share)
@@ -1332,11 +1535,11 @@
     first_share = lax.psum_scatter(first_grads, shards, scatter_dimension=0, tiled=True)
     input_grad, first_gain = back_two(
         grad_projected,
-        first_whole,
+        in_whole,
         token_rows,
-        grad_residual_low,
+        back,
         gains,
-        out_width,
+        0,
         seqs,
         tp_size,
         5,

time: 733 us -> 690 us (0.941)
  Pallas kernels: 650 us -> 606 us
  local copies, waits for them, and re-layouts: 16.6 us -> 5.57 us
  waiting for transfers between devices: 0.04 us -> 11 us
    pallas_call x6 -> x3, Pallas kernels: 486 us -> 440 us  [the longest x1 181 us: front(): pl.pallas_call(functools.partial(front_body, n, tp, fsdp, groups), out_sh...]
    reduce_scatter x1, waiting for transfers between devices: 0.01 us -> 11 us  [on_device(): lax.psum_scatter(second_grads, shards, scatter_dimension=0, tiled=True)]
  transfers between devices with their start and end apart: 2 -> 2, of which waited for: 0 -> 1; matrix products, arithmetic and copies ran while one was open for 4% -> 4% of each run, Pallas kernels for 50% -> 43%
where the time goes in v4:
time: 690 us; the launch traced here: 681 us
  Pallas kernels  606 us (88%)
  other arithmetic  43.3 us (6%)
  between operations  14.8 us (2%)
  waiting for transfers between devices  11 us (2%)
    pallas_call x1, Pallas kernels, front(): pl.pallas_call(functools.partial(front_body, n, tp, fsdp, groups), out_sh...  181 us
    pallas_call x1, Pallas kernels, back_one(): pl.pallas_call(functools.partial(back_one_body, n, tp, groups, late), out...  157 us
    pallas_call x1, Pallas kernels, back_two(): pl.pallas_call(functools.partial(back_two_body, tp, seqs, skip), out_shap...  110 us
    pallas_call x1, Pallas kernels, mid(): pl.pallas_call(functools.partial(mid_body, tp, seqs, early), out_shape=(s...  102 us
    pallas_call x1, Pallas kernels, hidden_units(): pl.pallas_call(hidden_body, grid=(steps,), out_shape=(jax.ShapeDtypeStruc...  29.2 us
    convert_element_type x4, other arithmetic, on_device(): results.append(updated[2].astype(low))  20.7 us
    pallas_call x1, Pallas kernels, first_grads_of(): pl.pallas_call(first_grads_body, out_shape=jax.ShapeDtypeStruct((width, c...  14.8 us
  transfers between devices with their start and end apart: 2, of which 1 were waited for; matrix products, arithmetic and copies ran while one was open for 4% of the time, Pallas kernels for 43%

profile of v4, /device:TPU:0, one launch (start us, length us, event | category | flops | bytes accessed | tf_op | source)
XLA Modules:
  0.0 681.0 jit_solution(11905833840859364413)
XLA Ops:
  7.2 0.0 reduce-scatter.3.cloned.1.call-start
  7.3 0.7 convert.14
  8.0 0.7 copy.48
  8.7 0.1 dynamic-slice
  8.7 0.1 select_reduce_fusion
  8.9 0.7 compare_convert_fusion
  9.6 0.2 copy.43
  9.8 0.9 slice.43
  10.7 0.7 fusion.11.tail_ref
  11.4 1.2 multiply_sine_fusion
  12.6 4.7 fusion.grad_out_ref
  17.4 0.0 copy-done.9
  17.4 181.3 %front.1 = (bf16[2560,1024]{1,0:T(8,128)(2,1)}, bf16[2560,640]{1,0:T(8,128)(2,1)}, bf16[2560,5376]{1,0:T(8,128)(2,1)}, bf16[768,2560]{1,0:T(8,128)(2,1)}, f32[8,...) custom-call(bf16[768,2560]{1,0:T(8,128)(2,1)} %bitcast.37, ...), custom_call_target="tpu_custom_call" | custom-call | flops 1966080 | bytes 157286400 | tf_op jit(solution)/shard_map/front/pallas_call | solution.py:680
  198.7 29.2 %hidden_units.1 = (bf16[768,1792]{1,0:T(8,128)(2,1)}, bf16[768,1792]{1,0:T(8,128)(2,1)}, bf16[768,1792]{1,0:T(8,128)(2,1)}) custom-call(bf16[768,2560]{1,0:T(8,128)(2,1)} %get-tuple-element.48.normal_ref, bf16[768,2560]{1,0:T(8,128)(2,1)} %fusion.grad_out_ref, bf16[2560,5376]{1,0:T(8,128)(2,1)} %get-tuple-element.49.gate_ref.up_ref.down_ref.whole_ref, ...), custom_call_target="tpu_custom_call" | custom-call | flops 21139292160 | bytes 35782656 | tf_op jit(solution)/shard_map/hidden_units/pallas_call | solution.py:1086
  227.9 102.1 %mid.1 = (bf16[2560,5376]{1,0:T(8,128)(2,1)}, bf16[768,2560]{1,0:T(8,128)(2,1)}, bf16[256,2560]{1,0:T(8,128)(2,1)}, bf16[512,2560]{1,0:T(8,128)(2,1)}) custom-call(bf16[768,2560]{1,0:T(8,128)(2,1)} %get-tuple-element.48.normal_ref, bf16[768,2560]{1,0:T(8,128)(2,1)} %fusion.grad_out_ref, bf16[768,1792]{1,0:T(8,128)(2,1)} %get-tuple-element.50.inner_ref, ...), custom_call_target="tpu_custom_call" | custom-call | flops 42278584320 | bytes 78643200 | tf_op jit(solution)/shard_map/mid/pallas_call | solution.py:1253
  330.0 0.0 reduce-scatter.3.cloned.1.call-update
  330.0 0.0 reduce-scatter.5.cloned.1.call-start
  330.1 0.0 copy-start.1
  330.1 156.9 %back_one.1 = (bf16[1024,2560]{1,0:T(8,128)(2,1)}, bf16[960,768]{1,0:T(8,128)(2,1)}, f32[8,2560]{1,0:T(8,128)}) custom-call(bf16[768,2560]{1,0:T(8,128)(2,1)} %get-tuple-element.55.normal_ref, bf16[256,2560]{1,0:T(8,128)(2,1)} %get-tuple-element.56.mixed_ref, bf16[768,2560]{1,0:T(8,128)(2,1)} %get-tuple-element.53.residual_ref, ...), custom_call_target="tpu_custom_call" | custom-call | flops 2621440 | bytes 209715200 | tf_op jit(solution)/shard_map/back_one/pallas_call | solution.py:955
  487.0 0.0 copy-done.1
  487.0 0.0 copy-start
  487.0 1.4 copy-done
  488.4 14.8 %first_grads.1 = bf16[2560,1600]{1,0:T(8,128)(2,1)} custom-call(bf16[768,2560]{1,0:T(8,128)(2,1)} %get-tuple-element.65.normal_ref, bf16[960,768]{1,0:T(8,128)(2,1)S(1)} %copy-done, bf16[1024,2560]{1,0:T(8,128)(2,1)} %get-tuple-element.63.residual_ref.residual_grad_ref, bf16[640,768]{1,0:T(8,128)(2,1)S(1)} %copy-done.1), custom_call_target="tpu_custom_call" | custom-call | flops 6291456000 | bytes 18513920 | tf_op jit(solution)/shard_map/first_grads/pallas_call | solution.py:1310
  503.2 11.0 %reduce-scatter.3.cloned.1.call-done = bf16[320,5376]{1,0:T(8,128)(2,1)} async-done(((bf16[2560,5376]{1,0:T(8,128)(2,1)}), bf16[320,5376]{1,0:T(8,128)(2,1)}) %reduce-scatter.3.cloned.1.call-update) | async-done | bytes 3440656 | tf_op jit(solution)/shard_map/reduce_scatter | solution.py:1510
  514.2 0.0 reduce-scatter.5.cloned.1.call-update
  514.2 0.0 copy-start.8
  514.2 1.4 slice.23
  515.6 0.0 copy-done.8
  515.7 0.1 stack.10
  515.8 3.9 pad_maximum_fusion
  519.7 110.3 %back_two.1 = (bf16[768,2560]{1,0:T(8,128)(2,1)}, f32[8,2560]{1,0:T(8,128)}) custom-call(bf16[960,768]{1,0:T(8,128)(2,1)} %get-tuple-element.68.proj_ref, bf16[2560,1024]{1,0:T(8,128)(2,1)} %get-tuple-element.69.weight_ref, bf16[768,2560]{1,0:T(8,128)(2,1)} %bitcast.38, bf16[1024,2560]{1,0:T(8,128)(2,1)} %get-tuple-element.63.residual_ref.residual_grad_ref, ...), custom_call_target="tpu_custom_call" | custom-call | flops 1966080 | bytes 157286400 | tf_op jit(solution)/shard_map/back_two/pallas_call | solution.py:1047
  630.0 0.0 copy-start.4
  630.0 1.1 reduce_sum.28
  631.1 0.1 stack.9
  631.2 0.7 pad.9.x_ref
  631.9 11.5 %gain_sum.1 = f32[8,384]{1,0:T(8,128)} custom-call(f32[8,8,384]{2,1,0:T(8,128)} %pad.9.x_ref), custom_call_target="tpu_custom_call" | custom-call | tf_op jit(solution)/shard_map/gain_sum/pallas_call | solution.py:1387
  643.4 0.0 copy-start.2
  643.4 0.0 slice-start
  643.4 0.0 slice-start.2
  643.5 0.0 slice-start.4
  643.5 7.3 %convert.17 = f32[3,1,256,2560]{3,2,1,0:T(8,128)} convert(bf16[3,1,256,2560]{3,2,1,0:T(8,128)(2,1)} %bitcast.45) | non-fusion elementwise | flops 1966080 | bytes 11796480
  650.8 0.0 copy-done.10
  650.8 0.0 copy-done.11
  650.8 0.0 copy-done.12
  650.8 2.1 multiply_subtract_fusion.4
  652.9 0.0 copy-done.4
  652.9 0.0 copy-done.2
  652.9 0.0 slice-start.3
  652.9 0.0 slice-start.5
  652.9 6.9 %fusion.23 = (bf16[1792,320]{0,1:T(8,128)(2,1)}, f32[1792,320]{0,1:T(8,128)}, f32[1792,320]{0,1:T(8,128)}, f32[1792,320]{0,1:T(8,128)}) fusion(f32[1792,320]{0,1:T(8,128)S(1)} %copy-done.2, bf16[320,5376]{1,0:T(8,128)(2,1)S(1)} %copy-done.4, f32[1792,320]{0,1:T(8,128)} %param.34, f32[1792,320]{0,1:T(8,128)} %param.33), kind=kLoop, calls=%fused_computation.54 | loop fusion | flops 9748480 | bytes 16056320 | tf_op jit(solution)/shard_map/convert_element_type | solution.py:1589
  659.8 0.0 slice-done
  659.8 0.0 slice-done.2
  659.8 0.0 slice-done.4
  659.8 0.0 slice-done.1
  659.8 0.0 slice-done.3
  659.8 0.0 slice-done.5
  659.9 7.1 %fusion.26 = (bf16[320,3584]{1,0:T(8,128)(2,1)}, f32[320,3584]{1,0:T(8,128)}, f32[320,3584]{1,0:T(8,128)}, f32[320,3584]{1,0:T(8,128)}) fusion(f32[320,3584]{1,0:T(8,128)S(1)} %bitcast.36, bf16[320,5376]{1,0:T(8,128)(2,1)S(1)} %copy-done.4, f32[320,3584]{1,0:T(8,128)S(1)} %bitcast.41, f32[320,3584]{1,0:T(8,128)S(1)} %bitcast.43), kind=kLoop, calls=%fused_computation.55 | loop fusion | flops 19496960 | bytes 32112640 | tf_op jit(solution)/shard_map/convert_element_type | solution.py:1589
  666.9 0.0 reduce-scatter.5.cloned.1.call-done
  666.9 0.0 copy-start.6
  667.0 0.0 copy-start.7
  667.0 3.9 fusion.29
  670.9 0.0 copy-done.3
  670.9 0.0 copy-done.5
  670.9 2.8 fusion.32
  (20 shorter events, 0.1 us)
Async XLA Ops:
  7.2 507.0 %reduce-scatter.3.cloned.1.call-start = ((), (), s32[]{:S(2)}) async-start(), calls=%async_computation.2 | async-start | bytes 30965760 | tf_op jit(solution)/shard_map/reduce_scatter | solution.py:1510
  8.7 8.7 %copy-start.9 = (s32[3,1,8]{2,0,1:T(4,128)}, s32[3,1,8]{2,0,1:T(4,128)S(1)}, u32[]{:S(2)}) copy-start(s32[3,1,8]{2,0,1:T(4,128)S(1)} %copy.48) | copy-start | bytes 292
  330.0 336.9 %reduce-scatter.5.cloned.1.call-start = ((), (), s32[]{:S(2)}) async-start(), calls=%async_computation.3 | async-start | bytes 9584640 | tf_op jit(solution)/shard_map/reduce_scatter | solution.py:1535
  330.1 156.9 %copy-start.1 = (bf16[640,768]{1,0:T(8,128)(2,1)S(1)}, bf16[640,768]{1,0:T(8,128)(2,1)}, u32[]{:S(2)}) copy-start(bf16[640,768]{1,0:T(8,128)(2,1)} %get-tuple-element.66.attended_ref) | copy-start | bytes 2949124
  487.0 1.4 copy-start
  514.2 1.4 copy-start.8
  519.7 131.1 %copy-start.10 = (f32[2,320]{1,0:T(2,128)S(1)}, f32[2,320]{1,0:T(2,128)}, u32[]{:S(2)}) copy-start(f32[2,320]{1,0:T(2,128)} %param.35) | copy-start | bytes 7684
  519.7 131.1 %copy-start.11 = (f32[2,320]{1,0:T(2,128)S(1)}, f32[2,320]{1,0:T(2,128)}, u32[]{:S(2)}) copy-start(f32[2,320]{1,0:T(2,128)} %param.37) | copy-start | bytes 7684
  519.7 131.1 %copy-start.12 = (f32[2,320]{1,0:T(2,128)S(1)}, f32[2,320]{1,0:T(2,128)}, u32[]{:S(2)}) copy-start(f32[2,320]{1,0:T(2,128)} %param.36) | copy-start | bytes 7684
  630.0 22.9 %copy-start.4 = (bf16[320,5376]{1,0:T(8,128)(2,1)S(1)}, bf16[320,5376]{1,0:T(8,128)(2,1)}, u32[]{:S(2)}) copy-start(bf16[320,5376]{1,0:T(8,128)(2,1)} %reduce-scatter.3.cloned.1.call-done) | copy-start | bytes 10321924
  643.4 9.5 %copy-start.2 = (f32[1792,320]{0,1:T(8,128)S(1)}, f32[1792,320]{0,1:T(8,128)}, u32[]{:S(2)}) copy-start(f32[1792,320]{0,1:T(8,128)} %param.32) | copy-start | bytes 6881284
  643.4 16.4 %slice-start = ((s8[4587520]{0:T(1024)(128)(4,1)}), s8[4194304]{0:T(1024)(128)(4,1)S(1)}, s32[]{:S(2)}) async-start(s8[4587520]{0:T(1024)(128)(4,1)} %bitcast.35), calls=%async_computation.4 | async-start | bytes 8388608
  643.4 16.4 %slice-start.2 = ((s8[4587520]{0:T(1024)(128)(4,1)}), s8[4194304]{0:T(1024)(128)(4,1)S(1)}, s32[]{:S(2)}) async-start(s8[4587520]{0:T(1024)(128)(4,1)} %bitcast.40), calls=%async_computation.6 | async-start | bytes 8388608
  643.5 16.4 %slice-start.4 = ((s8[4587520]{0:T(1024)(128)(4,1)}), s8[4194304]{0:T(1024)(128)(4,1)S(1)}, s32[]{:S(2)}) async-start(s8[4587520]{0:T(1024)(128)(4,1)} %bitcast.42), calls=%async_computation.8 | async-start | bytes 8388608
  652.9 6.9 %slice-start.1 = ((s8[4587520]{0:T(1024)(128)(4,1)}), s8[393216]{0:T(1024)(128)(4,1)S(1)}, s32[]{:S(2)}) async-start(s8[4587520]{0:T(1024)(128)(4,1)} %bitcast.35), calls=%async_computation.5 | async-start | bytes 786432
  652.9 6.9 %slice-start.3 = ((s8[4587520]{0:T(1024)(128)(4,1)}), s8[393216]{0:T(1024)(128)(4,1)S(1)}, s32[]{:S(2)}) async-start(s8[4587520]{0:T(1024)(128)(4,1)} %bitcast.40), calls=%async_computation.7 | async-start | bytes 786432
  652.9 6.9 %slice-start.5 = ((s8[4587520]{0:T(1024)(128)(4,1)}), s8[393216]{0:T(1024)(128)(4,1)S(1)}, s32[]{:S(2)}) async-start(s8[4587520]{0:T(1024)(128)(4,1)} %bitcast.42), calls=%async_computation.9 | async-start | bytes 786432
  666.9 3.9 copy-start.3
  666.9 3.9 copy-start.5
  666.9 3.9 copy-start.6
  667.0 3.9 copy-start.7
Sparse Core Ops, SparseCore 0:
  330.2 183.9 reduce-scatter.2
  517.7 69.8 reduce-scatter.4

commit v5 on v4

--- a/solution.py
+++ b/solution.py
@@ -366,12 +366,14 @@
     down_ref,
     cos_ref,
     sin_ref,
+    cotangent_ref,
     order_ref,
     length_ref,
     in_whole_ref,
     out_whole_ref,
     pair_whole_ref,
     normal_out_ref,
+    grad_out_ref,
     gain_ref,
     q_ref,
     kv_ref,
@@ -441,6 +443,9 @@
 
     for load in loads(0):
         load.start()
+    cotangent = pltpu.make_async_copy(cotangent_ref, parts, load_sem.at[2, 0])
+    grad_out = pltpu.make_async_copy(parts, grad_out_ref, load_sem.at[2, 1])
+    cotangent.start()
     in_pack[:, :whole_tiles] = in_ref[:, :whole_tiles].astype(jnp.bfloat16)
     in_pack[:, whole_tiles:] = tail_ref[...]
     out_pack[...] = out_weight_ref[...].astype(jnp.bfloat16)
@@ -464,6 +469,23 @@
         for load in loads(i):
             load.wait()
         pair_pack[low : low + length, :] = staged[i % 2, :length, :].astype(jnp.bfloat16)
+
+    cotangent.wait()
+    span = rows // 2
+
+    def keep(at, carry):
+        own = pl.ds(pl.multiple_of(at * span, CHUNK), span)
+        m = at // 2
+        position = order_ref[m, 2 * me + lax.rem(at, 2)] * span + lax.broadcasted_iota(
+            jnp.int32, (span, width), 0
+        )
+        parts[own, :] = jnp.where(
+            position < length_ref[m], parts[own, :].astype(jnp.float32), 0.0
+        ).astype(jnp.bfloat16)
+        return carry
+
+    lax.fori_loop(0, 2 * seqs, keep, 0)
+    grad_out.start()
     for piece in first:
         piece.forward()
     for piece in outer:
@@ -609,6 +631,7 @@
 
     ready(0)
     lax.fori_loop(0, heads, opening, 0)
+    grad_out.wait()
     for piece in outer:
         piece.corner()
     for piece in outer:
@@ -656,9 +679,10 @@
 
 
 def front(
-    tokens, in_weight, tail, out_weight, gate_up, down, where, seqs, n, tp, fsdp, ident
+    tokens, cotangent, in_weight, tail, out_weight, gate_up, down, where, seqs, n, tp, fsdp, ident
 ):
     all_rows, model_width = tokens.shape
+    cosine, sine, orders, lengths = where
     rows = all_rows // seqs
     block, in_width = in_weight.shape
     groups = in_width // ((GROUP + 2) * HEAD_DIMENSION)
@@ -684,6 +708,7 @@
             shape((shards * block, out_width), low),
             shape((shards * block, pair_width), low),
             shape((all_rows, model_width), low),
+            shape((all_rows, model_width), low),
             shape((8, model_width), wide),
             shape((seqs, heads * dim, rows), low),
             shape((seqs, n, groups, 2 * dim, rows), low),
@@ -693,8 +718,8 @@
             shape((all_rows, model_width), low),
             shape((all_rows, model_width), low),
         ),
-        in_specs=[vmem] * 4 + [hbm] * 2 + [vmem] * 2 + [smem] * 2,
-        out_specs=(hbm,) * 4 + (vmem,) * 8,
+        in_specs=[vmem] * 4 + [hbm] * 2 + [vmem] * 2 + [hbm] + [smem] * 2,
+        out_specs=(hbm,) * 5 + (vmem,) * 8,
         scratch_shapes=[
             VMEM((shards * block, padded), low),
             VMEM((shards * block, out_width), low),
@@ -706,7 +731,7 @@
             VMEM((seqs, in_width, rows), wide),
             VMEM((n * rows, rows), wide),
             VMEM((all_rows, model_width), low),
-            dma((2, 2)),
+            dma((3, 2)),
             dma((3,)),
             dma((seqs, n - 1)),
             dma((seqs, n - 1)),
@@ -720,7 +745,7 @@
         ),
         cost_estimate=line_cost(all_rows, model_width),
         name="front",
-    )(tokens, in_weight, tail, out_weight, gate_up, down, *where)
+    )(tokens, in_weight, tail, out_weight, gate_up, down, cosine, sine, cotangent, orders, lengths)
 
 
 def back_one_body(
@@ -728,31 +753,45 @@
     tp,
     groups,
     late,
-    normal_ref,
-    mixed_ref,
+    gate_ref,
+    up_ref,
+    pair_ref,
+    gain_ref,
+    log_ref,
+    cos_ref,
+    sin_ref,
+    inner_from,
+    residual_from,
+    grad_out_from,
+    weight_from,
+    q_from,
+    kv_from,
+    full_from,
+    early_from,
+    order_ref,
+    length_ref,
+    grad_to,
+    mixed_to,
+    proj_ref,
+    gain_sums,
+    out_ref,
+    parts,
+    weights,
+    inner_ref,
     residual_ref,
     grad_out_ref,
-    gain_ref,
-    weight_ref,
+    out_proj,
     q_ref,
     kv_ref,
     full_ref,
-    log_ref,
-    cos_ref,
-    sin_ref,
-    order_ref,
-    length_ref,
-    out_ref,
-    proj_ref,
-    gain_sums,
-    parts,
-    out_proj,
     grads,
     sums,
     bias,
     outbox,
     kv_inbox,
     load_sem,
+    save_sem,
+    weight_sem,
     send_sem,
     recv_sem,
     inbox,
@@ -762,17 +801,58 @@
     me = lax.axis_index("ctx")
     seqs, _, rows = q_ref.shape
     all_rows = seqs * rows
+    units = inner_ref.shape[1]
+    tile = weights.shape[1]
+    pieces = out_ref.shape[1] // tile
     loads = [
-        pltpu.make_async_copy(normal_ref, parts.at[pl.ds(0, all_rows)], load_sem.at[0]),
+        pltpu.make_async_copy(source, target, load_sem.at[at])
+        for at, (source, target) in enumerate(
+            (
+                (residual_from, residual_ref),
+                (grad_out_from, grad_out_ref),
+                (inner_from, inner_ref),
+                (weight_from, out_proj),
+                (q_from, q_ref),
+                (kv_from, kv_ref),
+                (full_from, full_ref),
+            )
+        )
+    ]
+
+    early_rows = all_rows - late * rows
+    saves = [
+        pltpu.make_async_copy(early_from, mixed_to.at[pl.ds(0, early_rows)], save_sem.at[0]),
+        pltpu.make_async_copy(out_ref.at[pl.ds(0, all_rows)], grad_to, save_sem.at[1]),
         pltpu.make_async_copy(
-            mixed_ref, parts.at[pl.ds(all_rows, late * rows)], load_sem.at[1]
-        ),
-        pltpu.make_async_copy(
-            weight_ref.at[:, pl.ds(0, out_proj.shape[1])], out_proj, load_sem.at[2]
+            out_ref.at[pl.ds(all_rows, late * rows)],
+            mixed_to.at[pl.ds(early_rows, late * rows)],
+            save_sem.at[2],
         ),
     ]
+
+    def tile_of(at):
+        return pl.ds(pl.multiple_of(at * tile, tile), tile)
+
+    def fetch(at):
+        slot = lax.rem(at, 2)
+        return pltpu.make_async_copy(
+            pair_ref.at[tile_of(lax.rem(at, pieces)), pl.ds(0, 2 * units)],
+            weights.at[slot],
+            weight_sem.at[slot],
+        )
+
+    def fetch_down(at):
+        slot = lax.rem(at, 2)
+        return pltpu.make_async_copy(
+            pair_ref.at[tile_of(at), pl.ds(2 * units, units)],
+            weights.at[slot, :, pl.ds(0, units)],
+            weight_sem.at[slot],
+        )
+
+    fetch(0).start()
     for load in loads:
         load.start()
+    saves[0].start()
     peers = line_greet(tp, z)
     barrier = pltpu.get_barrier_semaphore()
     for step in range(1, n):
@@ -896,13 +976,82 @@
         for step in range(1, n):
             copy(m, step).wait_send()
 
-    loads[0].wait()
-    line.run(0, line.ready(1))
-    loads[1].wait()
-    loads[2].wait()
+    contract = (((1,), (1,)), ((), ()))
+
+    def leave(m, tile_at):
+        at = m * pieces + tile_at
+        own = pl.ds(pl.multiple_of(m * rows, CHUNK), rows)
+        slot = lax.rem(at, 2)
+
+        @pl.when(at + 1 < seqs * pieces)
+        def _():
+            fetch(at + 1).start()
+
+        fetch(at).wait()
+        parts[own, tile_of(tile_at)] = (
+            lax.dot_general(
+                gate_ref[own, :],
+                weights[slot, :, :units],
+                contract,
+                preferred_element_type=jnp.float32,
+            )
+            + lax.dot_general(
+                up_ref[own, :],
+                weights[slot, :, units:],
+                contract,
+                preferred_element_type=jnp.float32,
+            )
+        ).astype(jnp.bfloat16)
+
+    def first_leave(tile_at, carry):
+        leave(0, tile_at)
+        return carry
+
+    lax.fori_loop(0, pieces, first_leave, 0)
+    for load in loads:
+        load.wait()
+    ticks_ahead = line.per_segment
+
+    def next_leave(m, carry):
+        def item(tile_at, inner):
+            @pl.when(tile_at < ticks_ahead)
+            def _():
+                line.tick((m - 1) * ticks_ahead + tile_at)
+
+            leave(m, tile_at)
+            return inner
+
+        lax.fori_loop(0, pieces, item, 0)
+        return carry
+
+    lax.fori_loop(1, seqs, next_leave, 0)
+    at_tick = (seqs - 1) * ticks_ahead
+    fetch_down(0).start()
+
+    def expand(at, carry):
+        @pl.when(at < ticks_ahead)
+        def _():
+            line.tick(at_tick + at)
+
+        @pl.when(at + 1 < pieces)
+        def _():
+            fetch_down(at + 1).start()
+
+        fetch_down(at).wait()
+        parts[pl.ds(all_rows, late * rows), tile_of(at)] = lax.dot_general(
+            inner_ref[pl.ds((seqs - late) * rows, late * rows), :],
+            weights[lax.rem(at, 2), :, :units],
+            contract,
+            preferred_element_type=jnp.float32,
+        ).astype(jnp.bfloat16)
+        return carry
+
+    lax.fori_loop(0, pieces, expand, 0)
+    opened = max(seqs * ticks_ahead, line.ready(1))
+    line.run(seqs * ticks_ahead, opened)
 
     def sequence(m, carry):
-        first = line.ready(1) + m * (heads + 1)
+        first = opened + m * (heads + 1)
         line.tick(first)
         attended_grads(m)
 
@@ -914,22 +1063,30 @@
         lax.fori_loop(0, heads, item, 0)
         for step in range(1, n):
             copy(m, step).start()
+
+        @pl.when(m > 0)
+        def _():
+            gather(m - 1)
+
         return carry
 
     lax.fori_loop(0, seqs, sequence, 0)
-    line.run(line.ready(1) + seqs * (heads + 1), line.ticks)
-
-    def collect(m, carry):
-        gather(m)
-        return carry
-
-    lax.fori_loop(0, seqs, collect, 0)
+    saves[1].start()
+    line.run(opened + seqs * (heads + 1), line.ticks)
+
+    saves[2].start()
+    gather(seqs - 1)
     line.drain()
+    for save in saves:
+        save.wait()
 
 
 def back_one(
-    normal_part,
-    mixed_part,
+    inner,
+    grad_gate,
+    grad_up,
+    pair_whole,
+    mixed_early,
     residual,
     grad_out,
     gains,
@@ -945,8 +1102,10 @@
 ):
     seqs, width, rows = queries.shape
     groups = key_values.shape[2]
-    all_rows, model_width = normal_part.shape
-    late = mixed_part.shape[0] // rows
+    all_rows, model_width = residual.shape
+    late = seqs - mixed_early.shape[0] // rows
+    cosine, sine, orders, lengths = where
+    units = inner.shape[1]
     line_rows = all_rows + late * rows
     vmem = pl.BlockSpec(memory_space=VMEM)
     hbm = pl.BlockSpec(memory_space=pl.ANY)
@@ -955,21 +1114,32 @@
     return pl.pallas_call(
         functools.partial(back_one_body, n, tp, groups, late),
         out_shape=(
-            shape((line_rows, model_width), jnp.bfloat16),
+            shape((all_rows, model_width), jnp.bfloat16),
+            shape((all_rows, model_width), jnp.bfloat16),
             shape((groups * (GROUP + 2) * HEAD_DIMENSION, all_rows), jnp.bfloat16),
             shape((8, model_width), jnp.float32),
         ),
-        in_specs=[hbm, hbm, vmem, vmem, vmem, hbm] + [vmem] * 6 + [smem] * 2,
-        out_specs=(vmem,) * 3,
+        in_specs=[vmem] * 2 + [hbm] + [vmem] * 4 + [hbm] * 8 + [smem] * 2,
+        out_specs=(hbm,) * 2 + (vmem,) * 2,
         scratch_shapes=[
             VMEM((line_rows, model_width), jnp.bfloat16),
+            VMEM((line_rows, model_width), jnp.bfloat16),
+            VMEM((2, 256, 2 * units), jnp.bfloat16),
+            VMEM((all_rows, units), jnp.bfloat16),
+            VMEM((all_rows, model_width), jnp.bfloat16),
+            VMEM((all_rows, model_width), jnp.bfloat16),
             VMEM((model_width, width), jnp.bfloat16),
+            VMEM(queries.shape, jnp.bfloat16),
+            VMEM(key_values.shape, jnp.bfloat16),
+            VMEM(full.shape, jnp.float32),
             VMEM((width, rows), jnp.bfloat16),
             VMEM((n, 2 * HEAD_DIMENSION, rows), jnp.float32),
             VMEM((n * rows, rows), jnp.float32),
             VMEM((seqs, n, groups, 2 * HEAD_DIMENSION, rows), jnp.bfloat16),
             VMEM((seqs, n - 1, groups, 2 * HEAD_DIMENSION, rows), jnp.bfloat16),
+            pltpu.SemaphoreType.DMA((7,)),
             pltpu.SemaphoreType.DMA((3,)),
+            pltpu.SemaphoreType.DMA((2,)),
             pltpu.SemaphoreType.DMA((seqs, n - 1)),
             pltpu.SemaphoreType.DMA((seqs, n - 1)),
         ]
@@ -980,17 +1150,23 @@
         cost_estimate=line_cost(line_rows, model_width),
         name="back_one",
     )(
-        normal_part,
-        mixed_part,
+        grad_gate,
+        grad_up,
+        pair_whole,
+        gains,
+        log_total,
+        cosine,
+        sine,
+        inner,
         residual,
         grad_out,
-        gains,
         out_whole,
         queries,
         key_values,
         full,
-        log_total,
-        *where,
+        mixed_early,
+        orders,
+        lengths,
     )
 
 
@@ -1000,16 +1176,29 @@
     skip,
     proj_ref,
     weight_ref,
+    gain_ref,
+    token_from,
+    residual_grad_from,
+    out_ref,
+    gain_sums,
     token_ref,
     residual_grad_ref,
-    gain_ref,
-    out_ref,
-    gain_sums,
     parts,
+    load_sem,
     inbox,
     *sems,
 ):
     z = lax.axis_index("tp")
+    loads = [
+        pltpu.make_async_copy(token_from, token_ref, load_sem.at[0]),
+        pltpu.make_async_copy(
+            residual_grad_from.at[pl.ds(0, residual_grad_ref.shape[0])],
+            residual_grad_ref,
+            load_sem.at[1],
+        ),
+    ]
+    for load in loads:
+        load.start()
     pl.semaphore_wait(pltpu.get_barrier_semaphore(), line_greet(tp, z))
     gain_sums[...] = jnp.zeros_like(gain_sums)
     rows = token_ref.shape[0] // seqs
@@ -1036,6 +1225,9 @@
     for m in range(seqs):
         product(m)
         line.run(2 * m, 2 * m + 2)
+        if m == 0:
+            for load in loads:
+                load.wait()
     line.run(2 * seqs, line.ticks)
     line.drain()
 
@@ -1043,232 +1235,223 @@
 def back_two(projected, first_whole, tokens, residual_grad, gains, skip, seqs, tp, ident):
     rows, width = tokens.shape
     vmem = pl.BlockSpec(memory_space=VMEM)
+    hbm = pl.BlockSpec(memory_space=pl.ANY)
     shape = jax.ShapeDtypeStruct
     return pl.pallas_call(
         functools.partial(back_two_body, tp, seqs, skip),
         out_shape=(shape((rows, width), jnp.bfloat16), shape((8, width), jnp.float32)),
-        in_specs=[vmem] * 5,
+        in_specs=[vmem] * 3 + [hbm] * 2,
         out_specs=(vmem,) * 2,
-        scratch_shapes=[VMEM((rows, width), jnp.bfloat16)]
+        scratch_shapes=[VMEM((rows, width), jnp.bfloat16)] * 3
+        + [pltpu.SemaphoreType.DMA((2,))]
         + line_scratch(rows, width, seqs, rows // seqs),
         compiler_params=pltpu.CompilerParams(
             collective_id=ident, has_side_effects=True, vmem_limit_bytes=56 * 2**20
         ),
         cost_estimate=line_cost(rows, width),
         name="back_two",
-    )(projected, first_whole, tokens, residual_grad, gains)
+    )(projected, first_whole, gains, tokens, residual_grad)
 
 
 def hidden_body(
-    normal_ref, grad_out_ref, gate_ref, up_ref, down_ref, inner_ref, grad_gate_ref, grad_up_ref
-):
-    def product(left, right):
-        return jnp.dot(left[...], right[...], preferred_element_type=jnp.float32)
-
-    gate = product(normal_ref, gate_ref)
-    up = product(normal_ref, up_ref)
-    grad_inner = product(grad_out_ref, down_ref)
-    sigmoid = jax.nn.sigmoid(gate)
-    silu = gate * sigmoid
-    inner_ref[...] = (silu * up).astype(jnp.bfloat16)
-    grad_gate_ref[...] = (
-        grad_inner * up * sigmoid * (1.0 + gate * (1.0 - sigmoid))
-    ).astype(jnp.bfloat16)
-    grad_up_ref[...] = (grad_inner * silu).astype(jnp.bfloat16)
-
-
-def hidden_units(normal, grad_out, whole, tile=256):
-    rows, width = normal.shape
-    columns = whole.shape[1]
-    units = columns // 3
-    steps = units // tile
-    vmem = pl.BlockSpec(memory_space=VMEM)
-    return pl.pallas_call(
-        hidden_body,
-        grid=(steps,),
-        out_shape=(jax.ShapeDtypeStruct((rows, units), jnp.bfloat16),) * 3,
-        in_specs=[vmem, vmem]
-        + [
-            pl.BlockSpec((width, tile), functools.partial(lambda k, i: (0, k * steps + i), k))
-            for k in range(3)
-        ],
-        out_specs=[pl.BlockSpec((rows, tile), lambda i: (0, i))] * 3,
-        compiler_params=pltpu.CompilerParams(vmem_limit_bytes=56 * 2**20),
-        cost_estimate=pl.CostEstimate(
-            flops=2 * rows * width * columns,
-            bytes_accessed=2 * (rows + width) * columns,
-            transcendentals=rows * units,
-        ),
-        name="hidden_units",
-    )(normal, grad_out, whole, whole, whole)
-
-
-def mid_body(
     tp,
     seqs,
     early,
     normal_ref,
     grad_out_ref,
+    residual_ref,
+    whole_ref,
+    grads_ref,
     inner_ref,
     gate_ref,
     up_ref,
-    residual_ref,
-    whole_ref,
-    grads_ref,
-    normal_part,
-    late_part,
     out_ref,
     residual,
     turned,
     staged,
+    columns,
     weights,
     parts,
     load_sem,
+    column_sem,
     weight_sem,
     store_sem,
     inbox,
     *sems,
 ):
     z = lax.axis_index("tp")
-    load = pltpu.make_async_copy(
-        residual_ref.at[pl.ds(0, residual.shape[0])], residual, load_sem.at[0]
-    )
-    load.start()
     rows, units = inner_ref.shape
     width = normal_ref.shape[1]
     tile = staged.shape[2]
     pieces = width // tile
     steps = units // tile
     early_rows = parts.shape[0]
-    contract = (((1,), (1,)), ((), ()))
-
-    def fetch(at, first, columns):
+
+    def columns_of(at):
+        return pl.ds(pl.multiple_of(at * tile, tile), tile)
+
+    def fetch_columns(at):
+        slot = lax.rem(at, 2)
+        return [
+            pltpu.make_async_copy(
+                whole_ref.at[:, columns_of(kind * steps + lax.rem(at, steps))],
+                columns.at[slot, kind],
+                column_sem.at[slot, kind],
+            )
+            for kind in range(3)
+        ]
+
+    def fetch(at):
         slot = lax.rem(at, 2)
         return pltpu.make_async_copy(
-            whole_ref.at[pl.ds(pl.multiple_of(at * tile, tile), tile), pl.ds(first, columns)],
-            weights.at[slot, :, pl.ds(0, columns)],
+            whole_ref.at[columns_of(at), pl.ds(2 * units, units)],
+            weights.at[slot],
             weight_sem.at[slot],
         )
 
-    def columns_of(at):
-        return pl.ds(pl.multiple_of(at * tile, tile), tile)
-
-    fetch(0, 2 * units, units).start()
+    load = pltpu.make_async_copy(
+        residual_ref.at[pl.ds(0, early_rows)], residual, load_sem.at[0]
+    )
+    for copy in fetch_columns(0):
+        copy.start()
+    load.start()
     pl.semaphore_wait(pltpu.get_barrier_semaphore(), line_greet(tp, z))
-
-    def expand(at, carry):
-        @pl.when(at + 1 < pieces)
-        def _():
-            fetch(at + 1, 2 * units, units).start()
-
-        fetch(at, 2 * units, units).wait()
-        part = lax.dot_general(
-            inner_ref[...],
-            weights[lax.rem(at, 2), :, :units],
-            contract,
-            preferred_element_type=jnp.float32,
-        ).astype(jnp.bfloat16)
-        parts[:, columns_of(at)] = part[:early_rows]
-        late_part[:, columns_of(at)] = part[early_rows:]
-        return carry
-
-    lax.fori_loop(0, pieces, expand, 0)
-    load.wait()
-    fetch(0, 0, 2 * units).start()
-    turned[...] = normal_ref[...].T
 
     def finish(segment, at, total):
         out_ref[at, :] = (residual[at, :].astype(jnp.float32) + total).astype(jnp.bfloat16)
 
     line = Line(tp, z, early, rows // seqs, parts, inbox, out_ref, sems, finish)
 
-    def store(kind, at):
+    early_opening = rows // seqs
+
+    def units_of(at, low, high):
+        slot = lax.rem(at, 2)
+
+        @pl.when(at + 1 < 2 * steps)
+        def _():
+            for copy in fetch_columns(at + 1):
+                copy.start()
+
+        for copy in fetch_columns(at):
+            copy.wait()
+
+        def product(left, kind):
+            return jnp.dot(
+                left[low:high, :], columns[slot, kind], preferred_element_type=jnp.float32
+            )
+
+        gate = product(normal_ref, 0)
+        up = product(normal_ref, 1)
+        grad_inner = product(grad_out_ref, 2)
+        sigmoid = jax.nn.sigmoid(gate)
+        silu = gate * sigmoid
+        to = columns_of(lax.rem(at, steps))
+        inner_ref[low:high, to] = (silu * up).astype(jnp.bfloat16)
+        gate_ref[low:high, to] = (
+            grad_inner * up * sigmoid * (1.0 + gate * (1.0 - sigmoid))
+        ).astype(jnp.bfloat16)
+        up_ref[low:high, to] = (grad_inner * silu).astype(jnp.bfloat16)
+
+    def opening(at, carry):
+        units_of(at, 0, early_opening)
+        return carry
+
+    fetch(0).start()
+    lax.fori_loop(0, steps, opening, 0)
+
+    def expand(low, high):
+        def item(at, carry):
+            @pl.when(at + 1 < pieces)
+            def _():
+                fetch(at + 1).start()
+
+            fetch(at).wait()
+            parts[low:high, columns_of(at)] = lax.dot_general(
+                inner_ref[low:high, :],
+                weights[lax.rem(at, 2)],
+                (((1,), (1,)), ((), ())),
+                preferred_element_type=jnp.float32,
+            ).astype(jnp.bfloat16)
+            return carry
+
+        lax.fori_loop(0, pieces, item, 0)
+
+    expand(0, early_opening)
+    load.wait()
+
+    def others(at, carry):
+        line.tick(at)
+        units_of(steps + at, early_opening, rows)
+        return carry
+
+    if early_rows > early_opening:
+        fetch(0).start()
+    lax.fori_loop(0, steps, others, 0)
+    if early_rows > early_opening:
+        expand(early_opening, early_rows)
+    turned[...] = normal_ref[...].T
+
+    def store(at):
+        slot = lax.rem(at, 2)
         return pltpu.make_async_copy(
-            staged.at[lax.rem(kind * steps + at, 2)],
-            grads_ref.at[:, columns_of(kind * steps + at)],
-            store_sem.at[lax.rem(kind * steps + at, 2)],
+            staged.at[slot], grads_ref.at[:, columns_of(at)], store_sem.at[slot]
         )
 
     for kind, right in enumerate((gate_ref, up_ref, inner_ref)):
         if kind == 2:
             turned[...] = grad_out_ref[...].T
 
-        def gradient(at, carry):
-            line.tick(kind * steps + at)
-
-            @pl.when(kind * steps + at >= 2)
+        def gradient(step, carry):
+            at = kind * steps + step
+            line.tick(steps + at)
+
+            @pl.when(at >= 2)
             def _():
-                store(kind, at - 2).wait()
-
-            staged[lax.rem(kind * steps + at, 2)] = jnp.dot(
-                turned[...], right[:, columns_of(at)], preferred_element_type=jnp.float32
+                store(at - 2).wait()
+
+            staged[lax.rem(at, 2)] = jnp.dot(
+                turned[...], right[:, columns_of(step)], preferred_element_type=jnp.float32
             ).astype(jnp.bfloat16)
-            store(kind, at).start()
+            store(at).start()
             return carry
 
         lax.fori_loop(0, steps, gradient, 0)
 
-    def leave(at, carry):
-        line.tick(3 * steps + at)
-
-        @pl.when(at + 1 < pieces)
-        def _():
-            fetch(at + 1, 0, 2 * units).start()
-
-        fetch(at, 0, 2 * units).wait()
-        slot = lax.rem(at, 2)
-        normal_part[:, columns_of(at)] = (
-            lax.dot_general(
-                gate_ref[...],
-                weights[slot, :, :units],
-                contract,
-                preferred_element_type=jnp.float32,
-            )
-            + lax.dot_general(
-                up_ref[...],
-                weights[slot, :, units:],
-                contract,
-                preferred_element_type=jnp.float32,
-            )
-        ).astype(jnp.bfloat16)
-        return carry
-
-    lax.fori_loop(0, pieces, leave, 0)
-    store(2, steps - 2).wait()
-    store(2, steps - 1).wait()
-    line.run(3 * steps + pieces, line.ticks)
+    store(3 * steps - 2).wait()
+    store(3 * steps - 1).wait()
+    line.run(4 * steps, line.ticks)
     line.drain()
 
 
-def mid(normal, grad_out, inner, grad_gate, grad_up, residual, whole, seqs, early, tp, ident):
+def hidden_units(normal, grad_out, residual, whole, seqs, early, tp, ident):
     all_rows, width = normal.shape
-    units = inner.shape[1]
     columns = whole.shape[1]
+    units = columns // 3
     rows = all_rows // seqs
     tile = 256
     low = jnp.bfloat16
     shape = jax.ShapeDtypeStruct
     vmem = pl.BlockSpec(memory_space=VMEM)
     hbm = pl.BlockSpec(memory_space=pl.ANY)
+    dma = pltpu.SemaphoreType.DMA
     return pl.pallas_call(
-        functools.partial(mid_body, tp, seqs, early),
-        out_shape=(
-            shape((width, columns), low),
-            shape((all_rows, width), low),
-            shape(((seqs - early) * rows, width), low),
-            shape((early * rows, width), low),
-        ),
-        in_specs=[vmem] * 5 + [hbm] * 2,
-        out_specs=(hbm,) + (vmem,) * 3,
+        functools.partial(hidden_body, tp, seqs, early),
+        out_shape=(shape((width, columns), low),)
+        + (shape((all_rows, units), low),) * 3
+        + (shape((early * rows, width), low),),
+        in_specs=[vmem] * 2 + [hbm] * 2,
+        out_specs=(hbm,) + (vmem,) * 4,
         scratch_shapes=[
             VMEM((early * rows, width), low),
             VMEM((width, all_rows), low),
             VMEM((2, width, tile), low),
-            VMEM((2, tile, 2 * units), low),
+            VMEM((2, 3, width, tile), low),
+            VMEM((2, tile, units), low),
             VMEM((early * rows, width), low),
-            pltpu.SemaphoreType.DMA((1,)),
-            pltpu.SemaphoreType.DMA((2,)),
-            pltpu.SemaphoreType.DMA((2,)),
+            dma((1,)),
+            dma((2, 3)),
+            dma((2,)),
+            dma((2,)),
         ]
         + line_scratch(early * rows, width, early, rows),
         compiler_params=pltpu.CompilerParams(
@@ -1277,41 +1460,33 @@
         cost_estimate=pl.CostEstimate(
             flops=4 * all_rows * width * columns,
             bytes_accessed=40 * all_rows * width,
-            transcendentals=0,
+            transcendentals=all_rows * units,
         ),
-        name="mid",
-    )(normal, grad_out, inner, grad_gate, grad_up, residual, whole)
+        name="hidden_units",
+    )(normal, grad_out, residual, whole)
 
 
 def first_grads_body(normal_ref, proj_ref, residual_ref, attended_ref, out_ref):
-    width = out_ref.shape[0]
     split = attended_ref.shape[0]
-    tile = 512 if width % 512 == 0 else width
     contract = (((1,), (1,)), ((), ()))
-    for low in range(0, width, tile):
-        out_ref[low : low + tile, :split] = lax.dot_general(
-            residual_ref[: normal_ref.shape[0], low : low + tile].T,
-            attended_ref[...],
-            contract,
-            preferred_element_type=jnp.float32,
-        ).astype(jnp.bfloat16)
-        out_ref[low : low + tile, split:] = lax.dot_general(
-            normal_ref[:, low : low + tile].T,
-            proj_ref[...],
-            contract,
-            preferred_element_type=jnp.float32,
+    for left, right, low in ((residual_ref, attended_ref, 0), (normal_ref, proj_ref, split)):
+        out_ref[:, low : low + right.shape[0]] = lax.dot_general(
+            left[...].T, right[...], contract, preferred_element_type=jnp.float32
         ).astype(jnp.bfloat16)
 
 
 def first_grads_of(normal, projected, residual_grad, attended):
     rows, width = normal.shape
     columns = projected.shape[0] + attended.shape[0]
+    tile = 512 if width % 512 == 0 else width
     vmem = pl.BlockSpec(memory_space=VMEM)
+    left = pl.BlockSpec((rows, tile), lambda i: (0, i))
     return pl.pallas_call(
         first_grads_body,
+        grid=(width // tile,),
         out_shape=jax.ShapeDtypeStruct((width, columns), jnp.bfloat16),
-        in_specs=[vmem] * 4,
-        out_specs=vmem,
+        in_specs=[left, vmem, left, vmem],
+        out_specs=pl.BlockSpec((tile, columns), lambda i: (i, 0)),
         compiler_params=pltpu.CompilerParams(vmem_limit_bytes=48 * 2**20),
         cost_estimate=pl.CostEstimate(
             flops=2 * rows * width * columns,
@@ -1466,6 +1641,7 @@
         out_whole,
         pair_whole,
         first_normal,
+        grad_out,
         gains,
         queries,
         key_values,
@@ -1476,6 +1652,7 @@
         second_normal,
     ) = front(
         token_rows,
+        out_cotangent.reshape(all_rows, model_width),
         attention_input_weight,
         tail,
         attend_out.T,
@@ -1489,29 +1666,19 @@
         1,
     )
 
-    keep = (pos_here < lengths[:, None]).astype(jnp.float32)[..., None]
-    grad_out = out_cotangent.reshape(seqs, row_count, model_width).astype(jnp.float32) * keep
-    grad_out = grad_out.astype(low).reshape(all_rows, model_width)
-    inner, grad_gate, grad_up = hidden_units(second_normal, grad_out, pair_whole)
-    early = seqs - 1
-    second_grads, normal_part, mixed_part, mixed_early = mid(
-        second_normal,
-        grad_out,
+    early = 1
+    second_grads, inner, grad_gate, grad_up, mixed_early = hidden_units(
+        second_normal, grad_out, residual, pair_whole, seqs, early, tp_size, 2
+    )
+    inner, second_grads = lax.optimization_barrier((inner, second_grads))
+    second_share = lax.psum_scatter(second_grads, shards, scatter_dimension=0, tiled=True)
+
+    grad_residual, mixed, grad_projected, second_gain = back_one(
         inner,
         grad_gate,
         grad_up,
-        residual,
         pair_whole,
-        seqs,
-        early,
-        tp_size,
-        2,
-    )
-    second_share = lax.psum_scatter(second_grads, shards, scatter_dimension=0, tiled=True)
-
-    back, grad_projected, second_gain = back_one(
-        normal_part,
-        mixed_part,
+        mixed_early,
         residual,
         grad_out,
         gains,
@@ -1525,9 +1692,8 @@
         tp_size,
         4,
     )
-    mixed = jnp.concatenate([mixed_early, back[all_rows:]], 0)
     first_grads = first_grads_of(
-        first_normal, grad_projected, back, attended
+        first_normal, grad_projected, grad_residual, attended
     )
     grad_projected, first_grads, second_share = lax.optimization_barrier(
         (grad_projected, first_grads, second_share)
@@ -1537,7 +1703,7 @@
         grad_projected,
         in_whole,
         token_rows,
-        back,
+        grad_residual,
         gains,
         0,
         seqs,

time: 690 us -> 655 us (0.949)
  Pallas kernels: 606 us -> 589 us
  waiting for transfers between devices: 11 us -> 0.05 us
  other arithmetic: 43.3 us -> 33.9 us
    pallas_call x3 -> x2, Pallas kernels: 146 us -> 99.3 us  [the longest x1 87.7 us: hidden_units(): pl.pallas_call(functools.partial(hidden_body, tp, seqs, early), out_shape...]
    pallas_call x1, Pallas kernels: 157 us -> 191 us  [back_one(): pl.pallas_call(functools.partial(back_one_body, n, tp, groups, late), out...]
    reduce_scatter x1, waiting for transfers between devices: 11 us -> 0.01 us  [on_device(): lax.psum_scatter(second_grads, shards, scatter_dimension=0, tiled=True)]
  transfers between devices with their start and end apart: 2 -> 2, of which waited for: 1 -> 0; matrix products, arithmetic and copies ran while one was open for 4% -> 4% of each run, Pallas kernels for 43% -> 50%
where the time goes in v5:
time: 655 us; the launch traced here: 646 us
  Pallas kernels  589 us (90%)
  other arithmetic  33.9 us (5%)
  between operations  14.8 us (2%)
  local copies, waits for them, and re-layouts  7.84 us (1%)
    pallas_call x1, Pallas kernels, back_one(): pl.pallas_call(functools.partial(back_one_body, n, tp, groups, late), out...  191 us
    pallas_call x1, Pallas kernels, front(): pl.pallas_call(functools.partial(front_body, n, tp, fsdp, groups), out_sh...  182 us
    pallas_call x1, Pallas kernels, back_two(): pl.pallas_call(functools.partial(back_two_body, tp, seqs, skip), out_shap...  107 us
    pallas_call x1, Pallas kernels, hidden_units(): pl.pallas_call(functools.partial(hidden_body, tp, seqs, early), out_shape...  87.7 us
    convert_element_type x4, other arithmetic, on_device(): results.append(updated[2].astype(low))  20.7 us
  transfers between devices with their start and end apart: 2, of which 0 were waited for; matrix products, arithmetic and copies ran while one was open for 4% of the time, Pallas kernels for 50%

profile of v5, /device:TPU:0, one launch (start us, length us, event | category | flops | bytes accessed | tf_op | source)
XLA Modules:
  0.0 645.6 jit_solution(451752090657862537)
XLA Ops:
  7.2 0.0 reduce-scatter.3.cloned.1.call-start
  7.3 0.7 convert.12
  8.0 0.7 copy.48
  8.7 0.2 copy.43
  8.8 0.9 slice.39
  9.8 0.1 dynamic-slice
  9.8 0.1 select_reduce_fusion
  10.0 0.7 fusion.10.tail_ref
  10.7 1.2 multiply_sine_fusion
  11.9 0.0 copy-done.10
  11.9 181.5 %front.1 = (bf16[2560,1024]{1,0:T(8,128)(2,1)}, bf16[2560,640]{1,0:T(8,128)(2,1)}, bf16[2560,5376]{1,0:T(8,128)(2,1)}, bf16[768,2560]{1,0:T(8,128)(2,1)}, bf16[7...) custom-call(bf16[768,2560]{1,0:T(8,128)(2,1)} %bitcast.35, ...), custom_call_target="tpu_custom_call" | custom-call | flops 1966080 | bytes 157286400 | tf_op jit(solution)/shard_map/front/pallas_call | solution.py:704
  193.4 87.7 %hidden_units.1 = (bf16[2560,5376]{1,0:T(8,128)(2,1)}, bf16[768,1792]{1,0:T(8,128)(2,1)}, bf16[768,1792]{1,0:T(8,128)(2,1)}, bf16[768,1792]{1,0:T(8,128)(2,1)}, bf16[256,2560]{1,0:T(8,128)(2,1)}) custom-call(bf16[768,2560]{1,0:T(8,128)(2,1)} %get-tuple-element.50.normal_ref, bf16[768,2560]{1,0:T(8,128)(2,1)} %get-tuple-element.51.grad_out_ref.grad_out_from, ...), custom_call_target="tpu_custom_call" | custom-call | flops 42278584320 | bytes 78643200 | tf_op jit(solution)/shard_map/hidden_units/pallas_call | solution.py:1437
  281.1 0.0 reduce-scatter.3.cloned.1.call-update
  281.1 0.0 reduce-scatter.5.cloned.1.call-start
  281.2 0.0 copy-start.1
  281.2 190.9 %back_one.1 = (bf16[768,2560]{1,0:T(8,128)(2,1)}, bf16[768,2560]{1,0:T(8,128)(2,1)}, bf16[960,768]{1,0:T(8,128)(2,1)}, f32[8,2560]{1,0:T(8,128)}) custom-call(bf16[768,1792]{1,0:T(8,128)(2,1)} %get-tuple-element.54.gate_ref, bf16[768,1792]{1,0:T(8,128)(2,1)} %get-tuple-element.55.up_ref, bf16[2560,5376]{1,0:T(8,128)(2,1)} %get-tuple-element.53.whole_ref.pair_ref, ...), custom_call_target="tpu_custom_call" | custom-call | flops 3276800 | bytes 262144000 | tf_op jit(solution)/shard_map/back_one/pallas_call | solution.py:1114
  472.1 0.0 copy-done.1
  472.1 0.0 copy-start
  472.1 1.4 copy-done
  473.5 11.6 %first_grads.1 = bf16[2560,1600]{1,0:T(8,128)(2,1)} custom-call(bf16[768,2560]{1,0:T(8,128)(2,1)} %get-tuple-element.68.normal_ref, bf16[960,768]{1,0:T(8,128)(2,1)S(1)} %copy-done, bf16[768,2560]{1,0:T(8,128)(2,1)} %get-tuple-element.69.residual_ref.residual_grad_from, bf16[640,768]{1,0:T(8,128)(2,1)S(1)} %copy-done.1), custom_call_target="tpu_custom_call" | custom-call | flops 6291456000 | bytes 18513920 | tf_op jit(solution)/shard_map/first_grads/pallas_call | solution.py:1484
  485.1 0.0 reduce-scatter.5.cloned.1.call-update
  485.1 0.9 copy-done.9
  486.0 0.1 stack.10
  486.1 0.0 copy-start.12
  486.1 0.0 copy-start.13
  486.1 106.5 %back_two.1 = (bf16[768,2560]{1,0:T(8,128)(2,1)}, f32[8,2560]{1,0:T(8,128)}) custom-call(bf16[960,768]{1,0:T(8,128)(2,1)} %get-tuple-element.72.proj_ref, bf16[2560,1024]{1,0:T(8,128)(2,1)} %get-tuple-element.73.weight_ref, f32[8,2560]{1,0:T(8,128)} %get-tuple-element.56.gain_ref, bf16[768,2560]{1,0:T(8,128)(2,1)} %bitcast.36, ...), custom_call_target="tpu_custom_call" | custom-call | flops 1966080 | bytes 157286400 | tf_op jit(solution)/shard_map/back_two/pallas_call | solution.py:1240
  592.6 0.0 copy-start.5
  592.6 1.1 reduce_sum.28
  593.7 0.1 stack.9
  593.8 0.7 pad.9.x_ref
  594.4 10.7 %gain_sum.1 = f32[8,384]{1,0:T(8,128)} custom-call(f32[8,8,384]{2,1,0:T(8,128)} %pad.9.x_ref), custom_call_target="tpu_custom_call" | custom-call | tf_op jit(solution)/shard_map/gain_sum/pallas_call | solution.py:1562
  605.1 0.0 copy-start.2
  605.1 0.0 slice-start
  605.2 0.0 slice-start.2
  605.2 0.0 slice-start.4
  605.2 7.3 %convert.14 = f32[3,1,256,2560]{3,2,1,0:T(8,128)} convert(bf16[3,1,256,2560]{3,2,1,0:T(8,128)(2,1)} %bitcast.44) | non-fusion elementwise | flops 1966080 | bytes 11796480
  612.5 0.0 copy-done.11
  612.5 0.0 copy-done.12
  612.5 0.0 copy-done.13
  612.5 2.1 multiply_subtract_fusion.4
  614.6 0.0 copy-done.5
  614.6 0.0 copy-done.2
  614.6 0.0 slice-start.3
  614.6 0.0 slice-start.5
  614.6 6.9 %fusion.22 = (bf16[1792,320]{0,1:T(8,128)(2,1)}, f32[1792,320]{0,1:T(8,128)}, f32[1792,320]{0,1:T(8,128)}, f32[1792,320]{0,1:T(8,128)}) fusion(f32[1792,320]{0,1:T(8,128)S(1)} %copy-done.2, bf16[320,5376]{1,0:T(8,128)(2,1)S(1)} %copy-done.5, f32[1792,320]{0,1:T(8,128)} %param.34, f32[1792,320]{0,1:T(8,128)} %param.33), kind=kLoop, calls=%fused_computation.50 | loop fusion | flops 9748480 | bytes 16056320 | tf_op jit(solution)/shard_map/convert_element_type | solution.py:1755
  621.5 0.0 slice-done
  621.5 0.0 slice-done.2
  621.5 0.0 slice-done.4
  621.5 0.0 slice-done.1
  621.5 0.0 slice-done.3
  621.6 0.0 slice-done.5
  621.6 7.1 %fusion.25 = (bf16[320,3584]{1,0:T(8,128)(2,1)}, f32[320,3584]{1,0:T(8,128)}, f32[320,3584]{1,0:T(8,128)}, f32[320,3584]{1,0:T(8,128)}) fusion(f32[320,3584]{1,0:T(8,128)S(1)} %bitcast.34, bf16[320,5376]{1,0:T(8,128)(2,1)S(1)} %copy-done.5, f32[320,3584]{1,0:T(8,128)S(1)} %bitcast.39, f32[320,3584]{1,0:T(8,128)S(1)} %bitcast.41), kind=kLoop, calls=%fused_computation.51 | loop fusion | flops 19496960 | bytes 32112640 | tf_op jit(solution)/shard_map/convert_element_type | solution.py:1755
  628.6 0.0 reduce-scatter.5.cloned.1.call-done
  628.7 0.0 copy-start.7
  628.7 0.0 copy-start.8
  628.7 3.9 fusion.28
  632.6 0.0 copy-done.3
  632.6 0.0 copy-done.6
  632.6 0.0 copy-done.7
  632.6 0.0 copy-done.8
  632.6 0.0 copy-start.4
  632.6 2.8 fusion.31
  635.4 0.9 copy-done.4
  636.4 1.9 copy.50
  (17 shorter events, 0.1 us)
Async XLA Ops:
  7.2 477.9 %reduce-scatter.3.cloned.1.call-start = ((), (), s32[]{:S(2)}) async-start(), calls=%async_computation.2 | async-start | bytes 30965760 | tf_op jit(solution)/shard_map/reduce_scatter | solution.py:1674
  8.7 3.2 copy-start.10
  281.1 347.5 %reduce-scatter.5.cloned.1.call-start = ((), (), s32[]{:S(2)}) async-start(), calls=%async_computation.3 | async-start | bytes 9584640 | tf_op jit(solution)/shard_map/reduce_scatter | solution.py:1701
  281.2 190.9 %copy-start.1 = (bf16[640,768]{1,0:T(8,128)(2,1)S(1)}, bf16[640,768]{1,0:T(8,128)(2,1)}, u32[]{:S(2)}) copy-start(bf16[640,768]{1,0:T(8,128)(2,1)} %get-tuple-element.70.attended_ref) | copy-start | bytes 2949124
  472.1 1.4 copy-start
  485.1 0.9 copy-start.9
  486.1 126.5 %copy-start.11 = (f32[2,320]{1,0:T(2,128)S(1)}, f32[2,320]{1,0:T(2,128)}, u32[]{:S(2)}) copy-start(f32[2,320]{1,0:T(2,128)} %param.35) | copy-start | bytes 7684
  486.1 126.5 %copy-start.12 = (f32[2,320]{1,0:T(2,128)S(1)}, f32[2,320]{1,0:T(2,128)}, u32[]{:S(2)}) copy-start(f32[2,320]{1,0:T(2,128)} %param.37) | copy-start | bytes 7684
  486.1 126.5 %copy-start.13 = (f32[2,320]{1,0:T(2,128)S(1)}, f32[2,320]{1,0:T(2,128)}, u32[]{:S(2)}) copy-start(f32[2,320]{1,0:T(2,128)} %param.36) | copy-start | bytes 7684
  592.6 22.0 %copy-start.5 = (bf16[320,5376]{1,0:T(8,128)(2,1)S(1)}, bf16[320,5376]{1,0:T(8,128)(2,1)}, u32[]{:S(2)}) copy-start(bf16[320,5376]{1,0:T(8,128)(2,1)} %reduce-scatter.3.cloned.1.call-done) | copy-start | bytes 10321924
  605.1 9.5 %copy-start.2 = (f32[1792,320]{0,1:T(8,128)S(1)}, f32[1792,320]{0,1:T(8,128)}, u32[]{:S(2)}) copy-start(f32[1792,320]{0,1:T(8,128)} %param.32) | copy-start | bytes 6881284
  605.1 16.4 %slice-start = ((s8[4587520]{0:T(1024)(128)(4,1)}), s8[4194304]{0:T(1024)(128)(4,1)S(1)}, s32[]{:S(2)}) async-start(s8[4587520]{0:T(1024)(128)(4,1)} %bitcast.33), calls=%async_computation.4 | async-start | bytes 8388608
  605.2 16.4 %slice-start.2 = ((s8[4587520]{0:T(1024)(128)(4,1)}), s8[4194304]{0:T(1024)(128)(4,1)S(1)}, s32[]{:S(2)}) async-start(s8[4587520]{0:T(1024)(128)(4,1)} %bitcast.38), calls=%async_computation.6 | async-start | bytes 8388608
  605.2 16.4 %slice-start.4 = ((s8[4587520]{0:T(1024)(128)(4,1)}), s8[4194304]{0:T(1024)(128)(4,1)S(1)}, s32[]{:S(2)}) async-start(s8[4587520]{0:T(1024)(128)(4,1)} %bitcast.40), calls=%async_computation.8 | async-start | bytes 8388608
  614.6 6.9 %slice-start.1 = ((s8[4587520]{0:T(1024)(128)(4,1)}), s8[393216]{0:T(1024)(128)(4,1)S(1)}, s32[]{:S(2)}) async-start(s8[4587520]{0:T(1024)(128)(4,1)} %bitcast.33), calls=%async_computation.5 | async-start | bytes 786432
  614.6 6.9 %slice-start.3 = ((s8[4587520]{0:T(1024)(128)(4,1)}), s8[393216]{0:T(1024)(128)(4,1)S(1)}, s32[]{:S(2)}) async-start(s8[4587520]{0:T(1024)(128)(4,1)} %bitcast.38), calls=%async_computation.7 | async-start | bytes 786432
  614.6 6.9 %slice-start.5 = ((s8[4587520]{0:T(1024)(128)(4,1)}), s8[393216]{0:T(1024)(128)(4,1)S(1)}, s32[]{:S(2)}) async-start(s8[4587520]{0:T(1024)(128)(4,1)} %bitcast.40), calls=%async_computation.9 | async-start | bytes 786432
  628.6 3.9 copy-start.3
  628.6 3.9 copy-start.6
  628.7 3.9 copy-start.7
  628.7 3.9 copy-start.8
  632.6 3.8 copy-start.4
Sparse Core Ops, SparseCore 0:
  281.3 178.8 reduce-scatter.2
  485.2 71.9 reduce-scatter.4

commit v6 on v5

--- a/solution.py
+++ b/solution.py
@@ -107,33 +107,32 @@
     def tick(self, t):
         n = self.n
         for flow in (0, 1):
+
+            @pl.when((self.hop(flow) == 0) & (t >= 0) & (t < self.chunks))
+            def _():
+                self.reduce_copy(flow, t, self.parts.at[self.rows(flow, t)]).start()
+
+        for flow in (0, 1):
             hop = self.hop(flow)
             g = t - hop * LAG
 
-            @pl.when((g >= 0) & (g < self.chunks))
+            @pl.when((hop > 0) & (g >= 0) & (g < self.chunks))
             def _():
                 rows = self.rows(flow, g)
-
-                @pl.when(hop == 0)
+                self.reduce_copy(flow, g, self.parts.at[rows]).wait_recv()
+                total = self.inbox[rows, :].astype(jnp.float32) + self.parts[rows, :].astype(
+                    jnp.float32
+                )
+
+                @pl.when(hop < n - 1)
                 def _():
-                    self.reduce_copy(flow, g, self.parts.at[rows]).start()
-
-                @pl.when(hop > 0)
+                    self.inbox[rows, :] = total.astype(jnp.bfloat16)
+                    self.reduce_copy(flow, g, self.inbox.at[rows]).start()
+
+                @pl.when(hop == n - 1)
                 def _():
-                    self.reduce_copy(flow, g, self.parts.at[rows]).wait_recv()
-                    total = self.inbox[rows, :].astype(jnp.float32) + self.parts[rows, :].astype(
-                        jnp.float32
-                    )
-
-                    @pl.when(hop < n - 1)
-                    def _():
-                        self.inbox[rows, :] = total.astype(jnp.bfloat16)
-                        self.reduce_copy(flow, g, self.inbox.at[rows]).start()
-
-                    @pl.when(hop == n - 1)
-                    def _():
-                        self.finish(g // self.per_segment, rows, total)
-                        self.back_copy(flow, g).start()
+                    self.finish(g // self.per_segment, rows, total)
+                    self.back_copy(flow, g).start()
 
         for flow in (0, 1):
             hop = self.hop(flow)
@@ -808,9 +807,9 @@
         pltpu.make_async_copy(source, target, load_sem.at[at])
         for at, (source, target) in enumerate(
             (
+                (inner_from, inner_ref),
                 (residual_from, residual_ref),
                 (grad_out_from, grad_out_ref),
-                (inner_from, inner_ref),
                 (weight_from, out_proj),
                 (q_from, q_ref),
                 (kv_from, kv_ref),
@@ -822,13 +821,19 @@
     early_rows = all_rows - late * rows
     saves = [
         pltpu.make_async_copy(early_from, mixed_to.at[pl.ds(0, early_rows)], save_sem.at[0]),
-        pltpu.make_async_copy(out_ref.at[pl.ds(0, all_rows)], grad_to, save_sem.at[1]),
+        pltpu.make_async_copy(out_ref.at[pl.ds(rows, all_rows)], grad_to, save_sem.at[1]),
         pltpu.make_async_copy(
-            out_ref.at[pl.ds(all_rows, late * rows)],
-            mixed_to.at[pl.ds(early_rows, late * rows)],
-            save_sem.at[2],
+            out_ref.at[pl.ds(0, rows)], mixed_to.at[pl.ds(early_rows, rows)], save_sem.at[2]
         ),
     ]
+    if late > 1:
+        saves.append(
+            pltpu.make_async_copy(
+                out_ref.at[pl.ds(rows + all_rows, (late - 1) * rows)],
+                mixed_to.at[pl.ds(early_rows + rows, (late - 1) * rows)],
+                save_sem.at[3],
+            )
+        )
 
     def tile_of(at):
         return pl.ds(pl.multiple_of(at * tile, tile), tile)
@@ -849,7 +854,7 @@
             weight_sem.at[slot],
         )
 
-    fetch(0).start()
+    fetch_down(0).start()
     for load in loads:
         load.start()
     saves[0].start()
@@ -868,20 +873,25 @@
     heads = groups * GROUP
     gain_sums[...] = jnp.zeros_like(gain_sums)
 
+    ahead = rows
+    first_late = seqs - late
+
     def finish(segment, at, total):
-        @pl.when(segment < seqs)
+        is_grad = (segment >= 1) & (segment <= seqs)
+
+        @pl.when(is_grad)
         def _():
+            own = pl.ds(pl.multiple_of(at.start - ahead, CHUNK), CHUNK)
             grad = norm_back(
-                total, residual_ref[at, :].astype(jnp.float32), gain_ref[1:2, :], gain_sums
+                total, residual_ref[own, :].astype(jnp.float32), gain_ref[1:2, :], gain_sums
             )
-            out_ref[at, :] = (grad_out_ref[at, :].astype(jnp.float32) + grad).astype(jnp.bfloat16)
-
-        @pl.when(segment >= seqs)
+            out_ref[at, :] = (grad_out_ref[own, :].astype(jnp.float32) + grad).astype(jnp.bfloat16)
+
+        @pl.when(jnp.logical_not(is_grad))
         def _():
-            start = pl.multiple_of(at.start - late * rows, CHUNK)
-            out_ref[at, :] = (
-                residual_ref[pl.ds(start, CHUNK), :].astype(jnp.float32) + total
-            ).astype(jnp.bfloat16)
+            moved = jnp.where(segment == 0, first_late * rows, (first_late - seqs) * rows)
+            own = pl.ds(pl.multiple_of(at.start + moved, CHUNK), CHUNK)
+            out_ref[at, :] = (residual_ref[own, :].astype(jnp.float32) + total).astype(jnp.bfloat16)
 
     line = Line(tp, z, seqs + late, rows, parts, inbox, out_ref, sems, finish)
 
@@ -902,7 +912,7 @@
     def attended_grads(m):
         grads[...] = (
             jnp.dot(
-                out_ref[pl.ds(pl.multiple_of(m * rows, CHUNK), rows), :],
+                out_ref[pl.ds(pl.multiple_of(ahead + m * rows, CHUNK), rows), :],
                 out_proj[...],
                 preferred_element_type=jnp.float32,
             )
@@ -977,6 +987,7 @@
             copy(m, step).wait_send()
 
     contract = (((1,), (1,)), ((), ()))
+    ticks_ahead = line.per_segment
 
     def leave(m, tile_at):
         at = m * pieces + tile_at
@@ -988,7 +999,7 @@
             fetch(at + 1).start()
 
         fetch(at).wait()
-        parts[own, tile_of(tile_at)] = (
+        parts[pl.ds(pl.multiple_of(ahead + m * rows, CHUNK), rows), tile_of(tile_at)] = (
             lax.dot_general(
                 gate_ref[own, :],
                 weights[slot, :, :units],
@@ -1003,20 +1014,40 @@
             )
         ).astype(jnp.bfloat16)
 
-    def first_leave(tile_at, carry):
-        leave(0, tile_at)
-        return carry
-
-    lax.fori_loop(0, pieces, first_leave, 0)
-    for load in loads:
+    def expand(low, count, to, first_tick):
+        def item(at, carry):
+            if first_tick is not None:
+
+                @pl.when(at < ticks_ahead)
+                def _():
+                    line.tick(first_tick + at)
+
+            @pl.when(at + 1 < pieces)
+            def _():
+                fetch_down(at + 1).start()
+
+            fetch_down(at).wait()
+            parts[pl.ds(to, count * rows), tile_of(at)] = lax.dot_general(
+                inner_ref[pl.ds(low * rows, count * rows), :],
+                weights[lax.rem(at, 2), :, :units],
+                contract,
+                preferred_element_type=jnp.float32,
+            ).astype(jnp.bfloat16)
+            return carry
+
+        lax.fori_loop(0, pieces, item, 0)
+
+    loads[0].wait()
+    expand(first_late, 1, 0, None)
+    fetch(0).start()
+    for load in loads[1:]:
         load.wait()
-    ticks_ahead = line.per_segment
 
     def next_leave(m, carry):
         def item(tile_at, inner):
             @pl.when(tile_at < ticks_ahead)
             def _():
-                line.tick((m - 1) * ticks_ahead + tile_at)
+                line.tick(m * ticks_ahead + tile_at)
 
             leave(m, tile_at)
             return inner
@@ -1024,43 +1055,31 @@
         lax.fori_loop(0, pieces, item, 0)
         return carry
 
-    lax.fori_loop(1, seqs, next_leave, 0)
-    at_tick = (seqs - 1) * ticks_ahead
-    fetch_down(0).start()
-
-    def expand(at, carry):
-        @pl.when(at < ticks_ahead)
-        def _():
-            line.tick(at_tick + at)
-
-        @pl.when(at + 1 < pieces)
-        def _():
-            fetch_down(at + 1).start()
-
-        fetch_down(at).wait()
-        parts[pl.ds(all_rows, late * rows), tile_of(at)] = lax.dot_general(
-            inner_ref[pl.ds((seqs - late) * rows, late * rows), :],
-            weights[lax.rem(at, 2), :, :units],
-            contract,
-            preferred_element_type=jnp.float32,
-        ).astype(jnp.bfloat16)
-        return carry
-
-    lax.fori_loop(0, pieces, expand, 0)
-    opened = max(seqs * ticks_ahead, line.ready(1))
-    line.run(seqs * ticks_ahead, opened)
+    lax.fori_loop(0, seqs, next_leave, 0)
+    done = seqs * ticks_ahead
+    if late > 1:
+        fetch_down(0).start()
+        expand(first_late + 1, late - 1, rows + all_rows, done)
+        done += ticks_ahead
+    opened = max(done, line.ready(2))
+    line.run(done, opened)
+    stride = max(heads // 2 + 1, -(-(line.ready(seqs + 1) - opened) // (seqs - 1)))
 
     def sequence(m, carry):
-        first = opened + m * (heads + 1)
+        first = opened + m * stride
         line.tick(first)
         attended_grads(m)
 
         def item(at, inner):
-            line.tick(first + 1 + at)
+            @pl.when(lax.rem(at, 2) == 0)
+            def _():
+                line.tick(first + 1 + at // 2)
+
             head(m, at)
             return inner
 
         lax.fori_loop(0, heads, item, 0)
+        line.run(first + 1 + heads // 2, first + stride)
         for step in range(1, n):
             copy(m, step).start()
 
@@ -1072,9 +1091,10 @@
 
     lax.fori_loop(0, seqs, sequence, 0)
     saves[1].start()
-    line.run(opened + seqs * (heads + 1), line.ticks)
-
-    saves[2].start()
+    line.run(opened + seqs * stride, line.ticks)
+
+    for save in saves[2:]:
+        save.start()
     gather(seqs - 1)
     line.drain()
     for save in saves:
@@ -1138,7 +1158,7 @@
             VMEM((seqs, n, groups, 2 * HEAD_DIMENSION, rows), jnp.bfloat16),
             VMEM((seqs, n - 1, groups, 2 * HEAD_DIMENSION, rows), jnp.bfloat16),
             pltpu.SemaphoreType.DMA((7,)),
-            pltpu.SemaphoreType.DMA((3,)),
+            pltpu.SemaphoreType.DMA((4,)),
             pltpu.SemaphoreType.DMA((2,)),
             pltpu.SemaphoreType.DMA((seqs, n - 1)),
             pltpu.SemaphoreType.DMA((seqs, n - 1)),
@@ -1171,20 +1191,30 @@
 
 
 def back_two_body(
+    n,
+    fsdp,
     tp,
     seqs,
     skip,
     proj_ref,
     weight_ref,
     gain_ref,
+    second_gain_ref,
     token_from,
     residual_grad_from,
     out_ref,
+    gains_to,
     gain_sums,
     token_ref,
     residual_grad_ref,
     parts,
+    mine,
+    box,
+    tp_mine,
+    tp_box,
     load_sem,
+    gain_sem,
+    tp_sem,
     inbox,
     *sems,
 ):
@@ -1199,7 +1229,22 @@
     ]
     for load in loads:
         load.start()
-    pl.semaphore_wait(pltpu.get_barrier_semaphore(), line_greet(tp, z))
+    me = lax.axis_index("fsdp") * n + lax.axis_index("ctx")
+    shards = n * fsdp
+
+    def shard_at(step):
+        other = lax.rem(me + step, shards)
+        return {"fsdp": other // n, "ctx": lax.rem(other, n)}
+
+    def line_at(step):
+        return {"tp": lax.rem(z + step, tp)}
+
+    barrier = pltpu.get_barrier_semaphore()
+    for step in range(1, shards):
+        pl.semaphore_signal(barrier, inc=1, device_id=shard_at(step), device_id_type=MESH)
+    for step in range(1, tp):
+        pl.semaphore_signal(barrier, inc=1, device_id=line_at(step), device_id_type=MESH)
+    pl.semaphore_wait(barrier, shards - 1 + tp - 1)
     gain_sums[...] = jnp.zeros_like(gain_sums)
     rows = token_ref.shape[0] // seqs
     width = weight_ref.shape[0]
@@ -1228,29 +1273,69 @@
         if m == 0:
             for load in loads:
                 load.wait()
-    line.run(2 * seqs, line.ticks)
+    finished = line.chunks + (tp - 1) * LAG
+    line.run(2 * seqs, finished)
+    mine[...] = jnp.zeros_like(mine)
+    mine[0:1, :] = jnp.sum(gain_sums[...], axis=0, keepdims=True)
+    mine[1:2, :] = jnp.sum(second_gain_ref[...], axis=0, keepdims=True)
+
+    def copy(source, boxes, sem, step, where):
+        return pltpu.make_async_remote_copy(
+            src_ref=source,
+            dst_ref=boxes.at[step - 1],
+            send_sem=sem.at[0, step - 1],
+            recv_sem=sem.at[1, step - 1],
+            device_id=where,
+            device_id_type=MESH,
+        )
+
+    for step in range(1, shards):
+        copy(mine, box, gain_sem, step, shard_at(step)).start()
+    line.run(finished, line.ticks)
+    total = mine[...]
+    for step in range(1, shards):
+        copy(mine, box, gain_sem, step, shard_at(step)).wait()
+        total += box[step - 1]
+    tp_mine[...] = total
+    for step in range(1, tp):
+        copy(tp_mine, tp_box, tp_sem, step, line_at(step)).start()
+    for step in range(1, tp):
+        copy(tp_mine, tp_box, tp_sem, step, line_at(step)).wait()
+        total += tp_box[step - 1]
+    gains_to[...] = total
     line.drain()
 
 
-def back_two(projected, first_whole, tokens, residual_grad, gains, skip, seqs, tp, ident):
+def back_two(
+    projected, first_whole, tokens, residual_grad, gains, second_gain, skip, seqs, n, fsdp, tp, ident
+):
     rows, width = tokens.shape
     vmem = pl.BlockSpec(memory_space=VMEM)
     hbm = pl.BlockSpec(memory_space=pl.ANY)
     shape = jax.ShapeDtypeStruct
     return pl.pallas_call(
-        functools.partial(back_two_body, tp, seqs, skip),
+        functools.partial(back_two_body, n, fsdp, tp, seqs, skip),
         out_shape=(shape((rows, width), jnp.bfloat16), shape((8, width), jnp.float32)),
-        in_specs=[vmem] * 3 + [hbm] * 2,
+        in_specs=[vmem] * 4 + [hbm] * 2,
         out_specs=(vmem,) * 2,
-        scratch_shapes=[VMEM((rows, width), jnp.bfloat16)] * 3
-        + [pltpu.SemaphoreType.DMA((2,))]
+        scratch_shapes=[VMEM((8, width), jnp.float32)]
+        + [VMEM((rows, width), jnp.bfloat16)] * 3
+        + [
+            VMEM((8, width), jnp.float32),
+            VMEM((n * fsdp - 1, 8, width), jnp.float32),
+            VMEM((8, width), jnp.float32),
+            VMEM((tp - 1, 8, width), jnp.float32),
+            pltpu.SemaphoreType.DMA((2,)),
+            pltpu.SemaphoreType.DMA((2, n * fsdp - 1)),
+            pltpu.SemaphoreType.DMA((2, tp - 1)),
+        ]
         + line_scratch(rows, width, seqs, rows // seqs),
         compiler_params=pltpu.CompilerParams(
             collective_id=ident, has_side_effects=True, vmem_limit_bytes=56 * 2**20
         ),
         cost_estimate=line_cost(rows, width),
         name="back_two",
-    )(projected, first_whole, gains, tokens, residual_grad)
+    )(projected, first_whole, gains, second_gain, tokens, residual_grad)
 
 
 def hidden_body(
@@ -1497,91 +1582,6 @@
     )(normal, projected, residual_grad, attended)
 
 
-def gain_body(ctx_size, tp, x_ref, o_ref, inbox, tp_inbox, send_sem, recv_sem, tp_send, tp_recv):
-    shards = x_ref.shape[0]
-    me = lax.axis_index("fsdp") * ctx_size + lax.axis_index("ctx")
-    z = lax.axis_index("tp")
-
-    def to(step):
-        other = lax.rem(me + step, shards)
-        return other, {"fsdp": other // ctx_size, "ctx": lax.rem(other, ctx_size)}
-
-    barrier = pltpu.get_barrier_semaphore()
-    for step in range(1, shards):
-        pl.semaphore_signal(barrier, inc=1, device_id=to(step)[1], device_id_type=MESH)
-    for step in range(1, tp):
-        pl.semaphore_signal(
-            barrier, inc=1, device_id={"tp": lax.rem(z + step, tp)}, device_id_type=MESH
-        )
-    pl.semaphore_wait(barrier, shards - 1 + tp - 1)
-
-    def copy(step):
-        other, where = to(step)
-        return pltpu.make_async_remote_copy(
-            src_ref=x_ref.at[other],
-            dst_ref=inbox.at[step - 1],
-            send_sem=send_sem.at[step - 1],
-            recv_sem=recv_sem.at[step - 1],
-            device_id=where,
-            device_id_type=MESH,
-        )
-
-    def tp_copy(step):
-        return pltpu.make_async_remote_copy(
-            src_ref=tp_inbox.at[0],
-            dst_ref=tp_inbox.at[step],
-            send_sem=tp_send.at[step - 1],
-            recv_sem=tp_recv.at[step - 1],
-            device_id={"tp": lax.rem(z + step, tp)},
-            device_id_type=MESH,
-        )
-
-    for step in range(1, shards):
-        copy(step).start()
-    total = x_ref[me]
-    for step in range(1, shards):
-        copy(step).wait()
-        total += inbox[step - 1]
-    tp_inbox[0] = total
-    for step in range(1, tp):
-        tp_copy(step).start()
-    for step in range(1, tp):
-        tp_copy(step).wait()
-        total += tp_inbox[step]
-    o_ref[...] = total
-
-
-def gain_sum(partial, shards, ctx_size, tp, ident):
-    two, width = partial.shape
-    own = width // shards
-    padded = -(-own // 128) * 128
-    pieces = jnp.pad(
-        partial.reshape(two, shards, own).transpose(1, 0, 2),
-        ((0, 0), (0, 8 - two), (0, padded - own)),
-    )
-    total = pl.pallas_call(
-        functools.partial(gain_body, ctx_size, tp),
-        out_shape=jax.ShapeDtypeStruct((8, padded), jnp.float32),
-        in_specs=[pl.BlockSpec(memory_space=VMEM)],
-        out_specs=pl.BlockSpec(memory_space=VMEM),
-        scratch_shapes=[
-            VMEM((shards - 1, 8, padded), jnp.float32),
-            VMEM((tp, 8, padded), jnp.float32),
-            pltpu.SemaphoreType.DMA((shards - 1,)),
-            pltpu.SemaphoreType.DMA((shards - 1,)),
-            pltpu.SemaphoreType.DMA((tp - 1,)),
-            pltpu.SemaphoreType.DMA((tp - 1,)),
-        ],
-        compiler_params=pltpu.CompilerParams(collective_id=ident, has_side_effects=True),
-        name="gain_sum",
-    )(pieces)
-    return total[:two, :own]
-
-
-def dot(spec, left, right):
-    return jnp.einsum(spec, left, right, preferred_element_type=jnp.float32)
-
-
 def on_device(
     tokens,
     out_cotangent,
@@ -1699,24 +1699,24 @@
         (grad_projected, first_grads, second_share)
     )
     first_share = lax.psum_scatter(first_grads, shards, scatter_dimension=0, tiled=True)
-    input_grad, first_gain = back_two(
+    fsdp_size = lax.axis_size("fsdp")
+    input_grad, gain_grads = back_two(
         grad_projected,
         in_whole,
         token_rows,
         grad_residual,
         gains,
+        second_gain,
         0,
         seqs,
+        ctx_size,
+        fsdp_size,
         tp_size,
         5,
     )
-    gain_share = gain_sum(
-        jnp.stack([first_gain.sum(0), second_gain.sum(0)]),
-        lax.axis_size("fsdp") * ctx_size,
-        ctx_size,
-        tp_size,
-        7,
-    )
+    own = norm_gains.shape[1]
+    shard = lax.axis_index("fsdp") * ctx_size + lax.axis_index("ctx")
+    gain_share = lax.dynamic_slice_in_dim(gain_grads[:2], shard * own, own, 1)
 
     gradients = (
         first_share[:, out_width:],

time: 655 us -> 650 us (level)
    pallas_call x2 -> x1, Pallas kernels: 117 us -> 118 us  [back_two(): pl.pallas_call(functools.partial(back_two_body, n, fsdp, tp, seqs, skip),...]
  transfers between devices with their start and end apart: 2 -> 2, of which waited for: 0 -> 0; matrix products, arithmetic and copies ran while one was open for 4% -> 3% of each run, Pallas kernels for 50% -> 50%
where the time goes in v6:
time: 650 us; the launch traced here: 641 us
  Pallas kernels  590 us (91%)
  other arithmetic  28.8 us (4%)
  between operations  14.8 us (2%)
  local copies, waits for them, and re-layouts  7.08 us (1%)
    pallas_call x1, Pallas kernels, back_one(): pl.pallas_call(functools.partial(back_one_body, n, tp, groups, late), out...  190 us
    pallas_call x1, Pallas kernels, front(): pl.pallas_call(functools.partial(front_body, n, tp, fsdp, groups), out_sh...  182 us
    pallas_call x1, Pallas kernels, back_two(): pl.pallas_call(functools.partial(back_two_body, n, fsdp, tp, seqs, skip),...  118 us
    pallas_call x1, Pallas kernels, hidden_units(): pl.pallas_call(functools.partial(hidden_body, tp, seqs, early), out_shape...  87.9 us
    convert_element_type x4, other arithmetic, on_device(): results.append(updated[2].astype(low))  18 us
  transfers between devices with their start and end apart: 2, of which 0 were waited for; matrix products, arithmetic and copies ran while one was open for 3% of the time, Pallas kernels for 50%

profile of v6, /device:TPU:0, one launch (start us, length us, event | category | flops | bytes accessed | tf_op | source)
XLA Modules:
  0.0 640.6 jit_solution(8316666107375783796)
XLA Ops:
  7.2 0.0 reduce-scatter.3.cloned.1.call-start
  7.3 0.7 convert.12
  8.0 0.7 copy.48
  8.7 0.2 copy.43
  8.8 0.9 slice.37
  9.8 0.1 dynamic-slice
  9.8 0.1 select_reduce_fusion
  10.0 0.7 fusion.10.tail_ref
  10.7 1.2 multiply_sine_fusion
  11.9 0.0 copy-done.12
  11.9 181.6 %front.1 = (bf16[2560,1024]{1,0:T(8,128)(2,1)}, bf16[2560,640]{1,0:T(8,128)(2,1)}, bf16[2560,5376]{1,0:T(8,128)(2,1)}, bf16[768,2560]{1,0:T(8,128)(2,1)}, bf16[7...) custom-call(bf16[768,2560]{1,0:T(8,128)(2,1)} %bitcast.33, ...), custom_call_target="tpu_custom_call" | custom-call | flops 1966080 | bytes 157286400 | tf_op jit(solution)/shard_map/front/pallas_call | solution.py:703
  193.5 87.9 %hidden_units.1 = (bf16[2560,5376]{1,0:T(8,128)(2,1)}, bf16[768,1792]{1,0:T(8,128)(2,1)}, bf16[768,1792]{1,0:T(8,128)(2,1)}, bf16[768,1792]{1,0:T(8,128)(2,1)}, bf16[256,2560]{1,0:T(8,128)(2,1)}) custom-call(bf16[768,2560]{1,0:T(8,128)(2,1)} %get-tuple-element.50.normal_ref, bf16[768,2560]{1,0:T(8,128)(2,1)} %get-tuple-element.51.grad_out_ref.grad_out_from, ...), custom_call_target="tpu_custom_call" | custom-call | flops 42278584320 | bytes 78643200 | tf_op jit(solution)/shard_map/hidden_units/pallas_call | solution.py:1522
  281.4 0.0 reduce-scatter.3.cloned.1.call-update
  281.4 0.0 reduce-scatter.5.cloned.1.call-start
  281.5 0.0 copy-start.1
  281.5 190.4 %back_one.1 = (bf16[768,2560]{1,0:T(8,128)(2,1)}, bf16[768,2560]{1,0:T(8,128)(2,1)}, bf16[960,768]{1,0:T(8,128)(2,1)}, f32[8,2560]{1,0:T(8,128)}) custom-call(bf16[768,1792]{1,0:T(8,128)(2,1)} %get-tuple-element.54.gate_ref, bf16[768,1792]{1,0:T(8,128)(2,1)} %get-tuple-element.55.up_ref, bf16[2560,5376]{1,0:T(8,128)(2,1)} %get-tuple-element.53.whole_ref.pair_ref, ...), custom_call_target="tpu_custom_call" | custom-call | flops 3276800 | bytes 262144000 | tf_op jit(solution)/shard_map/back_one/pallas_call | solution.py:1134
  471.9 0.0 copy-done.1
  471.9 0.0 copy-start
  471.9 1.4 copy-done
  473.3 11.6 %first_grads.1 = bf16[2560,1600]{1,0:T(8,128)(2,1)} custom-call(bf16[768,2560]{1,0:T(8,128)(2,1)} %get-tuple-element.68.normal_ref, bf16[960,768]{1,0:T(8,128)(2,1)S(1)} %copy-done, bf16[768,2560]{1,0:T(8,128)(2,1)} %get-tuple-element.69.residual_ref.residual_grad_from, bf16[640,768]{1,0:T(8,128)(2,1)S(1)} %copy-done.1), custom_call_target="tpu_custom_call" | custom-call | flops 6291456000 | bytes 18513920 | tf_op jit(solution)/shard_map/first_grads/pallas_call | solution.py:1569
  484.9 0.0 reduce-scatter.5.cloned.1.call-update
  484.9 0.0 copy-start.13
  485.0 0.0 copy-start.14
  485.0 0.0 copy-start.15
  485.0 0.0 copy-start.5
  485.0 0.0 copy-start.7
  485.0 0.0 copy-start.8
  485.0 118.2 %back_two.1 = (bf16[768,2560]{1,0:T(8,128)(2,1)}, f32[8,2560]{1,0:T(8,128)}) custom-call(bf16[960,768]{1,0:T(8,128)(2,1)} %get-tuple-element.72.proj_ref, bf16[2560,1024]{1,0:T(8,128)(2,1)} %get-tuple-element.73.weight_ref, f32[8,2560]{1,0:T(8,128)} %get-tuple-element.56.gain_ref, f32[8,2560]{1,0:T(8,128)} %get-tuple-element.74.second_gain_ref, ...), custom_call_target="tpu_custom_call" | custom-call | flops 1966080 | bytes 157286400 | tf_op jit(solution)/shard_map/back_two/pallas_call | solution.py:1316
  603.3 0.9 slice.24
  604.2 0.0 slice-start.2
  604.2 0.0 slice-start.4
  604.2 7.3 %convert.14 = f32[3,1,256,2560]{3,2,1,0:T(8,128)} convert(bf16[3,1,256,2560]{3,2,1,0:T(8,128)(2,1)} %bitcast.42) | non-fusion elementwise | flops 1966080 | bytes 11796480
  611.5 0.0 copy-done.13
  611.5 0.0 copy-done.14
  611.5 0.0 copy-done.15
  611.5 0.7 multiply_subtract_fusion.4
  612.2 0.0 copy-done.5
  612.2 0.0 copy-done.7
  612.2 0.0 copy-done.8
  612.2 0.0 copy-done.2
  612.2 0.0 slice-start.1
  612.2 0.0 slice-start.3
  612.3 0.0 slice-start.5
  612.3 4.5 fusion.22
  616.8 0.0 slice-done
  616.8 0.0 slice-done.2
  616.8 0.0 slice-done.4
  616.8 0.0 slice-done.1
  616.8 0.0 slice-done.3
  616.8 0.0 slice-done.5
  616.9 0.0 copy-start.6
  616.9 7.0 %fusion.25 = (bf16[320,3584]{1,0:T(8,128)(2,1)}, f32[320,3584]{1,0:T(8,128)}, f32[320,3584]{1,0:T(8,128)}, f32[320,3584]{1,0:T(8,128)}) fusion(f32[320,3584]{1,0:T(8,128)S(1)} %bitcast.32, bf16[320,5376]{1,0:T(8,128)(2,1)S(1)} %copy-done.5, f32[320,3584]{1,0:T(8,128)S(1)} %bitcast.37, f32[320,3584]{1,0:T(8,128)S(1)} %bitcast.39), kind=kLoop, calls=%fused_computation.50 | loop fusion | flops 19496960 | bytes 32112640 | tf_op jit(solution)/shard_map/convert_element_type | solution.py:1755
  623.9 0.0 reduce-scatter.5.cloned.1.call-done
  623.9 0.0 copy-done.6
  623.9 0.0 copy-start.10
  623.9 0.0 copy-start.11
  623.9 3.6 fusion.28
  627.6 0.0 copy-done.3
  627.6 0.0 copy-done.9
  627.6 0.0 copy-done.10
  627.6 0.0 copy-done.11
  627.6 2.8 fusion.31
  630.4 0.9 copy-done.4
  631.4 1.9 copy.50
  (15 shorter events, 0.1 us)
Async XLA Ops:
  7.2 477.7 %reduce-scatter.3.cloned.1.call-start = ((), (), s32[]{:S(2)}) async-start(), calls=%async_computation.2 | async-start | bytes 30965760 | tf_op jit(solution)/shard_map/reduce_scatter | solution.py:1674
  8.7 3.2 copy-start.12
  281.4 342.5 %reduce-scatter.5.cloned.1.call-start = ((), (), s32[]{:S(2)}) async-start(), calls=%async_computation.3 | async-start | bytes 9584640 | tf_op jit(solution)/shard_map/reduce_scatter | solution.py:1701
  281.5 190.4 %copy-start.1 = (bf16[640,768]{1,0:T(8,128)(2,1)S(1)}, bf16[640,768]{1,0:T(8,128)(2,1)}, u32[]{:S(2)}) copy-start(bf16[640,768]{1,0:T(8,128)(2,1)} %get-tuple-element.70.attended_ref) | copy-start | bytes 2949124
  471.9 1.4 copy-start
  484.9 126.6 %copy-start.13 = (f32[2,320]{1,0:T(2,128)S(1)}, f32[2,320]{1,0:T(2,128)}, u32[]{:S(2)}) copy-start(f32[2,320]{1,0:T(2,128)} %param.35) | copy-start | bytes 7684
  485.0 126.6 %copy-start.14 = (f32[2,320]{1,0:T(2,128)S(1)}, f32[2,320]{1,0:T(2,128)}, u32[]{:S(2)}) copy-start(f32[2,320]{1,0:T(2,128)} %param.37) | copy-start | bytes 7684
  485.0 126.6 %copy-start.15 = (f32[2,320]{1,0:T(2,128)S(1)}, f32[2,320]{1,0:T(2,128)}, u32[]{:S(2)}) copy-start(f32[2,320]{1,0:T(2,128)} %param.36) | copy-start | bytes 7684
  485.0 127.2 %copy-start.5 = (bf16[320,5376]{1,0:T(8,128)(2,1)S(1)}, bf16[320,5376]{1,0:T(8,128)(2,1)}, u32[]{:S(2)}) copy-start(bf16[320,5376]{1,0:T(8,128)(2,1)} %reduce-scatter.3.cloned.1.call-done) | copy-start | bytes 10321924
  485.0 127.2 %copy-start.7 = (f32[1792,320]{0,1:T(8,128)S(1)}, f32[1792,320]{0,1:T(8,128)}, u32[]{:S(2)}) copy-start(f32[1792,320]{0,1:T(8,128)} %param.34) | copy-start | bytes 6881284
  485.0 127.2 %copy-start.8 = (f32[1792,320]{0,1:T(8,128)S(1)}, f32[1792,320]{0,1:T(8,128)}, u32[]{:S(2)}) copy-start(f32[1792,320]{0,1:T(8,128)} %param.33) | copy-start | bytes 6881284
  604.2 8.1 %copy-start.2 = (f32[1792,320]{0,1:T(8,128)S(1)}, f32[1792,320]{0,1:T(8,128)}, u32[]{:S(2)}) copy-start(f32[1792,320]{0,1:T(8,128)} %param.32) | copy-start | bytes 6881284
  604.2 12.6 %slice-start = ((s8[4587520]{0:T(1024)(128)(4,1)}), s8[4194304]{0:T(1024)(128)(4,1)S(1)}, s32[]{:S(2)}) async-start(s8[4587520]{0:T(1024)(128)(4,1)} %bitcast.31), calls=%async_computation.4 | async-start | bytes 8388608
  604.2 12.6 %slice-start.2 = ((s8[4587520]{0:T(1024)(128)(4,1)}), s8[4194304]{0:T(1024)(128)(4,1)S(1)}, s32[]{:S(2)}) async-start(s8[4587520]{0:T(1024)(128)(4,1)} %bitcast.36), calls=%async_computation.6 | async-start | bytes 8388608
  604.2 12.6 %slice-start.4 = ((s8[4587520]{0:T(1024)(128)(4,1)}), s8[4194304]{0:T(1024)(128)(4,1)S(1)}, s32[]{:S(2)}) async-start(s8[4587520]{0:T(1024)(128)(4,1)} %bitcast.38), calls=%async_computation.8 | async-start | bytes 8388608
  612.2 4.6 slice-start.1
  612.2 4.6 slice-start.3
  612.3 4.6 slice-start.5
  616.9 7.1 %copy-start.6 = (f32[640,320]{0,1:T(8,128)S(1)}, f32[640,320]{0,1:T(8,128)}, u32[]{:S(2)}) copy-start(f32[640,320]{0,1:T(8,128)} %param.26) | copy-start | bytes 2457604
  623.9 3.7 copy-start.3
  623.9 3.7 copy-start.9
  623.9 3.7 copy-start.10
  623.9 3.7 copy-start.11
  627.6 3.8 copy-start.4
Sparse Core Ops, SparseCore 0:
  281.6 184.7 reduce-scatter.2
  485.1 73.8 reduce-scatter.4

commit v7 on v6

--- a/solution.py
+++ b/solution.py
@@ -55,18 +55,20 @@
 
 
 class Line:
-    def __init__(self, n, z, segments, segment_rows, parts, inbox, out, sems, finish):
-        self.n, self.z = n, z
+    def __init__(
+        self, n, z, segments, segment_rows, parts, inbox, out, sems, finish, lag=LAG
+    ):
+        self.n, self.z, self.lag = n, z, lag
         self.segment_rows = segment_rows
         self.per_segment = segment_rows // (2 * CHUNK)
         self.chunks = segments * self.per_segment
         self.parts, self.inbox, self.out = parts, inbox, out
         self.red_send, self.red_recv, self.back_send, self.back_recv = sems
         self.finish = finish
-        self.ticks = self.chunks + 2 * (n - 1) * LAG
+        self.ticks = self.chunks + 2 * (n - 1) * self.lag
 
     def ready(self, segments):
-        return segments * self.per_segment + 2 * (self.n - 1) * LAG
+        return segments * self.per_segment + 2 * (self.n - 1) * self.lag
 
     def rows(self, flow, g):
         start = (
@@ -114,7 +116,7 @@
 
         for flow in (0, 1):
             hop = self.hop(flow)
-            g = t - hop * LAG
+            g = t - hop * self.lag
 
             @pl.when((hop > 0) & (g >= 0) & (g < self.chunks))
             def _():
@@ -136,7 +138,7 @@
 
         for flow in (0, 1):
             hop = self.hop(flow)
-            back = t - (n - 1) * LAG - (n - 1 - hop) * LAG
+            back = t - (n - 1) * self.lag - (n - 1 - hop) * self.lag
 
             @pl.when((back >= 0) & (back < self.chunks) & (hop < n - 1))
             def _():
@@ -1273,7 +1275,7 @@
         if m == 0:
             for load in loads:
                 load.wait()
-    finished = line.chunks + (tp - 1) * LAG
+    finished = line.chunks + (tp - 1) * line.lag
     line.run(2 * seqs, finished)
     mine[...] = jnp.zeros_like(mine)
     mine[0:1, :] = jnp.sum(gain_sums[...], axis=0, keepdims=True)
@@ -1405,7 +1407,7 @@
     def finish(segment, at, total):
         out_ref[at, :] = (residual[at, :].astype(jnp.float32) + total).astype(jnp.bfloat16)
 
-    line = Line(tp, z, early, rows // seqs, parts, inbox, out_ref, sems, finish)
+    line = Line(tp, z, early, rows // seqs, parts, inbox, out_ref, sems, finish, LAG + 1)
 
     early_opening = rows // seqs
 

time: 650 us -> 643 us (0.989)
  Pallas kernels: 590 us -> 582 us
    pallas_call x1, Pallas kernels: 87.9 us -> 80.5 us  [hidden_units(): pl.pallas_call(functools.partial(hidden_body, tp, seqs, early), out_shape...]
  transfers between devices with their start and end apart: 2 -> 2, of which waited for: 0 -> 0; matrix products, arithmetic and copies ran while one was open for 3% -> 3% of each run, Pallas kernels for 50% -> 51%
where the time goes in v7:
time: 643 us; the launch traced here: 633 us
  Pallas kernels  582 us (91%)
  other arithmetic  28.8 us (4%)
  between operations  14.8 us (2%)
  local copies, waits for them, and re-layouts  7.08 us (1%)
    pallas_call x1, Pallas kernels, back_one(): pl.pallas_call(functools.partial(back_one_body, n, tp, groups, late), out...  190 us
    pallas_call x1, Pallas kernels, front(): pl.pallas_call(functools.partial(front_body, n, tp, fsdp, groups), out_sh...  182 us
    pallas_call x1, Pallas kernels, back_two(): pl.pallas_call(functools.partial(back_two_body, n, fsdp, tp, seqs, skip),...  118 us
    pallas_call x1, Pallas kernels, hidden_units(): pl.pallas_call(functools.partial(hidden_body, tp, seqs, early), out_shape...  80.5 us
    convert_element_type x4, other arithmetic, on_device(): results.append(updated[2].astype(low))  18 us
  transfers between devices with their start and end apart: 2, of which 0 were waited for; matrix products, arithmetic and copies ran while one was open for 3% of the time, Pallas kernels for 51%

profile of v7, /device:TPU:0, one launch (start us, length us, event | category | flops | bytes accessed | tf_op | source)
XLA Modules:
  0.0 633.2 jit_solution(2725503492357997024)
XLA Ops:
  7.2 0.0 reduce-scatter.3.cloned.1.call-start
  7.3 0.7 convert.12
  8.0 0.7 copy.48
  8.7 0.2 copy.43
  8.8 0.9 slice.37
  9.8 0.1 dynamic-slice
  9.8 0.1 select_reduce_fusion
  10.0 0.7 fusion.10.tail_ref
  10.7 1.2 multiply_sine_fusion
  11.9 0.0 copy-done.12
  11.9 181.6 %front.1 = (bf16[2560,1024]{1,0:T(8,128)(2,1)}, bf16[2560,640]{1,0:T(8,128)(2,1)}, bf16[2560,5376]{1,0:T(8,128)(2,1)}, bf16[768,2560]{1,0:T(8,128)(2,1)}, bf16[7...) custom-call(bf16[768,2560]{1,0:T(8,128)(2,1)} %bitcast.33, ...), custom_call_target="tpu_custom_call" | custom-call | flops 1966080 | bytes 157286400 | tf_op jit(solution)/shard_map/front/pallas_call | solution.py:705
  193.5 80.5 %hidden_units.1 = (bf16[2560,5376]{1,0:T(8,128)(2,1)}, bf16[768,1792]{1,0:T(8,128)(2,1)}, bf16[768,1792]{1,0:T(8,128)(2,1)}, bf16[768,1792]{1,0:T(8,128)(2,1)}, bf16[256,2560]{1,0:T(8,128)(2,1)}) custom-call(bf16[768,2560]{1,0:T(8,128)(2,1)} %get-tuple-element.50.normal_ref, bf16[768,2560]{1,0:T(8,128)(2,1)} %get-tuple-element.51.grad_out_ref.grad_out_from, ...), custom_call_target="tpu_custom_call" | custom-call | flops 42278584320 | bytes 78643200 | tf_op jit(solution)/shard_map/hidden_units/pallas_call | solution.py:1524
  274.0 0.0 reduce-scatter.3.cloned.1.call-update
  274.0 0.0 reduce-scatter.5.cloned.1.call-start
  274.1 0.0 copy-start.1
  274.1 190.4 %back_one.1 = (bf16[768,2560]{1,0:T(8,128)(2,1)}, bf16[768,2560]{1,0:T(8,128)(2,1)}, bf16[960,768]{1,0:T(8,128)(2,1)}, f32[8,2560]{1,0:T(8,128)}) custom-call(bf16[768,1792]{1,0:T(8,128)(2,1)} %get-tuple-element.54.gate_ref, bf16[768,1792]{1,0:T(8,128)(2,1)} %get-tuple-element.55.up_ref, bf16[2560,5376]{1,0:T(8,128)(2,1)} %get-tuple-element.53.whole_ref.pair_ref, ...), custom_call_target="tpu_custom_call" | custom-call | flops 3276800 | bytes 262144000 | tf_op jit(solution)/shard_map/back_one/pallas_call | solution.py:1136
  464.5 0.0 copy-done.1
  464.5 0.0 copy-start
  464.5 1.4 copy-done
  465.9 11.6 %first_grads.1 = bf16[2560,1600]{1,0:T(8,128)(2,1)} custom-call(bf16[768,2560]{1,0:T(8,128)(2,1)} %get-tuple-element.68.normal_ref, bf16[960,768]{1,0:T(8,128)(2,1)S(1)} %copy-done, bf16[768,2560]{1,0:T(8,128)(2,1)} %get-tuple-element.69.residual_ref.residual_grad_from, bf16[640,768]{1,0:T(8,128)(2,1)S(1)} %copy-done.1), custom_call_target="tpu_custom_call" | custom-call | flops 6291456000 | bytes 18513920 | tf_op jit(solution)/shard_map/first_grads/pallas_call | solution.py:1571
  477.5 0.0 reduce-scatter.5.cloned.1.call-update
  477.5 0.0 copy-start.13
  477.6 0.0 copy-start.14
  477.6 0.0 copy-start.15
  477.6 0.0 copy-start.5
  477.6 0.0 copy-start.7
  477.6 0.0 copy-start.8
  477.6 118.2 %back_two.1 = (bf16[768,2560]{1,0:T(8,128)(2,1)}, f32[8,2560]{1,0:T(8,128)}) custom-call(bf16[960,768]{1,0:T(8,128)(2,1)} %get-tuple-element.72.proj_ref, bf16[2560,1024]{1,0:T(8,128)(2,1)} %get-tuple-element.73.weight_ref, f32[8,2560]{1,0:T(8,128)} %get-tuple-element.56.gain_ref, f32[8,2560]{1,0:T(8,128)} %get-tuple-element.74.second_gain_ref, ...), custom_call_target="tpu_custom_call" | custom-call | flops 1966080 | bytes 157286400 | tf_op jit(solution)/shard_map/back_two/pallas_call | solution.py:1318
  595.8 0.9 slice.24
  596.8 0.0 slice-start.2
  596.8 0.0 slice-start.4
  596.8 7.3 %convert.14 = f32[3,1,256,2560]{3,2,1,0:T(8,128)} convert(bf16[3,1,256,2560]{3,2,1,0:T(8,128)(2,1)} %bitcast.42) | non-fusion elementwise | flops 1966080 | bytes 11796480
  604.1 0.0 copy-done.13
  604.1 0.0 copy-done.14
  604.1 0.0 copy-done.15
  604.1 0.7 multiply_subtract_fusion.4
  604.8 0.0 copy-done.5
  604.8 0.0 copy-done.7
  604.8 0.0 copy-done.8
  604.8 0.0 copy-done.2
  604.8 0.0 slice-start.1
  604.8 0.0 slice-start.3
  604.8 0.0 slice-start.5
  604.9 4.5 fusion.22
  609.4 0.0 slice-done
  609.4 0.0 slice-done.2
  609.4 0.0 slice-done.4
  609.4 0.0 slice-done.1
  609.4 0.0 slice-done.3
  609.4 0.0 slice-done.5
  609.4 0.0 copy-start.6
  609.5 7.0 %fusion.25 = (bf16[320,3584]{1,0:T(8,128)(2,1)}, f32[320,3584]{1,0:T(8,128)}, f32[320,3584]{1,0:T(8,128)}, f32[320,3584]{1,0:T(8,128)}) fusion(f32[320,3584]{1,0:T(8,128)S(1)} %bitcast.32, bf16[320,5376]{1,0:T(8,128)(2,1)S(1)} %copy-done.5, f32[320,3584]{1,0:T(8,128)S(1)} %bitcast.37, f32[320,3584]{1,0:T(8,128)S(1)} %bitcast.39), kind=kLoop, calls=%fused_computation.50 | loop fusion | flops 19496960 | bytes 32112640 | tf_op jit(solution)/shard_map/convert_element_type | solution.py:1757
  616.5 0.0 reduce-scatter.5.cloned.1.call-done
  616.5 0.0 copy-done.6
  616.5 0.0 copy-start.10
  616.5 0.0 copy-start.11
  616.5 3.6 fusion.28
  620.2 0.0 copy-done.3
  620.2 0.0 copy-done.9
  620.2 0.0 copy-done.10
  620.2 0.0 copy-done.11
  620.2 2.8 fusion.31
  623.0 0.9 copy-done.4
  624.0 1.9 copy.50
  (15 shorter events, 0.1 us)
Async XLA Ops:
  7.2 470.3 %reduce-scatter.3.cloned.1.call-start = ((), (), s32[]{:S(2)}) async-start(), calls=%async_computation.2 | async-start | bytes 30965760 | tf_op jit(solution)/shard_map/reduce_scatter | solution.py:1676
  8.7 3.2 copy-start.12
  274.0 342.5 %reduce-scatter.5.cloned.1.call-start = ((), (), s32[]{:S(2)}) async-start(), calls=%async_computation.3 | async-start | bytes 9584640 | tf_op jit(solution)/shard_map/reduce_scatter | solution.py:1703
  274.1 190.4 %copy-start.1 = (bf16[640,768]{1,0:T(8,128)(2,1)S(1)}, bf16[640,768]{1,0:T(8,128)(2,1)}, u32[]{:S(2)}) copy-start(bf16[640,768]{1,0:T(8,128)(2,1)} %get-tuple-element.70.attended_ref) | copy-start | bytes 2949124
  464.5 1.4 copy-start
  477.5 126.6 %copy-start.13 = (f32[2,320]{1,0:T(2,128)S(1)}, f32[2,320]{1,0:T(2,128)}, u32[]{:S(2)}) copy-start(f32[2,320]{1,0:T(2,128)} %param.35) | copy-start | bytes 7684
  477.6 126.6 %copy-start.14 = (f32[2,320]{1,0:T(2,128)S(1)}, f32[2,320]{1,0:T(2,128)}, u32[]{:S(2)}) copy-start(f32[2,320]{1,0:T(2,128)} %param.37) | copy-start | bytes 7684
  477.6 126.6 %copy-start.15 = (f32[2,320]{1,0:T(2,128)S(1)}, f32[2,320]{1,0:T(2,128)}, u32[]{:S(2)}) copy-start(f32[2,320]{1,0:T(2,128)} %param.36) | copy-start | bytes 7684
  477.6 127.2 %copy-start.5 = (bf16[320,5376]{1,0:T(8,128)(2,1)S(1)}, bf16[320,5376]{1,0:T(8,128)(2,1)}, u32[]{:S(2)}) copy-start(bf16[320,5376]{1,0:T(8,128)(2,1)} %reduce-scatter.3.cloned.1.call-done) | copy-start | bytes 10321924
  477.6 127.2 %copy-start.7 = (f32[1792,320]{0,1:T(8,128)S(1)}, f32[1792,320]{0,1:T(8,128)}, u32[]{:S(2)}) copy-start(f32[1792,320]{0,1:T(8,128)} %param.34) | copy-start | bytes 6881284
  477.6 127.2 %copy-start.8 = (f32[1792,320]{0,1:T(8,128)S(1)}, f32[1792,320]{0,1:T(8,128)}, u32[]{:S(2)}) copy-start(f32[1792,320]{0,1:T(8,128)} %param.33) | copy-start | bytes 6881284
  596.7 8.1 %copy-start.2 = (f32[1792,320]{0,1:T(8,128)S(1)}, f32[1792,320]{0,1:T(8,128)}, u32[]{:S(2)}) copy-start(f32[1792,320]{0,1:T(8,128)} %param.32) | copy-start | bytes 6881284
  596.7 12.6 %slice-start = ((s8[4587520]{0:T(1024)(128)(4,1)}), s8[4194304]{0:T(1024)(128)(4,1)S(1)}, s32[]{:S(2)}) async-start(s8[4587520]{0:T(1024)(128)(4,1)} %bitcast.31), calls=%async_computation.4 | async-start | bytes 8388608
  596.8 12.6 %slice-start.2 = ((s8[4587520]{0:T(1024)(128)(4,1)}), s8[4194304]{0:T(1024)(128)(4,1)S(1)}, s32[]{:S(2)}) async-start(s8[4587520]{0:T(1024)(128)(4,1)} %bitcast.36), calls=%async_computation.6 | async-start | bytes 8388608
  596.8 12.6 %slice-start.4 = ((s8[4587520]{0:T(1024)(128)(4,1)}), s8[4194304]{0:T(1024)(128)(4,1)S(1)}, s32[]{:S(2)}) async-start(s8[4587520]{0:T(1024)(128)(4,1)} %bitcast.38), calls=%async_computation.8 | async-start | bytes 8388608
  604.8 4.6 slice-start.1
  604.8 4.6 slice-start.3
  604.8 4.6 slice-start.5
  609.4 7.1 %copy-start.6 = (f32[640,320]{0,1:T(8,128)S(1)}, f32[640,320]{0,1:T(8,128)}, u32[]{:S(2)}) copy-start(f32[640,320]{0,1:T(8,128)} %param.26) | copy-start | bytes 2457604
  616.5 3.7 copy-start.3
  616.5 3.7 copy-start.9
  616.5 3.7 copy-start.10
  616.5 3.7 copy-start.11
  620.2 3.8 copy-start.4
Sparse Core Ops, SparseCore 0:
  274.1 185.0 reduce-scatter.2
  477.6 73.8 reduce-scatter.4
